TPU v7x, 128 devices: a whole 4x4x4 slice. The times are simulated.
128 devices in a mesh: tasks: 32 (over y, x, core), grp: 4 (over z).
Axes of the slice: x: 4, y: 4, z: 4, core: 2. Of those that a mesh axis runs over, the one named last changes fastest.
Arguments:
- t2_store: bfloat16 [4, 2048, 128, 128], P('grp', 'tasks'), may hold values from -0.046875 to 0.046875
- ovvo_store: bfloat16 [4096, 128, 128], P(('tasks', 'grp')), may hold values from -6 to 6
- ovvv_store: bfloat16 [4096, 128, 128], P(('tasks', 'grp')), may hold values from -6 to 6
- dressing: bfloat16 [128, 128], replicated, may hold values from -0.5 to 0.5
- t_home: int32 [4, 2048], P('grp'), may hold values from 0 to 2047, as said below
- t_send: int32 [4, 32, 32, 2], P('grp', 'tasks'), may hold values from 0 to 2047, as said below
- w_home: int32 [4096], replicated, may hold values from 0 to 4095, as said below
- w_send: int32 [128, 128, 1], P(('tasks', 'grp')), may hold values from 0 to 4095, as said below
- task_t: int32 [4, 32, 32, 32], P('grp', 'tasks'), may hold values from 0 to 63
- task_w: int32 [4, 32, 32, 32], P('grp', 'tasks'), may hold values from 0 to 127
- recv_rows: int32 [4, 32, 32, 1], P('grp', 'tasks'), may hold values from 0 to 15, as said below
- pair_orbitals: int32 [32, 2], replicated, may hold values from 0 to 299
- eps_occ: float32 [300], replicated, may hold values from -0.9 to -0.4
- eps_vir: float32 [1024], replicated, may hold values from 0.3 to 1.2
Outputs:
- amplitude_update: float32 [4, 512, 128, 128], P('grp', 'tasks')
Inputs may be any that keep to these rules, and one draw needn't show every extreme that they name: Each row t_home[g] is a permutation; tile id n of group g lies in storage row t_home[g, n], on device t_home[g, n] // 64 of tasks. t_send[g, o, d, c] is a tile id stored on owner o: t_home[g, t_send[g, o, d, c]] // 64 equals o. w_home is a permutation; tile id n lies in storage row w_home[n], on the device with index w_home[n] // 32 = tasks index * 4 + grp index. w_send[o, q, c] is a tile id stored on device o: w_home[w_send[o, q, c]] // 32 equals o. For each g and o, every value below 16 appears exactly twice among recv_rows[g, o].
All inputs are finite; a program needn't handle non-finite values.
Results may differ from a plain program's by a relative error of at most 0.0029.
Values may be sent and summed in bfloat16 or wider, within the bound.
No kernel may reach another device: no remote copies, remote signals or barrier semaphores. Data moves between devices by JAX's collectives and lax.ppermute only.
A program may use at most 64 MiB of HBM per device.

v0:
```python
import jax
import jax.numpy as jnp
from jax import lax
from jax.sharding import PartitionSpec as P

NV = 8


def select_tiles(table_flat, indices, tile_width):
    table_size = table_flat.shape[0]
    flat_idx = indices.reshape(-1)
    onehot_rows = (flat_idx[:, None] == jnp.arange(table_size, dtype=jnp.int32)[None, :]).astype(
        jnp.bfloat16
    )
    picked = jnp.dot(onehot_rows, table_flat, preferred_element_type=jnp.float32).astype(
        jnp.bfloat16
    )
    return picked.reshape(indices.shape + (tile_width, tile_width))


def slot_products(t_fetched, w_fetched, task_rows_t, task_rows_w):
    slot_count, per_slot = task_rows_t.shape
    tile_width = t_fetched.shape[1]
    t_flat = t_fetched.reshape(t_fetched.shape[0], tile_width * tile_width)
    w_flat = w_fetched.reshape(w_fetched.shape[0], tile_width * tile_width)
    t_blocks = task_rows_t.reshape(slot_count // 4, 4, per_slot)
    w_blocks = task_rows_w.reshape(slot_count // 4, 4, per_slot)

    def product(indices):
        left_tiles = select_tiles(t_flat, indices[0], tile_width)
        right_tiles = select_tiles(w_flat, indices[1], tile_width)
        return jnp.einsum(
            "skab,skbc->sac", left_tiles, right_tiles, preferred_element_type=jnp.float32
        )

    block_sums = lax.map(product, (t_blocks, w_blocks))
    return block_sums.reshape(slot_count, tile_width, tile_width)


def per_device(
    t2_store,
    ovvo_store,
    ovvv_store,
    dressing,
    t_home,
    t_send,
    w_home,
    w_send,
    task_t,
    task_w,
    recv_rows,
    pair_orbitals,
    eps_occ,
    eps_vir,
):
    tasks_count = lax.axis_size("tasks")
    groups = lax.axis_size("grp")
    tasks_pos = lax.axis_index("tasks")
    group_pos = lax.axis_index("grp")
    tile_width = t2_store.shape[2]
    t_per_dev = t2_store.shape[1]
    t_rows = t_home[0][t_send[0, 0]] - tasks_pos * t_per_dev
    t_outgoing = t2_store[0][t_rows]
    t_incoming = lax.all_to_all(t_outgoing, "tasks", split_axis=0, concat_axis=0, tiled=True)
    t_fetched = t_incoming.reshape(-1, tile_width, tile_width)
    w_per_dev = ovvo_store.shape[0]
    dressed = jnp.dot(
        ovvv_store.reshape(-1, tile_width), dressing, preferred_element_type=jnp.float32
    )
    dressed = dressed.reshape(w_per_dev, tile_width, tile_width)
    formed = (ovvo_store.astype(jnp.float32) + dressed).astype(jnp.bfloat16)
    owner_pos = tasks_pos * groups + group_pos
    w_rows = w_home[w_send[0]] - owner_pos * w_per_dev
    w_outgoing = formed[w_rows]
    w_incoming = lax.all_to_all(
        w_outgoing, ("tasks", "grp"), split_axis=0, concat_axis=0, tiled=True
    )
    w_fetched = w_incoming.reshape(-1, tile_width, tile_width)
    partials = slot_products(t_fetched, w_fetched, task_t[0, 0], task_w[0, 0])
    slot_count = partials.shape[0]
    outgoing = partials.reshape(tasks_count, -1, tile_width, tile_width)
    incoming = lax.all_to_all(outgoing, "tasks", split_axis=0, concat_axis=0, tiled=True)
    res_dev = slot_count // 2
    targets = recv_rows[0, 0].reshape(-1)
    selector = (jnp.arange(res_dev, dtype=jnp.int32)[:, None] == targets[None, :]).astype(
        jnp.float32
    )
    residual = jnp.dot(
        selector,
        incoming.reshape(slot_count, tile_width * tile_width),
        precision=lax.Precision.HIGHEST,
    )
    residual = residual.reshape(res_dev, tile_width, tile_width)
    per_pair = NV * NV
    group_pairs = tasks_count * res_dev // per_pair
    tile_ids = tasks_pos * res_dev + jnp.arange(res_dev, dtype=jnp.int32)
    pair_index = group_pos * group_pairs + tile_ids // per_pair
    occupied = pair_orbitals[pair_index]
    occ_sum = eps_occ[occupied[:, 0]] + eps_occ[occupied[:, 1]]
    vir_tiles = eps_vir.reshape(NV, tile_width)
    left_vir = vir_tiles[tile_ids // NV % NV]
    right_vir = vir_tiles[tile_ids % NV]
    denominator = occ_sum[:, None, None] - left_vir[:, :, None] - right_vir[:, None, :]
    return (residual / denominator)[None]


def solution(mesh):
    return jax.shard_map(
        per_device,
        mesh=mesh,
        in_specs=(
            P("grp", "tasks", None, None),
            P(("tasks", "grp"), None, None),
            P(("tasks", "grp"), None, None),
            P(),
            P("grp", None),
            P("grp", "tasks", None, None),
            P(),
            P(("tasks", "grp"), None, None),
            P("grp", "tasks", None, None),
            P("grp", "tasks", None, None),
            P("grp", "tasks", None, None),
            P(),
            P(),
            P(),
        ),
        out_specs=P("grp", "tasks", None, None),
        check_vma=False,
    )
```

profile of v0, /device:TPU:33, one launch (start us, length us, event | category | flops | bytes accessed | tf_op | source)
XLA Modules:
  0.0 262.3 jit_solution(16865431595803546687)
XLA Ops:
  0.0 0.8 compare_select_fusion.6
  2.3 2.1 gather_fusion.1
  4.4 7.9 %all-to-all-start = ((bf16[32,2,128,128]{3,2,1,0:T(8,128)(2,1)}), bf16[32,2,128,128]{3,2,1,0:T(8,128)(2,1)}, u32[]{:S(2)}, u32[]{:S(2)}) async-start(bf16[32,2,128,128]{3,2,1,0:T(8,128)(2,1)} %bitcast.115), calls=%async_computation | async-start | bytes 4194304 | tf_op jit(solution)/shard_map/all_to_all | solution.py:64
  12.4 1.1 gather_fusion.2
  13.6 2.0 add_convert_fusion
  15.6 3.0 %gather_fusion.3 = bf16[128,128,128]{2,1,0:T(8,128)(2,1)} fusion(bf16[32,128,128]{2,1,0:T(8,128)(2,1)S(1)} %add_convert_fusion, s32[1024]{0:T(1024)S(1)} %pad_clamp_fusion.5), kind=kCustom, calls=%fused_computation.3 | custom fusion | bytes 8389120 | tf_op jit(solution)/shard_map/gather | solution.py:74
  18.6 21.7 %all-to-all-done = bf16[32,2,128,128]{3,2,1,0:T(8,128)(2,1)} async-done(((bf16[32,2,128,128]{3,2,1,0:T(8,128)(2,1)}), bf16[32,2,128,128]{3,2,1,0:T(8,128)(2,1)}, u32[]{:S(2)}, u32[]{:S(2)}) %all-to-all-start) | async-done | bytes 2097184 | tf_op jit(solution)/shard_map/all_to_all | solution.py:64
  40.3 8.4 %all-to-all-start.1 = ((bf16[128,1,128,128]{3,2,1,0:T(8,128)(2,1)}), bf16[128,1,128,128]{3,2,1,0:T(8,128)(2,1)}, u32[]{:S(2)}, u32[]{:S(2)}) async-start(bf16[128,1,128,128]{3,2,1,0:T(8,128)(2,1)} %bitcast.114), calls=%async_computation.1 | async-start | bytes 8388608 | tf_op jit(solution)/shard_map/all_to_all | solution.py:75
  48.7 4.3 %copy.63 = bf16[8,8,128,128]{3,1,2,0:T(8,128)(2,1)} copy(bf16[8,8,128,128]{3,2,1,0:T(8,128)(2,1)} %bitcast.34) | data formatting | bytes 4194304
  53.0 47.6 %all-to-all-done.1 = bf16[128,1,128,128]{3,2,1,0:T(8,128)(2,1)} async-done(((bf16[128,1,128,128]{3,2,1,0:T(8,128)(2,1)}), bf16[128,1,128,128]{3,2,1,0:T(8,128)(2,1)}, u32[]{:S(2)}, u32[]{:S(2)}) %all-to-all-start.1) | async-done | bytes 4194336 | tf_op jit(solution)/shard_map/all_to_all | solution.py:75
  100.6 7.7 %copy.62 = bf16[16,8,128,128]{3,1,2,0:T(8,128)(2,1)} copy(bf16[16,8,128,128]{3,2,1,0:T(8,128)(2,1)} %bitcast.37) | data formatting | bytes 8388608
  108.3 116.8 %while.10 = (s32[]{:T(128)}, f32[8,4,128,128]{3,2,1,0:T(8,128)}, s32[8,4,32]{2,1,0:T(4,128)}, bf16[64,16384]{1,0:T(8,128)(2,1)}, s32[8,4,32]{2,1,0:T(4,128)}, /*index=5*/bf16[128,16384]{1,0:T(8,128)(2,1)}, s32[]{:T(128)}) while((s32[]{:T(128)}, f32[8,4,128,128]{3,2,1,0:T(8,128)}, s32[8,4,32]{2,1,0:T(4,128)}, bf16[64,16384]{1,0:T(8,128)(2,1)}, ...), condition=%wide.region_1.2_spmd, body=%wide.region_0.1_spmd.sunk | while | flops 1346396160 | bytes 56890988 | solution.py:36
  109.0 3.5 %fusion.55 = bf16[16,8,128,128]{3,1,2,0:T(8,128)(2,1)S(1)} fusion(bf16[128,16384]{1,0:T(8,128)(2,1)} %get-tuple-element.116, s32[128]{0:T(128)S(1)} %eq.94), kind=kOutput, calls=%fused_computation.15.clone.1 | convolution fusion | flops 538984448 | bytes 8389120 | tf_op jit(solution)/shard_map/while/body/eval_jaxpr/dot_general | solution.py:15
  112.5 3.2 %copy.66 = bf16[16,8,128,128]{3,2,1,0:T(8,128)(2,1)} copy(bf16[16,8,128,128]{3,1,2,0:T(8,128)(2,1)S(1)} %fusion.55) | data formatting | bytes 8388608 | tf_op jit(solution)/shard_map/while
  115.8 2.9 %fusion.56 = bf16[16,8,128,128]{3,1,2,0:T(8,128)(2,1)S(1)} fusion(bf16[64,16384]{1,0:T(8,128)(2,1)} %get-tuple-element.114, s32[128]{0:T(128)S(1)} %eq.95), kind=kOutput, calls=%fused_computation.14.clone.1 | convolution fusion | flops 270540800 | bytes 6291968 | tf_op jit(solution)/shard_map/while/body/eval_jaxpr/dot_general | solution.py:15
  118.7 1.2 copy.67
  120.0 0.9 copy-done.3
  120.9 1.9 fusion.57
  123.6 3.5 %fusion.55 = bf16[16,8,128,128]{3,1,2,0:T(8,128)(2,1)S(1)} fusion(bf16[128,16384]{1,0:T(8,128)(2,1)} %get-tuple-element.116, s32[128]{0:T(128)S(1)} %eq.94), kind=kOutput, calls=%fused_computation.15.clone.1 | convolution fusion | flops 538984448 | bytes 8389120 | tf_op jit(solution)/shard_map/while/body/eval_jaxpr/dot_general | solution.py:15
  127.1 3.2 %copy.66 = bf16[16,8,128,128]{3,2,1,0:T(8,128)(2,1)} copy(bf16[16,8,128,128]{3,1,2,0:T(8,128)(2,1)S(1)} %fusion.55) | data formatting | bytes 8388608 | tf_op jit(solution)/shard_map/while
  130.4 2.9 %fusion.56 = bf16[16,8,128,128]{3,1,2,0:T(8,128)(2,1)S(1)} fusion(bf16[64,16384]{1,0:T(8,128)(2,1)} %get-tuple-element.114, s32[128]{0:T(128)S(1)} %eq.95), kind=kOutput, calls=%fused_computation.14.clone.1 | convolution fusion | flops 270540800 | bytes 6291968 | tf_op jit(solution)/shard_map/while/body/eval_jaxpr/dot_general | solution.py:15
  133.3 1.2 copy.67
  134.6 0.9 copy-done.3
  135.5 2.0 fusion.57
  138.2 3.5 %fusion.55 = bf16[16,8,128,128]{3,1,2,0:T(8,128)(2,1)S(1)} fusion(bf16[128,16384]{1,0:T(8,128)(2,1)} %get-tuple-element.116, s32[128]{0:T(128)S(1)} %eq.94), kind=kOutput, calls=%fused_computation.15.clone.1 | convolution fusion | flops 538984448 | bytes 8389120 | tf_op jit(solution)/shard_map/while/body/eval_jaxpr/dot_general | solution.py:15
  141.7 3.2 %copy.66 = bf16[16,8,128,128]{3,2,1,0:T(8,128)(2,1)} copy(bf16[16,8,128,128]{3,1,2,0:T(8,128)(2,1)S(1)} %fusion.55) | data formatting | bytes 8388608 | tf_op jit(solution)/shard_map/while
  145.0 2.9 %fusion.56 = bf16[16,8,128,128]{3,1,2,0:T(8,128)(2,1)S(1)} fusion(bf16[64,16384]{1,0:T(8,128)(2,1)} %get-tuple-element.114, s32[128]{0:T(128)S(1)} %eq.95), kind=kOutput, calls=%fused_computation.14.clone.1 | convolution fusion | flops 270540800 | bytes 6291968 | tf_op jit(solution)/shard_map/while/body/eval_jaxpr/dot_general | solution.py:15
  147.9 1.2 copy.67
  149.2 0.9 copy-done.3
  150.1 2.0 fusion.57
  152.9 3.5 %fusion.55 = bf16[16,8,128,128]{3,1,2,0:T(8,128)(2,1)S(1)} fusion(bf16[128,16384]{1,0:T(8,128)(2,1)} %get-tuple-element.116, s32[128]{0:T(128)S(1)} %eq.94), kind=kOutput, calls=%fused_computation.15.clone.1 | convolution fusion | flops 538984448 | bytes 8389120 | tf_op jit(solution)/shard_map/while/body/eval_jaxpr/dot_general | solution.py:15
  156.3 3.2 %copy.66 = bf16[16,8,128,128]{3,2,1,0:T(8,128)(2,1)} copy(bf16[16,8,128,128]{3,1,2,0:T(8,128)(2,1)S(1)} %fusion.55) | data formatting | bytes 8388608 | tf_op jit(solution)/shard_map/while
  159.6 2.9 %fusion.56 = bf16[16,8,128,128]{3,1,2,0:T(8,128)(2,1)S(1)} fusion(bf16[64,16384]{1,0:T(8,128)(2,1)} %get-tuple-element.114, s32[128]{0:T(128)S(1)} %eq.95), kind=kOutput, calls=%fused_computation.14.clone.1 | convolution fusion | flops 270540800 | bytes 6291968 | tf_op jit(solution)/shard_map/while/body/eval_jaxpr/dot_general | solution.py:15
  162.5 1.2 copy.67
  163.8 0.9 copy-done.3
  164.7 2.0 fusion.57
  167.5 3.5 %fusion.55 = bf16[16,8,128,128]{3,1,2,0:T(8,128)(2,1)S(1)} fusion(bf16[128,16384]{1,0:T(8,128)(2,1)} %get-tuple-element.116, s32[128]{0:T(128)S(1)} %eq.94), kind=kOutput, calls=%fused_computation.15.clone.1 | convolution fusion | flops 538984448 | bytes 8389120 | tf_op jit(solution)/shard_map/while/body/eval_jaxpr/dot_general | solution.py:15
  170.9 3.2 %copy.66 = bf16[16,8,128,128]{3,2,1,0:T(8,128)(2,1)} copy(bf16[16,8,128,128]{3,1,2,0:T(8,128)(2,1)S(1)} %fusion.55) | data formatting | bytes 8388608 | tf_op jit(solution)/shard_map/while
  174.2 2.9 %fusion.56 = bf16[16,8,128,128]{3,1,2,0:T(8,128)(2,1)S(1)} fusion(bf16[64,16384]{1,0:T(8,128)(2,1)} %get-tuple-element.114, s32[128]{0:T(128)S(1)} %eq.95), kind=kOutput, calls=%fused_computation.14.clone.1 | convolution fusion | flops 270540800 | bytes 6291968 | tf_op jit(solution)/shard_map/while/body/eval_jaxpr/dot_general | solution.py:15
  177.1 1.2 copy.67
  178.4 0.9 copy-done.3
  179.3 1.9 fusion.57
  182.1 3.5 %fusion.55 = bf16[16,8,128,128]{3,1,2,0:T(8,128)(2,1)S(1)} fusion(bf16[128,16384]{1,0:T(8,128)(2,1)} %get-tuple-element.116, s32[128]{0:T(128)S(1)} %eq.94), kind=kOutput, calls=%fused_computation.15.clone.1 | convolution fusion | flops 538984448 | bytes 8389120 | tf_op jit(solution)/shard_map/while/body/eval_jaxpr/dot_general | solution.py:15
  185.5 3.2 %copy.66 = bf16[16,8,128,128]{3,2,1,0:T(8,128)(2,1)} copy(bf16[16,8,128,128]{3,1,2,0:T(8,128)(2,1)S(1)} %fusion.55) | data formatting | bytes 8388608 | tf_op jit(solution)/shard_map/while
  188.8 2.9 %fusion.56 = bf16[16,8,128,128]{3,1,2,0:T(8,128)(2,1)S(1)} fusion(bf16[64,16384]{1,0:T(8,128)(2,1)} %get-tuple-element.114, s32[128]{0:T(128)S(1)} %eq.95), kind=kOutput, calls=%fused_computation.14.clone.1 | convolution fusion | flops 270540800 | bytes 6291968 | tf_op jit(solution)/shard_map/while/body/eval_jaxpr/dot_general | solution.py:15
  191.7 1.2 copy.67
  193.0 0.9 copy-done.3
  193.9 1.9 fusion.57
  196.6 3.5 %fusion.55 = bf16[16,8,128,128]{3,1,2,0:T(8,128)(2,1)S(1)} fusion(bf16[128,16384]{1,0:T(8,128)(2,1)} %get-tuple-element.116, s32[128]{0:T(128)S(1)} %eq.94), kind=kOutput, calls=%fused_computation.15.clone.1 | convolution fusion | flops 538984448 | bytes 8389120 | tf_op jit(solution)/shard_map/while/body/eval_jaxpr/dot_general | solution.py:15
  200.1 3.2 %copy.66 = bf16[16,8,128,128]{3,2,1,0:T(8,128)(2,1)} copy(bf16[16,8,128,128]{3,1,2,0:T(8,128)(2,1)S(1)} %fusion.55) | data formatting | bytes 8388608 | tf_op jit(solution)/shard_map/while
  203.4 2.9 %fusion.56 = bf16[16,8,128,128]{3,1,2,0:T(8,128)(2,1)S(1)} fusion(bf16[64,16384]{1,0:T(8,128)(2,1)} %get-tuple-element.114, s32[128]{0:T(128)S(1)} %eq.95), kind=kOutput, calls=%fused_computation.14.clone.1 | convolution fusion | flops 270540800 | bytes 6291968 | tf_op jit(solution)/shard_map/while/body/eval_jaxpr/dot_general | solution.py:15
  206.3 1.2 copy.67
  207.6 0.9 copy-done.3
  208.5 1.9 fusion.57
  211.2 3.5 %fusion.55 = bf16[16,8,128,128]{3,1,2,0:T(8,128)(2,1)S(1)} fusion(bf16[128,16384]{1,0:T(8,128)(2,1)} %get-tuple-element.116, s32[128]{0:T(128)S(1)} %eq.94), kind=kOutput, calls=%fused_computation.15.clone.1 | convolution fusion | flops 538984448 | bytes 8389120 | tf_op jit(solution)/shard_map/while/body/eval_jaxpr/dot_general | solution.py:15
  214.7 3.2 %copy.66 = bf16[16,8,128,128]{3,2,1,0:T(8,128)(2,1)} copy(bf16[16,8,128,128]{3,1,2,0:T(8,128)(2,1)S(1)} %fusion.55) | data formatting | bytes 8388608 | tf_op jit(solution)/shard_map/while
  218.0 2.9 %fusion.56 = bf16[16,8,128,128]{3,1,2,0:T(8,128)(2,1)S(1)} fusion(bf16[64,16384]{1,0:T(8,128)(2,1)} %get-tuple-element.114, s32[128]{0:T(128)S(1)} %eq.95), kind=kOutput, calls=%fused_computation.14.clone.1 | convolution fusion | flops 270540800 | bytes 6291968 | tf_op jit(solution)/shard_map/while/body/eval_jaxpr/dot_general | solution.py:15
  220.9 1.2 copy.67
  222.2 0.9 copy-done.3
  223.1 2.0 fusion.57
  225.1 4.9 %all-to-all-start.2 = ((f32[32,1,128,128]{3,2,1,0:T(8,128)}), f32[32,1,128,128]{3,2,1,0:T(8,128)}, u32[]{:S(2)}, u32[]{:S(2)}) async-start(f32[32,1,128,128]{3,2,1,0:T(8,128)} %bitcast.18), calls=%async_computation.2 | async-start | bytes 4194304 | tf_op jit(solution)/shard_map/all_to_all | solution.py:82
  233.8 23.5 %all-to-all-done.2 = f32[32,1,128,128]{3,2,1,0:T(8,128)} async-done(((f32[32,1,128,128]{3,2,1,0:T(8,128)}), f32[32,1,128,128]{3,2,1,0:T(8,128)}, u32[]{:S(2)}, u32[]{:S(2)}) %all-to-all-start.2) | async-done | bytes 2097184 | tf_op jit(solution)/shard_map/all_to_all | solution.py:82
  257.3 3.6 %fusion.23 = f32[1,16,128,128]{3,1,2,0:T(8,128)S(1)} fusion(f32[16,128]{1,0:T(8,128)S(1)} %gather_fusion.8, f32[16,128]{0,1:T(8,128)S(1)} %copy.40, s32[32]{0:T(128)S(1)} %bitcast.120, f32[4,8,128,128]{3,2,1,0:T(8,128)} %bitcast.40), kind=kOutput, calls=%fused_computation.32 | convolution fusion | flops 101188096 | bytes 3162240 | tf_op jit(solution)/shard_map/dot_general | solution.py:88
  261.0 1.3 copy.41
  (83 shorter events, 12.1 us)
Async XLA Ops:
  0.0 2.3 copy-start
  0.0 1.1 copy-start.1
  4.4 8.0 %copy-start.8 = (s32[1,128,1]{1,2,0:T(1,128)S(1)}, s32[1,128,1]{1,2,0:T(1,128)}, u32[]{:S(2)}) copy-start(s32[1,128,1]{1,2,0:T(1,128)} %param.23) | copy-start | bytes 1540
  4.4 8.0 %copy-start.4 = (s32[4096]{0:T(1024)S(1)}, s32[4096]{0:T(1024)}, u32[]{:S(2)}) copy-start(s32[4096]{0:T(1024)} %param.22) | copy-start | bytes 49156
  4.4 9.2 %copy-start.6 = (bf16[128,128]{1,0:T(8,128)(2,1)S(1)}, bf16[128,128]{1,0:T(8,128)(2,1)}, u32[]{:S(2)}) copy-start(bf16[128,128]{1,0:T(8,128)(2,1)} %param.19) | copy-start | bytes 98308
  4.4 35.8 %all-to-all-start = ((bf16[32,2,128,128]{3,2,1,0:T(8,128)(2,1)}), bf16[32,2,128,128]{3,2,1,0:T(8,128)(2,1)}, u32[]{:S(2)}, u32[]{:S(2)}) async-start(bf16[32,2,128,128]{3,2,1,0:T(8,128)(2,1)} %bitcast.115), calls=%async_computation | async-start | bytes 4194304 | tf_op jit(solution)/shard_map/all_to_all | solution.py:64
  40.3 60.3 %all-to-all-start.1 = ((bf16[128,1,128,128]{3,2,1,0:T(8,128)(2,1)}), bf16[128,1,128,128]{3,2,1,0:T(8,128)(2,1)}, u32[]{:S(2)}, u32[]{:S(2)}) async-start(bf16[128,1,128,128]{3,2,1,0:T(8,128)(2,1)} %bitcast.114), calls=%async_computation.1 | async-start | bytes 8388608 | tf_op jit(solution)/shard_map/all_to_all | solution.py:75
  118.7 2.2 copy-start.3
  133.3 2.2 copy-start.3
  147.9 2.2 copy-start.3
  162.5 2.2 copy-start.3
  177.1 2.2 copy-start.3
  191.7 2.2 copy-start.3
  206.3 2.2 copy-start.3
  220.9 2.2 copy-start.3
  225.1 4.9 %copy-start.7 = (s32[32,2]{0,1:T(2,128)S(1)}, s32[32,2]{0,1:T(2,128)}, u32[]{:S(2)}) copy-start(s32[32,2]{0,1:T(2,128)} %param.27) | copy-start | bytes 772
  225.1 5.9 %copy-start.2 = (f32[300]{0:T(512)S(1)}, f32[300]{0:T(512)}, u32[]{:S(2)}) copy-start(f32[300]{0:T(512)} %param.28) | copy-start | bytes 3604
  225.1 7.3 %copy-start.5 = (f32[1024]{0:T(1024)S(1)}, f32[1024]{0:T(1024)}, u32[]{:S(2)}) copy-start(f32[1024]{0:T(1024)} %param.29) | copy-start | bytes 12292
  225.1 32.2 %copy-start.9 = (s32[1,1,32,1]{2,3,1,0:T(1,128)S(1)}, s32[1,1,32,1]{2,3,1,0:T(1,128)}, u32[]{:S(2)}) copy-start(s32[1,1,32,1]{2,3,1,0:T(1,128)} %param.26) | copy-start | bytes 388
  225.1 32.2 %all-to-all-start.2 = ((f32[32,1,128,128]{3,2,1,0:T(8,128)}), f32[32,1,128,128]{3,2,1,0:T(8,128)}, u32[]{:S(2)}, u32[]{:S(2)}) async-start(f32[32,1,128,128]{3,2,1,0:T(8,128)} %bitcast.18), calls=%async_computation.2 | async-start | bytes 4194304 | tf_op jit(solution)/shard_map/all_to_all | solution.py:82
where the time goes:
time: 267 us; the launch traced here: 262 us
  waiting for transfers between devices  92.7 us (35%)
  local copies, waits for them, and re-layouts  74.3 us (28%)
  matrix products  72.1 us (27%)
  starting transfers between devices  21.3 us (8%)
    dot_general x16, matrix products, select_tiles(): jnp.dot(onehot_rows, table_flat, preferred_element_type=jnp.float32)  50.9 us
    all_to_all x1, waiting for transfers between devices, per_device(): lax.all_to_all(w_outgoing, ('tasks', 'grp'), split_axis=0, concat_axis=0,...  47.6 us
    while x32, local copies, waits for them, and re-layouts  43.2 us
    all_to_all x1, waiting for transfers between devices, per_device(): lax.all_to_all(outgoing, 'tasks', split_axis=0, concat_axis=0, tiled=True)  23.5 us
    all_to_all x1, waiting for transfers between devices, per_device(): lax.all_to_all(t_outgoing, 'tasks', split_axis=0, concat_axis=0, tiled=True)  21.7 us
    dot_general x8, matrix products, product(): jnp.einsum('skab,skbc->sac', left_tiles, right_tiles, preferred_element_t...  15.6 us
    unnamed x21, local copies, waits for them, and re-layouts  12.1 us
    all_to_all x1, starting transfers between devices, per_device(): lax.all_to_all(w_outgoing, ('tasks', 'grp'), split_axis=0, concat_axis=0,...  8.44 us
  transfers between devices with their start and end apart: 3, of which 3 were waited for; matrix products, arithmetic and copies ran while one was open for 5% of the time, Pallas kernels for 0%

commit v1 on v0

v1 whole, which is shorter than its diff:
```python
import jax
import jax.numpy as jnp
from jax import lax
from jax.experimental import pallas as pl
from jax.experimental.pallas import tpu as pltpu
from jax.sharding import PartitionSpec as P

NV = 8
SMEM = pl.BlockSpec(memory_space=pltpu.SMEM)
VMEM = pl.BlockSpec(memory_space=pltpu.VMEM)
ANY = pl.BlockSpec(memory_space=pl.ANY)


def pick_t_kernel(home_ref, send_ref, store_ref, out_ref, sem):
    count = out_ref.shape[0]
    per_dev = store_ref.shape[0]

    def start(i, carry):
        row = lax.rem(home_ref[send_ref[i]], per_dev)
        pltpu.make_async_copy(store_ref.at[row], out_ref.at[i], sem).start()
        return carry

    lax.fori_loop(0, count, start, 0, unroll=8)
    pltpu.make_async_copy(out_ref, out_ref, sem).wait()


def pick_t(home, send, store):
    count = send.shape[0]
    _, rows, cols = store.shape
    return pl.pallas_call(
        pick_t_kernel,
        out_shape=jax.ShapeDtypeStruct((count, rows, cols), store.dtype),
        in_specs=[SMEM, SMEM, ANY],
        out_specs=ANY,
        scratch_shapes=[pltpu.SemaphoreType.DMA],
        name="pick_t",
    )(home, send, store)


def form_w_kernel(home_ref, send_ref, ovvo_ref, ovvv_ref, dress_ref, out_ref, formed, sem):
    count = out_ref.shape[0]
    per_dev, rows, cols = formed.shape
    step = 4

    def form(i, carry):
        block = ovvv_ref[pl.ds(i * step, step)].reshape(step * rows, cols)
        dressed = jnp.dot(block, dress_ref[...], preferred_element_type=jnp.float32)
        total = ovvo_ref[pl.ds(i * step, step)].astype(jnp.float32) + dressed.reshape(step, rows, cols)
        formed[pl.ds(i * step, step)] = total.astype(jnp.bfloat16)
        return carry

    lax.fori_loop(0, per_dev // step, form, 0)

    def start(i, carry):
        row = lax.rem(home_ref[send_ref[i]], per_dev)
        pltpu.make_async_copy(formed.at[row], out_ref.at[i], sem).start()
        return carry

    lax.fori_loop(0, count, start, 0, unroll=8)
    pltpu.make_async_copy(out_ref, out_ref, sem).wait()


def form_w(home, send, ovvo, ovvv, dressing):
    count = send.shape[0]
    per_dev, rows, cols = ovvo.shape
    return pl.pallas_call(
        form_w_kernel,
        out_shape=jax.ShapeDtypeStruct((count, rows, cols), jnp.bfloat16),
        in_specs=[SMEM, SMEM, VMEM, VMEM, VMEM],
        out_specs=ANY,
        scratch_shapes=[pltpu.VMEM((per_dev, rows, cols), jnp.bfloat16), pltpu.SemaphoreType.DMA],
        compiler_params=pltpu.CompilerParams(vmem_limit_bytes=32 * 1024 * 1024),
        cost_estimate=pl.CostEstimate(flops=2 * per_dev * rows * cols * cols, bytes_accessed=12 << 20, transcendentals=0),
        name="form_w",
    )(home, send, ovvo, ovvv, dressing)


def products_kernel(task_t_ref, task_w_ref, t_ref, w_ref, out_ref):
    slots, rows, cols = out_ref.shape
    per_slot = task_t_ref.shape[0] // slots
    width = 4

    def slot(s, carry):
        acc = jnp.zeros((rows, cols), jnp.float32)
        for k in range(0, per_slot, width):
            base = s * per_slot + k
            left = jnp.concatenate([t_ref[task_t_ref[base + j]] for j in range(width)], axis=1)
            right = jnp.concatenate([w_ref[task_w_ref[base + j]] for j in range(width)], axis=0)
            acc = acc + jnp.dot(left, right, preferred_element_type=jnp.float32)
        out_ref[s] = acc.astype(out_ref.dtype)
        return carry

    lax.fori_loop(0, slots, slot, 0)


def products(task_t, task_w, t_fetched, w_fetched, slots):
    _, rows, cols = t_fetched.shape
    count = task_t.shape[0]
    return pl.pallas_call(
        products_kernel,
        out_shape=jax.ShapeDtypeStruct((slots, rows, cols), jnp.bfloat16),
        in_specs=[SMEM, SMEM, VMEM, VMEM],
        out_specs=VMEM,
        compiler_params=pltpu.CompilerParams(vmem_limit_bytes=32 * 1024 * 1024),
        cost_estimate=pl.CostEstimate(flops=2 * count * rows * cols * cols, bytes_accessed=7 << 20, transcendentals=0),
        name="products",
    )(task_t, task_w, t_fetched, w_fetched)


def finish_kernel(recv_ref, in_ref, base_ref, right_ref, out_ref, total):
    slots = in_ref.shape[0]
    res_dev = out_ref.shape[0]
    total[...] = jnp.zeros_like(total)

    def add(d, carry):
        row = recv_ref[d]
        total[row] = total[row] + in_ref[d].astype(jnp.float32)
        return carry

    lax.fori_loop(0, slots, add, 0)

    def divide(j, carry):
        denominator = base_ref[j // NV] - right_ref[pl.ds(lax.rem(j, NV), 1), :]
        out_ref[j] = total[j] / denominator
        return carry

    lax.fori_loop(0, res_dev, divide, 0)


def finish(recv, incoming, base, right, res_dev):
    slots, rows, cols = incoming.shape
    return pl.pallas_call(
        finish_kernel,
        out_shape=jax.ShapeDtypeStruct((res_dev, rows, cols), jnp.float32),
        in_specs=[SMEM, VMEM, VMEM, VMEM],
        out_specs=VMEM,
        scratch_shapes=[pltpu.VMEM((res_dev, rows, cols), jnp.float32)],
        compiler_params=pltpu.CompilerParams(vmem_limit_bytes=32 * 1024 * 1024),
        name="finish",
    )(recv, incoming, base, right)


def per_device(
    t2_store,
    ovvo_store,
    ovvv_store,
    dressing,
    t_home,
    t_send,
    w_home,
    w_send,
    task_t,
    task_w,
    recv_rows,
    pair_orbitals,
    eps_occ,
    eps_vir,
):
    tasks_count = lax.axis_size("tasks")
    groups = lax.axis_size("grp")
    tasks_pos = lax.axis_index("tasks")
    group_pos = lax.axis_index("grp")
    tile = t2_store.shape[2]
    slots = task_t.shape[2]
    res_dev = slots // 2

    t_out = pick_t(t_home[0], t_send.reshape(-1), t2_store[0])
    t_in = lax.all_to_all(
        t_out.reshape(tasks_count, -1, tile, tile), "tasks", split_axis=0, concat_axis=0, tiled=True
    ).reshape(-1, tile, tile)
    w_out = form_w(w_home, w_send.reshape(-1), ovvo_store, ovvv_store, dressing)
    w_in = lax.all_to_all(w_out, ("tasks", "grp"), split_axis=0, concat_axis=0, tiled=True)
    partials = products(task_t.reshape(-1), task_w.reshape(-1), t_in, w_in, slots)
    incoming = lax.all_to_all(partials, "tasks", split_axis=0, concat_axis=0, tiled=True)

    per_pair = NV * NV
    group_pairs = tasks_count * res_dev // per_pair
    first = tasks_pos * res_dev
    pair = pair_orbitals[group_pos * group_pairs + first // per_pair]
    occ_sum = eps_occ[pair[0]] + eps_occ[pair[1]]
    vir = eps_vir.reshape(NV, tile)
    left = lax.dynamic_slice_in_dim(vir, first // NV % NV, res_dev // NV, axis=0)
    base = jnp.broadcast_to((occ_sum - left)[:, :, None], (res_dev // NV, tile, tile))
    return finish(recv_rows.reshape(-1), incoming, base, vir, res_dev)[None]


def solution(mesh):
    return jax.shard_map(
        per_device,
        mesh=mesh,
        in_specs=(
            P("grp", "tasks", None, None),
            P(("tasks", "grp"), None, None),
            P(("tasks", "grp"), None, None),
            P(),
            P("grp", None),
            P("grp", "tasks", None, None),
            P(),
            P(("tasks", "grp"), None, None),
            P("grp", "tasks", None, None),
            P("grp", "tasks", None, None),
            P("grp", "tasks", None, None),
            P(),
            P(),
            P(),
        ),
        out_specs=P("grp", "tasks", None, None),
        check_vma=False,
    )
```

time: 267 us -> 206 us (0.77)
  Pallas kernels: 0 us -> 93.5 us
  matrix products: 72.1 us -> 0 us
  local copies, waits for them, and re-layouts: 74.3 us -> 6.17 us
  waiting for transfers between devices: 92.7 us -> 77.9 us
  between operations: 0.24 us -> 5.25 us
    pallas_call x0 -> x4, Pallas kernels: none -> 93.5 us  [the longest x1 65.4 us: pick_t(): pl.pallas_call(pick_t_kernel, out_shape=jax.ShapeDtypeStruct((count, rows...]
    dot_general x26 -> x0, matrix products: 72.1 us -> none  [the longest x16 50.9 us: select_tiles(): jnp.dot(onehot_rows, table_flat, preferred_element_type=jnp.float32)]
    while x32 -> x0, local copies, waits for them, and re-layouts: 43.2 us -> none
    all_to_all x3, waiting for transfers between devices: 92.7 us -> 77.9 us  [the longest x1 51.7 us: per_device(): lax.all_to_all(w_out, ('tasks', 'grp'), split_axis=0, concat_axis=0, tile...]
    gather x9 -> x0, local copies, waits for them, and re-layouts: 10.1 us -> none  [the longest x1 3.02 us: per_device(): w_outgoing = formed[w_rows]]
    unnamed x21 -> x25, local copies, waits for them, and re-layouts: 12.1 us -> 3.99 us
    dynamic_slice x8 -> x2, local copies, waits for them, and re-layouts: 5.6 us -> 0.74 us  [the longest x1 0.67 us: per_device(): occ_sum = eps_occ[pair[0]] + eps_occ[pair[1]]]
  transfers between devices with their start and end apart: 3 -> 3, of which waited for: 3 -> 3; matrix products, arithmetic and copies ran while one was open for 5% -> 1% of each run, Pallas kernels for 0% -> 4%
where the time goes in v1:
time: 206 us; the launch traced here: 203 us
  Pallas kernels  93.5 us (45%)
  waiting for transfers between devices  77.9 us (38%)
  starting transfers between devices  20.2 us (10%)
  local copies, waits for them, and re-layouts  6.17 us (3%)
  between operations  5.25 us (3%)
    pallas_call x1, Pallas kernels, pick_t(): pl.pallas_call(pick_t_kernel, out_shape=jax.ShapeDtypeStruct((count, rows...  65.4 us
    all_to_all x1, waiting for transfers between devices, per_device(): lax.all_to_all(w_out, ('tasks', 'grp'), split_axis=0, concat_axis=0, tile...  51.7 us
    pallas_call x1, Pallas kernels, products(): pl.pallas_call(products_kernel, out_shape=jax.ShapeDtypeStruct((slots, ro...  16.8 us
    all_to_all x1, waiting for transfers between devices, per_device(): lax.all_to_all(t_out.reshape(tasks_count, -1, tile, tile), 'tasks', split...  15.7 us
    all_to_all x1, waiting for transfers between devices, per_device(): lax.all_to_all(partials, 'tasks', split_axis=0, concat_axis=0, tiled=True)  10.5 us
    pallas_call x1, Pallas kernels, form_w(): pl.pallas_call(form_w_kernel, out_shape=jax.ShapeDtypeStruct((count, rows...  8.94 us
    all_to_all x1, starting transfers between devices, per_device(): lax.all_to_all(w_out, ('tasks', 'grp'), split_axis=0, concat_axis=0, tile...  8.42 us
    all_to_all x1, starting transfers between devices, per_device(): lax.all_to_all(t_out.reshape(tasks_count, -1, tile, tile), 'tasks', split...  7.9 us
  transfers between devices with their start and end apart: 3, of which 3 were waited for; matrix products, arithmetic and copies ran while one was open for 1% of the time, Pallas kernels for 4%

profile of v1, /device:TPU:33, one launch (start us, length us, event | category | flops | bytes accessed | tf_op | source)
XLA Modules:
  0.0 203.0 jit_solution(17165166430267124576)
XLA Ops:
  0.0 0.0 copy-start
  0.0 0.8 copy.16
  0.8 0.6 reshape.33.send_ref
  1.4 65.4 %pick_t.1 = bf16[64,128,128]{2,1,0:T(8,128)(2,1)} custom-call(s32[2048]{0:T(1024)} %bitcast.24, s32[64]{0:T(128)} %reshape.33.send_ref, bf16[64,128,128]{2,1,0:T(8,128)(2,1)} %bitcast.23), custom_call_target="tpu_custom_call" | custom-call | tf_op jit(solution)/shard_map/pick_t/pallas_call | solution.py:30
  66.8 0.0 copy-start.2
  66.9 0.0 copy-start.4
  66.9 0.0 copy-start.5
  66.9 0.0 copy-start.7
  66.9 7.9 %all-to-all-start = ((bf16[32,2,128,128]{3,2,1,0:T(8,128)(2,1)}), bf16[32,2,128,128]{3,2,1,0:T(8,128)(2,1)S(1)}, u32[]{:S(2)}, u32[]{:S(2)}) async-start(bf16[32,2,128,128]{3,2,1,0:T(8,128)(2,1)} %bitcast.22), calls=%async_computation | async-start | bytes 4194304 | tf_op jit(solution)/shard_map/all_to_all | solution.py:168
  74.8 0.0 copy-done.2
  74.8 0.0 copy-done.4
  74.8 0.0 copy-done.5
  74.8 0.0 copy-done.7
  74.8 0.0 copy-start.3
  74.9 1.2 copy-done.3
  76.1 8.9 %form_w.1 = bf16[128,128,128]{2,1,0:T(8,128)(2,1)S(1)} custom-call(s32[4096]{0:T(1024)S(1)} %copy-done.5, s32[128]{0:T(128)S(1)} %bitcast.20, bf16[32,128,128]{2,1,0:T(8,128)(2,1)S(1)} %copy-done.2, bf16[32,128,128]{2,1,0:T(8,128)(2,1)S(1)} %copy-done.3, bf16[128,128]{1,0:T(8,128)(2,1)S(1)} %copy-done.4), custom_call_target="tpu_custom_call" | custom-call | flops 134217728 | bytes 12582912 | tf_op jit(solution)/shard_map/form_w/pallas_call | solution.py:66
  85.0 0.0 copy-start.1
  85.0 1.9 copy-done.1
  87.0 0.0 copy-start.9
  87.0 0.0 copy-start.10
  87.0 15.7 %all-to-all-done = bf16[32,2,128,128]{3,2,1,0:T(8,128)(2,1)S(1)} async-done(((bf16[32,2,128,128]{3,2,1,0:T(8,128)(2,1)}), bf16[32,2,128,128]{3,2,1,0:T(8,128)(2,1)S(1)}, u32[]{:S(2)}, u32[]{:S(2)}) %all-to-all-start) | async-done | bytes 2097184 | tf_op jit(solution)/shard_map/all_to_all | solution.py:168
  102.7 8.4 %all-to-all-start.1 = ((bf16[128,128,128]{2,1,0:T(8,128)(2,1)}), bf16[128,128,128]{2,1,0:T(8,128)(2,1)}, u32[]{:S(2)}, u32[]{:S(2)}) async-start(bf16[128,128,128]{2,1,0:T(8,128)(2,1)} %copy-done.1), calls=%async_computation.1 | async-start | bytes 8388608 | tf_op jit(solution)/shard_map/all_to_all | solution.py:172
  111.1 0.0 copy-done.9
  111.1 0.1 reshape.31.task_t_ref
  111.2 0.0 copy-done.10
  111.2 0.1 reshape.32.task_w_ref
  111.2 51.7 %all-to-all-done.1.w_ref = bf16[128,128,128]{2,1,0:T(8,128)(2,1)} async-done(((bf16[128,128,128]{2,1,0:T(8,128)(2,1)}), bf16[128,128,128]{2,1,0:T(8,128)(2,1)}, u32[]{:S(2)}, u32[]{:S(2)}) %all-to-all-start.1) | async-done | bytes 4194336 | tf_op jit(solution)/shard_map/all_to_all | solution.py:172
  163.0 16.8 %products.1 = bf16[32,128,128]{2,1,0:T(8,128)(2,1)} custom-call(s32[1024]{0:T(1024)S(1)} %reshape.31.task_t_ref, s32[1024]{0:T(1024)S(1)} %reshape.32.task_w_ref, bf16[64,128,128]{2,1,0:T(8,128)(2,1)S(1)} %bitcast.17, bf16[128,128,128]{2,1,0:T(8,128)(2,1)} %all-to-all-done.1.w_ref), custom_call_target="tpu_custom_call" | custom-call | flops 4294967296 | bytes 7340032 | tf_op jit(solution)/shard_map/products/pallas_call | solution.py:99
  179.8 0.0 copy-start.11
  179.8 0.0 copy-start.6
  179.8 0.0 copy-start.8
  179.8 3.9 %all-to-all-start.2 = ((bf16[32,128,128]{2,1,0:T(8,128)(2,1)}), bf16[32,128,128]{2,1,0:T(8,128)(2,1)S(1)}, u32[]{:S(2)}, u32[]{:S(2)}) async-start(bf16[32,128,128]{2,1,0:T(8,128)(2,1)} %products.1), calls=%async_computation.2 | async-start | bytes 2097152 | tf_op jit(solution)/shard_map/all_to_all | solution.py:174
  183.7 0.0 copy-done
  183.7 0.1 constant_dynamic-slice_fusion
  183.8 0.6 fusion.1
  188.1 0.0 copy-done.11
  188.1 0.7 fusion
  190.1 0.0 copy-done.6
  190.1 10.5 %all-to-all-done.2.in_ref = bf16[32,128,128]{2,1,0:T(8,128)(2,1)S(1)} async-done(((bf16[32,128,128]{2,1,0:T(8,128)(2,1)}), bf16[32,128,128]{2,1,0:T(8,128)(2,1)S(1)}, u32[]{:S(2)}, u32[]{:S(2)}) %all-to-all-start.2) | async-done | bytes 1048608 | tf_op jit(solution)/shard_map/all_to_all | solution.py:174
  200.6 0.1 broadcast_in_dim.4.base_ref
  200.7 0.0 copy-done.8
  200.7 2.3 %finish.1 = f32[16,128,128]{2,1,0:T(8,128)} custom-call(s32[32]{0:T(128)S(1)} %bitcast.21, bf16[32,128,128]{2,1,0:T(8,128)(2,1)S(1)} %all-to-all-done.2.in_ref, f32[2,128,128]{2,1,0:T(8,128)S(1)} %broadcast_in_dim.4.base_ref, f32[8,128]{1,0:T(8,128)S(1)} %bitcast.19), custom_call_target="tpu_custom_call" | custom-call | tf_op jit(solution)/shard_map/finish/pallas_call | solution.py:132
  (1 shorter events, 0.0 us)
Async XLA Ops:
  0.0 183.7 %copy-start = (s32[32,2]{0,1:T(2,128)S(1)}, s32[32,2]{0,1:T(2,128)}, u32[]{:S(2)}) copy-start(s32[32,2]{0,1:T(2,128)} %param.25) | copy-start | bytes 772
  66.8 8.0 %copy-start.2 = (bf16[32,128,128]{2,1,0:T(8,128)(2,1)S(1)}, bf16[32,128,128]{2,1,0:T(8,128)(2,1)}, u32[]{:S(2)}) copy-start(bf16[32,128,128]{2,1,0:T(8,128)(2,1)} %ovvo_ref.1) | copy-start | bytes 3145732
  66.9 8.0 %copy-start.4 = (bf16[128,128]{1,0:T(8,128)(2,1)S(1)}, bf16[128,128]{1,0:T(8,128)(2,1)}, u32[]{:S(2)}) copy-start(bf16[128,128]{1,0:T(8,128)(2,1)} %dress_ref.1) | copy-start | bytes 98308
  66.9 8.0 %copy-start.5 = (s32[4096]{0:T(1024)S(1)}, s32[4096]{0:T(1024)}, u32[]{:S(2)}) copy-start(s32[4096]{0:T(1024)} %home_ref.1) | copy-start | bytes 49156
  66.9 8.0 %copy-start.7 = (s32[1,128,1]{1,2,0:T(1,128)S(1)}, s32[1,128,1]{1,2,0:T(1,128)}, u32[]{:S(2)}) copy-start(s32[1,128,1]{1,2,0:T(1,128)} %param.21) | copy-start | bytes 1540
  66.9 35.8 %all-to-all-start = ((bf16[32,2,128,128]{3,2,1,0:T(8,128)(2,1)}), bf16[32,2,128,128]{3,2,1,0:T(8,128)(2,1)S(1)}, u32[]{:S(2)}, u32[]{:S(2)}) async-start(bf16[32,2,128,128]{3,2,1,0:T(8,128)(2,1)} %bitcast.22), calls=%async_computation | async-start | bytes 4194304 | tf_op jit(solution)/shard_map/all_to_all | solution.py:168
  74.8 1.2 copy-start.3
  85.0 2.0 copy-start.1
  87.0 24.1 %copy-start.9 = (s32[1,1,32,32]{3,2,1,0:T(8,128)S(1)}, s32[1,1,32,32]{3,2,1,0:T(8,128)}, u32[]{:S(2)}) copy-start(s32[1,1,32,32]{3,2,1,0:T(8,128)} %param.22) | copy-start | bytes 12292
  87.0 24.2 %copy-start.10 = (s32[1,1,32,32]{3,2,1,0:T(8,128)S(1)}, s32[1,1,32,32]{3,2,1,0:T(8,128)}, u32[]{:S(2)}) copy-start(s32[1,1,32,32]{3,2,1,0:T(8,128)} %param.23) | copy-start | bytes 12292
  102.7 60.3 %all-to-all-start.1 = ((bf16[128,128,128]{2,1,0:T(8,128)(2,1)}), bf16[128,128,128]{2,1,0:T(8,128)(2,1)}, u32[]{:S(2)}, u32[]{:S(2)}) async-start(bf16[128,128,128]{2,1,0:T(8,128)(2,1)} %copy-done.1), calls=%async_computation.1 | async-start | bytes 8388608 | tf_op jit(solution)/shard_map/all_to_all | solution.py:172
  179.8 8.4 %copy-start.11 = (f32[300]{0:T(512)S(1)}, f32[300]{0:T(512)}, u32[]{:S(2)}) copy-start(f32[300]{0:T(512)} %param.26) | copy-start | bytes 3604
  179.8 10.3 %copy-start.6 = (f32[1024]{0:T(1024)S(1)}, f32[1024]{0:T(1024)}, u32[]{:S(2)}) copy-start(f32[1024]{0:T(1024)} %param.27) | copy-start | bytes 12292
  179.8 20.9 %copy-start.8 = (s32[1,1,32,1]{2,3,1,0:T(1,128)S(1)}, s32[1,1,32,1]{2,3,1,0:T(1,128)}, u32[]{:S(2)}) copy-start(s32[1,1,32,1]{2,3,1,0:T(1,128)} %param.24) | copy-start | bytes 388
  179.8 20.8 %all-to-all-start.2 = ((bf16[32,128,128]{2,1,0:T(8,128)(2,1)}), bf16[32,128,128]{2,1,0:T(8,128)(2,1)S(1)}, u32[]{:S(2)}, u32[]{:S(2)}) async-start(bf16[32,128,128]{2,1,0:T(8,128)(2,1)} %products.1), calls=%async_computation.2 | async-start | bytes 2097152 | tf_op jit(solution)/shard_map/all_to_all | solution.py:174

commit v2 on v1

v2 whole, which is shorter than its diff:
```python
import jax
import jax.numpy as jnp
from jax import lax
from jax.experimental import pallas as pl
from jax.experimental.pallas import tpu as pltpu
from jax.sharding import PartitionSpec as P

NV = 8
SMEM = pl.BlockSpec(memory_space=pltpu.SMEM)
VMEM = pl.BlockSpec(memory_space=pltpu.VMEM)
HBM = pl.BlockSpec(memory_space=pltpu.HBM)
CHUNKS = 4
VMEM_BYTES = 48 * 1024 * 1024


def pick_t_kernel(home_ref, send_ref, store_ref, out_ref, stage, sems):
    count = out_ref.shape[0]
    per_dev = store_ref.shape[0]
    cap = send_ref.shape[0]
    chunk = count // CHUNKS
    copies = []
    for c in range(CHUNKS):
        part = pl.ds(c * chunk, chunk)
        for i in range(c * chunk, (c + 1) * chunk):
            stage[i] = store_ref[lax.rem(home_ref[0, send_ref[i % cap, i // cap]], per_dev)]
        copies.append(pltpu.make_async_copy(stage.at[part], out_ref.at[part], sems.at[c]))
        copies[-1].start()
    for copy in copies:
        copy.wait()


def pick_t(home, send, store):
    count = send.shape[0] * send.shape[1]
    _, rows, cols = store.shape
    return pl.pallas_call(
        pick_t_kernel,
        out_shape=jax.ShapeDtypeStruct((count, rows, cols), store.dtype),
        in_specs=[SMEM, SMEM, VMEM],
        out_specs=HBM,
        scratch_shapes=[pltpu.VMEM((count, rows, cols), store.dtype), pltpu.SemaphoreType.DMA((CHUNKS,))],
        compiler_params=pltpu.CompilerParams(vmem_limit_bytes=VMEM_BYTES),
        name="pick_t",
    )(home, send, store)


def form_w_kernel(home_ref, send_ref, ovvo_ref, ovvv_ref, dress_ref, out_ref, formed, stage, sems):
    count = out_ref.shape[0]
    per_dev, rows, cols = formed.shape
    step = 4
    for i in range(0, per_dev, step):
        block = ovvv_ref[i : i + step].reshape(step * rows, cols)
        dressed = jnp.dot(block, dress_ref[...], preferred_element_type=jnp.float32)
        total = ovvo_ref[i : i + step].astype(jnp.float32) + dressed.reshape(step, rows, cols)
        formed[i : i + step] = total.astype(jnp.bfloat16)
    chunk = count // CHUNKS
    copies = []
    for c in range(CHUNKS):

        def pick(i, carry):
            stage[i] = formed[lax.rem(home_ref[send_ref[0, i]], per_dev)]
            return carry

        lax.fori_loop(c * chunk, (c + 1) * chunk, pick, 0, unroll=8)
        part = pl.ds(c * chunk, chunk)
        copies.append(pltpu.make_async_copy(stage.at[part], out_ref.at[part], sems.at[c]))
        copies[-1].start()
    for copy in copies:
        copy.wait()


def form_w(home, send, ovvo, ovvv, dressing):
    count = send.shape[1]
    per_dev, rows, cols = ovvo.shape
    return pl.pallas_call(
        form_w_kernel,
        out_shape=jax.ShapeDtypeStruct((count, rows, cols), jnp.bfloat16),
        in_specs=[SMEM, SMEM, VMEM, VMEM, VMEM],
        out_specs=HBM,
        scratch_shapes=[
            pltpu.VMEM((per_dev, rows, cols), jnp.bfloat16),
            pltpu.VMEM((count, rows, cols), jnp.bfloat16),
            pltpu.SemaphoreType.DMA((CHUNKS,)),
        ],
        compiler_params=pltpu.CompilerParams(vmem_limit_bytes=VMEM_BYTES),
        cost_estimate=pl.CostEstimate(flops=2 * per_dev * rows * cols * cols, bytes_accessed=12 << 20, transcendentals=0),
        name="form_w",
    )(home, send, ovvo, ovvv, dressing)


def products_kernel(task_t_ref, task_w_ref, t_ref, w_ref, out_ref):
    slots, rows, cols = out_ref.shape
    per_slot = task_t_ref.shape[1]
    width, together = 4, 8

    def group(i, carry):
        for u in range(together):
            s = i * together + u
            acc = jnp.zeros((rows, cols), jnp.float32)
            for k in range(0, per_slot, width):
                left = jnp.concatenate([t_ref[task_t_ref[s, k + j]] for j in range(width)], axis=1)
                right = jnp.concatenate([w_ref[task_w_ref[s, k + j]] for j in range(width)], axis=0)
                acc = acc + jnp.dot(left, right, preferred_element_type=jnp.float32)
            out_ref[s] = acc.astype(out_ref.dtype)
        return carry

    lax.fori_loop(0, slots // together, group, 0)


def products(task_t, task_w, t_fetched, w_fetched):
    _, rows, cols = t_fetched.shape
    slots, per_slot = task_t.shape
    return pl.pallas_call(
        products_kernel,
        out_shape=jax.ShapeDtypeStruct((slots, rows, cols), jnp.bfloat16),
        in_specs=[SMEM, SMEM, VMEM, VMEM],
        out_specs=VMEM,
        compiler_params=pltpu.CompilerParams(vmem_limit_bytes=VMEM_BYTES),
        cost_estimate=pl.CostEstimate(flops=2 * slots * per_slot * rows * cols * cols, bytes_accessed=7 << 20, transcendentals=0),
        name="products",
    )(task_t, task_w, t_fetched, w_fetched)


def finish_kernel(recv_ref, in_ref, base_ref, right_ref, out_ref, total):
    slots = in_ref.shape[0]
    res_dev = out_ref.shape[0]
    total[...] = jnp.zeros_like(total)

    def add(d, carry):
        row = recv_ref[0, d]
        total[row] = total[row] + in_ref[d].astype(jnp.float32)
        return carry

    lax.fori_loop(0, slots, add, 0)

    def divide(j, carry):
        denominator = base_ref[j // NV] - right_ref[pl.ds(lax.rem(j, NV), 1), :]
        out_ref[j] = total[j] / denominator
        return carry

    lax.fori_loop(0, res_dev, divide, 0)


def finish(recv, incoming, base, right, res_dev):
    slots, rows, cols = incoming.shape
    return pl.pallas_call(
        finish_kernel,
        out_shape=jax.ShapeDtypeStruct((res_dev, rows, cols), jnp.float32),
        in_specs=[SMEM, VMEM, VMEM, VMEM],
        out_specs=VMEM,
        scratch_shapes=[pltpu.VMEM((res_dev, rows, cols), jnp.float32)],
        compiler_params=pltpu.CompilerParams(vmem_limit_bytes=VMEM_BYTES),
        name="finish",
    )(recv, incoming, base, right)


def per_device(
    t2_store,
    ovvo_store,
    ovvv_store,
    dressing,
    t_home,
    t_send,
    w_home,
    w_send,
    task_t,
    task_w,
    recv_rows,
    pair_orbitals,
    eps_occ,
    eps_vir,
):
    tasks_count = lax.axis_size("tasks")
    groups = lax.axis_size("grp")
    tasks_pos = lax.axis_index("tasks")
    group_pos = lax.axis_index("grp")
    tile = t2_store.shape[2]
    slots = task_t.shape[2]
    res_dev = slots // 2

    t_out = pick_t(t_home, t_send[0, 0].T, t2_store[0])
    t_in = lax.all_to_all(
        t_out.reshape(tasks_count, -1, tile, tile), "tasks", split_axis=0, concat_axis=0, tiled=True
    ).reshape(-1, tile, tile)
    w_out = form_w(w_home, w_send[0].T, ovvo_store, ovvv_store, dressing)
    w_in = lax.all_to_all(w_out, ("tasks", "grp"), split_axis=0, concat_axis=0, tiled=True)
    partials = products(task_t[0, 0], task_w[0, 0], t_in, w_in)
    incoming = lax.all_to_all(partials, "tasks", split_axis=0, concat_axis=0, tiled=True)

    per_pair = NV * NV
    group_pairs = tasks_count * res_dev // per_pair
    first = tasks_pos * res_dev
    pair = pair_orbitals[group_pos * group_pairs + first // per_pair]
    occ_sum = eps_occ[pair[0]] + eps_occ[pair[1]]
    vir = eps_vir.reshape(NV, tile)
    left = lax.dynamic_slice_in_dim(vir, first // NV % NV, res_dev // NV, axis=0)
    base = jnp.broadcast_to((occ_sum - left)[:, :, None], (res_dev // NV, tile, tile))
    return finish(recv_rows[0, 0].T, incoming, base, vir, res_dev)[None]


def solution(mesh):
    return jax.shard_map(
        per_device,
        mesh=mesh,
        in_specs=(
            P("grp", "tasks", None, None),
            P(("tasks", "grp"), None, None),
            P(("tasks", "grp"), None, None),
            P(),
            P("grp", None),
            P("grp", "tasks", None, None),
            P(),
            P(("tasks", "grp"), None, None),
            P("grp", "tasks", None, None),
            P("grp", "tasks", None, None),
            P("grp", "tasks", None, None),
            P(),
            P(),
            P(),
        ),
        out_specs=P("grp", "tasks", None, None),
        check_vma=False,
    )
```

time: 206 us -> 140 us (0.68)
  Pallas kernels: 93.5 us -> 20.3 us
  blocking collectives: 0 us -> 60.3 us
  waiting for transfers between devices: 77.9 us -> 33.7 us
  starting transfers between devices: 20.2 us -> 11.8 us
    pallas_call x1, Pallas kernels: 65.4 us -> 2.12 us  [pick_t(): pl.pallas_call(pick_t_kernel, out_shape=jax.ShapeDtypeStruct((count, rows...]
    all_to_all x0 -> x1, blocking collectives: none -> 60.3 us  [per_device(): lax.all_to_all(w_out, ('tasks', 'grp'), split_axis=0, concat_axis=0, tile...]
    all_to_all x1 -> x0, waiting for transfers between devices: 51.7 us -> none  [per_device(): lax.all_to_all(w_out, ('tasks', 'grp'), split_axis=0, concat_axis=0, tile...]
    all_to_all x1 -> x0, starting transfers between devices: 8.42 us -> none  [per_device(): lax.all_to_all(w_out, ('tasks', 'grp'), split_axis=0, concat_axis=0, tile...]
    all_to_all x1, waiting for transfers between devices: 15.7 us -> 23.2 us  [per_device(): lax.all_to_all(t_out.reshape(tasks_count, -1, tile, tile), 'tasks', split...]
    pallas_call x1, Pallas kernels: 8.94 us -> 3.32 us  [form_w(): pl.pallas_call(form_w_kernel, out_shape=jax.ShapeDtypeStruct((count, rows...]
    pallas_call x1, Pallas kernels: 16.8 us -> 12.5 us  [products(): pl.pallas_call(products_kernel, out_shape=jax.ShapeDtypeStruct((slots, ro...]
    unnamed x25 -> x28, local copies, waits for them, and re-layouts: 3.99 us -> 4.25 us
  transfers between devices with their start and end apart: 3 -> 2, of which waited for: 3 -> 2; matrix products, arithmetic and copies ran while one was open for 1% -> 1% of each run, Pallas kernels for 4% -> 2%
where the time goes in v2:
time: 140 us; the launch traced here: 137 us
  blocking collectives  60.3 us (43%)
  waiting for transfers between devices  33.7 us (24%)
  Pallas kernels  20.3 us (14%)
  starting transfers between devices  11.8 us (8%)
  local copies, waits for them, and re-layouts  5.68 us (4%)
  between operations  5.24 us (4%)
    all_to_all x1, blocking collectives, per_device(): lax.all_to_all(w_out, ('tasks', 'grp'), split_axis=0, concat_axis=0, tile...  60.3 us
    all_to_all x1, waiting for transfers between devices, per_device(): lax.all_to_all(t_out.reshape(tasks_count, -1, tile, tile), 'tasks', split...  23.2 us
    pallas_call x1, Pallas kernels, products(): pl.pallas_call(products_kernel, out_shape=jax.ShapeDtypeStruct((slots, ro...  12.5 us
    all_to_all x1, waiting for transfers between devices, per_device(): lax.all_to_all(partials, 'tasks', split_axis=0, concat_axis=0, tiled=True)  10.5 us
    all_to_all x1, starting transfers between devices, per_device(): lax.all_to_all(t_out.reshape(tasks_count, -1, tile, tile), 'tasks', split...  7.9 us
    unnamed x28, local copies, waits for them, and re-layouts  4.25 us
    all_to_all x1, starting transfers between devices, per_device(): lax.all_to_all(partials, 'tasks', split_axis=0, concat_axis=0, tiled=True)  3.86 us
    pallas_call x1, Pallas kernels, form_w(): pl.pallas_call(form_w_kernel, out_shape=jax.ShapeDtypeStruct((count, rows...  3.32 us
  transfers between devices with their start and end apart: 2, of which 2 were waited for; matrix products, arithmetic and copies ran while one was open for 1% of the time, Pallas kernels for 2%

profile of v2, /device:TPU:33, one launch (start us, length us, event | category | flops | bytes accessed | tf_op | source)
XLA Modules:
  0.0 137.0 jit_solution(9015457882516004519)
XLA Ops:
  0.0 0.0 copy-start
  0.0 0.0 copy-start.1
  0.0 1.6 %copy-done.1 = bf16[1,64,128,128]{3,2,1,0:T(8,128)(2,1)S(1)} copy-done((bf16[1,64,128,128]{3,2,1,0:T(8,128)(2,1)S(1)}, bf16[1,64,128,128]{3,2,1,0:T(8,128)(2,1)}, u32[]{:S(2)}) %copy-start.1) | copy-done | bytes 2097176
  1.6 0.0 copy-start.6
  1.6 0.7 copy-done.6
  2.3 0.0 copy-start.8
  2.3 0.7 copy-done.8
  3.0 2.1 %pick_t.1 = bf16[64,128,128]{2,1,0:T(8,128)(2,1)} custom-call(s32[1,2048]{1,0:T(1,128)S(1)} %copy-done.6, s32[2,32]{1,0:T(2,128)S(1)} %bitcast.19, bf16[64,128,128]{2,1,0:T(8,128)(2,1)S(1)} %bitcast.15), custom_call_target="tpu_custom_call" | custom-call | tf_op jit(solution)/shard_map/pick_t/pallas_call | solution.py:35
  5.1 0.0 copy-start.2
  5.1 0.0 copy-start.4
  5.1 0.0 copy-start.5
  5.1 0.0 copy-start.9
  5.2 7.9 %all-to-all-start = ((bf16[32,2,128,128]{3,2,1,0:T(8,128)(2,1)}), bf16[32,2,128,128]{3,2,1,0:T(8,128)(2,1)S(1)}, u32[]{:S(2)}, u32[]{:S(2)}) async-start(bf16[32,2,128,128]{3,2,1,0:T(8,128)(2,1)} %bitcast.6), calls=%async_computation | async-start | bytes 4194304 | tf_op jit(solution)/shard_map/all_to_all | solution.py:181
  13.1 0.0 copy-done.2
  13.1 0.0 copy-done.4
  13.1 0.0 copy-done.5
  13.1 0.0 copy-done.9
  13.1 0.0 copy-start.3
  13.1 1.2 copy-done.3
  14.3 3.3 %form_w.1 = bf16[128,128,128]{2,1,0:T(8,128)(2,1)} custom-call(s32[4096]{0:T(1024)S(1)} %copy-done.5, s32[1,128]{1,0:T(1,128)S(1)} %bitcast.20, bf16[32,128,128]{2,1,0:T(8,128)(2,1)S(1)} %copy-done.2, bf16[32,128,128]{2,1,0:T(8,128)(2,1)S(1)} %copy-done.3, bf16[128,128]{1,0:T(8,128)(2,1)S(1)} %copy-done.4), custom_call_target="tpu_custom_call" | custom-call | flops 134217728 | bytes 12582912 | tf_op jit(solution)/shard_map/form_w/pallas_call | solution.py:74
  17.7 0.0 copy-start.11
  17.7 0.0 copy-start.12
  17.7 23.2 %all-to-all-done = bf16[32,2,128,128]{3,2,1,0:T(8,128)(2,1)S(1)} async-done(((bf16[32,2,128,128]{3,2,1,0:T(8,128)(2,1)}), bf16[32,2,128,128]{3,2,1,0:T(8,128)(2,1)S(1)}, u32[]{:S(2)}, u32[]{:S(2)}) %all-to-all-start) | async-done | bytes 2097184 | tf_op jit(solution)/shard_map/all_to_all | solution.py:181
  40.9 60.3 %all_to_all.15.w_ref = bf16[128,128,128]{2,1,0:T(8,128)(2,1)} all-to-all(bf16[128,128,128]{2,1,0:T(8,128)(2,1)} %form_w.1), channel_id=1, replica_groups=mesh['tasks'=32,'grp'=4] {'tasks','grp'}, dimensions={0} | all-to-all | bytes 8388608 | tf_op jit(solution)/shard_map/all_to_all | solution.py:185
  101.2 0.0 copy-done.11
  101.2 0.0 copy-done.12
  101.2 12.5 %products.1 = bf16[32,128,128]{2,1,0:T(8,128)(2,1)} custom-call(s32[32,32]{1,0:T(8,128)S(1)} %bitcast.22, s32[32,32]{1,0:T(8,128)S(1)} %bitcast.23, bf16[64,128,128]{2,1,0:T(8,128)(2,1)S(1)} %bitcast.16, bf16[128,128,128]{2,1,0:T(8,128)(2,1)} %all_to_all.15.w_ref), custom_call_target="tpu_custom_call" | custom-call | flops 4294967296 | bytes 7340032 | tf_op jit(solution)/shard_map/products/pallas_call | solution.py:112
  113.8 0.0 copy-start.13
  113.8 0.0 copy-start.7
  113.8 0.0 copy-start.10
  113.8 3.9 %all-to-all-start.2 = ((bf16[32,128,128]{2,1,0:T(8,128)(2,1)}), bf16[32,128,128]{2,1,0:T(8,128)(2,1)S(1)}, u32[]{:S(2)}, u32[]{:S(2)}) async-start(bf16[32,128,128]{2,1,0:T(8,128)(2,1)} %products.1), calls=%async_computation.2 | async-start | bytes 2097152 | tf_op jit(solution)/shard_map/all_to_all | solution.py:187
  117.7 0.0 copy-done
  117.7 0.1 constant_dynamic-slice_fusion
  117.8 0.6 fusion.1
  122.1 0.0 copy-done.13
  122.2 0.7 fusion
  124.1 0.0 copy-done.7
  124.1 10.5 %all-to-all-done.2.in_ref = bf16[32,128,128]{2,1,0:T(8,128)(2,1)S(1)} async-done(((bf16[32,128,128]{2,1,0:T(8,128)(2,1)}), bf16[32,128,128]{2,1,0:T(8,128)(2,1)S(1)}, u32[]{:S(2)}, u32[]{:S(2)}) %all-to-all-start.2) | async-done | bytes 1048608 | tf_op jit(solution)/shard_map/all_to_all | solution.py:187
  134.6 0.1 broadcast_in_dim.4.base_ref
  134.7 0.0 copy-done.10
  134.7 2.3 %finish.1 = f32[16,128,128]{2,1,0:T(8,128)} custom-call(s32[1,32]{1,0:T(1,128)S(1)} %bitcast.21, bf16[32,128,128]{2,1,0:T(8,128)(2,1)S(1)} %all-to-all-done.2.in_ref, f32[2,128,128]{2,1,0:T(8,128)S(1)} %broadcast_in_dim.4.base_ref, f32[8,128]{1,0:T(8,128)S(1)} %bitcast.18), custom_call_target="tpu_custom_call" | custom-call | tf_op jit(solution)/shard_map/finish/pallas_call | solution.py:145
  (1 shorter events, 0.0 us)
Async XLA Ops:
  0.0 117.7 %copy-start = (s32[32,2]{0,1:T(2,128)S(1)}, s32[32,2]{0,1:T(2,128)}, u32[]{:S(2)}) copy-start(s32[32,2]{0,1:T(2,128)} %param.25) | copy-start | bytes 772
  0.0 1.6 %copy-start.1 = (bf16[1,64,128,128]{3,2,1,0:T(8,128)(2,1)S(1)}, bf16[1,64,128,128]{3,2,1,0:T(8,128)(2,1)}, u32[]{:S(2)}) copy-start(bf16[1,64,128,128]{3,2,1,0:T(8,128)(2,1)} %param.14) | copy-start | bytes 6291460
  1.6 0.7 copy-start.6
  2.3 0.7 copy-start.8
  5.1 8.0 %copy-start.2 = (bf16[32,128,128]{2,1,0:T(8,128)(2,1)S(1)}, bf16[32,128,128]{2,1,0:T(8,128)(2,1)}, u32[]{:S(2)}) copy-start(bf16[32,128,128]{2,1,0:T(8,128)(2,1)} %ovvo_ref.1) | copy-start | bytes 3145732
  5.1 8.0 %copy-start.4 = (bf16[128,128]{1,0:T(8,128)(2,1)S(1)}, bf16[128,128]{1,0:T(8,128)(2,1)}, u32[]{:S(2)}) copy-start(bf16[128,128]{1,0:T(8,128)(2,1)} %dress_ref.1) | copy-start | bytes 98308
  5.1 8.0 %copy-start.5 = (s32[4096]{0:T(1024)S(1)}, s32[4096]{0:T(1024)}, u32[]{:S(2)}) copy-start(s32[4096]{0:T(1024)} %home_ref.3) | copy-start | bytes 49156
  5.1 8.0 %copy-start.9 = (s32[1,128,1]{1,2,0:T(1,128)S(1)}, s32[1,128,1]{1,2,0:T(1,128)}, u32[]{:S(2)}) copy-start(s32[1,128,1]{1,2,0:T(1,128)} %param.21) | copy-start | bytes 1540
  5.2 35.8 %all-to-all-start = ((bf16[32,2,128,128]{3,2,1,0:T(8,128)(2,1)}), bf16[32,2,128,128]{3,2,1,0:T(8,128)(2,1)S(1)}, u32[]{:S(2)}, u32[]{:S(2)}) async-start(bf16[32,2,128,128]{3,2,1,0:T(8,128)(2,1)} %bitcast.6), calls=%async_computation | async-start | bytes 4194304 | tf_op jit(solution)/shard_map/all_to_all | solution.py:181
  13.1 1.2 copy-start.3
  17.7 83.6 %copy-start.11 = (s32[1,1,32,32]{3,2,1,0:T(8,128)S(1)}, s32[1,1,32,32]{3,2,1,0:T(8,128)}, u32[]{:S(2)}) copy-start(s32[1,1,32,32]{3,2,1,0:T(8,128)} %param.22) | copy-start | bytes 12292
  17.7 83.6 %copy-start.12 = (s32[1,1,32,32]{3,2,1,0:T(8,128)S(1)}, s32[1,1,32,32]{3,2,1,0:T(8,128)}, u32[]{:S(2)}) copy-start(s32[1,1,32,32]{3,2,1,0:T(8,128)} %param.23) | copy-start | bytes 12292
  113.8 8.4 %copy-start.13 = (f32[300]{0:T(512)S(1)}, f32[300]{0:T(512)}, u32[]{:S(2)}) copy-start(f32[300]{0:T(512)} %param.26) | copy-start | bytes 3604
  113.8 10.3 %copy-start.7 = (f32[1024]{0:T(1024)S(1)}, f32[1024]{0:T(1024)}, u32[]{:S(2)}) copy-start(f32[1024]{0:T(1024)} %param.27) | copy-start | bytes 12292
  113.8 20.9 %copy-start.10 = (s32[1,1,32,1]{2,3,1,0:T(1,128)S(1)}, s32[1,1,32,1]{2,3,1,0:T(1,128)}, u32[]{:S(2)}) copy-start(s32[1,1,32,1]{2,3,1,0:T(1,128)} %param.24) | copy-start | bytes 388
  113.8 20.8 %all-to-all-start.2 = ((bf16[32,128,128]{2,1,0:T(8,128)(2,1)}), bf16[32,128,128]{2,1,0:T(8,128)(2,1)S(1)}, u32[]{:S(2)}, u32[]{:S(2)}) async-start(bf16[32,128,128]{2,1,0:T(8,128)(2,1)} %products.1), calls=%async_computation.2 | async-start | bytes 2097152 | tf_op jit(solution)/shard_map/all_to_all | solution.py:187

commit v3 on v2

v3 whole, which is shorter than its diff:
```python
import jax
import jax.numpy as jnp
from jax import lax
from jax.experimental import pallas as pl
from jax.experimental.pallas import tpu as pltpu
from jax.sharding import PartitionSpec as P

NV = 8
SMEM = pl.BlockSpec(memory_space=pltpu.SMEM)
VMEM = pl.BlockSpec(memory_space=pltpu.VMEM)
HBM = pl.BlockSpec(memory_space=pltpu.HBM)
CHUNKS = 4
SIDE = 4
VMEM_BYTES = 16 * 1024 * 1024


def prepare_kernel(t_home_hbm, t_send_hbm, store_hbm, w_home_hbm, w_send_hbm, ovvo_hbm, ovvv_hbm, dress_hbm, *refs):
    t_outs, w_out, scratch = refs[:SIDE], refs[SIDE], refs[SIDE + 1 :]
    t_home, t_send, store, w_home, w_send, ovvo, ovvv, dress, t_stage, formed, w_stage, in_sems, t_sems, w_sems = scratch
    loads = []
    for i, (src, dst) in enumerate(
        (
            (t_home_hbm, t_home),
            (t_send_hbm, t_send),
            (store_hbm, store),
            (ovvv_hbm, ovvv),
            (ovvo_hbm, ovvo),
            (dress_hbm, dress),
            (w_home_hbm, w_home),
            (w_send_hbm, w_send),
        )
    ):
        loads.append(pltpu.make_async_copy(src, dst, in_sems.at[i]))
        loads[-1].start()

    for load in loads[:3]:
        load.wait()
    t_per_dev = store.shape[0]
    cap = t_send.shape[0]
    pos = lax.axis_index("tasks")
    y, x, core = pos // (2 * SIDE), lax.rem(pos // 2, SIDE), lax.rem(pos, 2)
    copies = []
    for first in (1, 2, 3, 0):
        for second in range(SIDE):
            dy = jnp.where(core == 0, first, second)
            dx = jnp.where(core == 0, second, first)
            chip = lax.rem(y + dy, SIDE) * SIDE + lax.rem(x + dx, SIDE)
            for other in range(2):
                there = chip * 2 + (1 - core if other else core)
                for c in range(cap):
                    row = lax.rem(t_home[0, t_send[c, there]], t_per_dev)
                    t_stage[first, (second * 2 + other) * cap + c] = store[row]
        copies.append(pltpu.make_async_copy(t_stage.at[first], t_outs[first], t_sems.at[first]))
        copies[-1].start()

    for load in loads[3:]:
        load.wait()
    w_per_dev, rows, cols = formed.shape
    step = 4
    for i in range(0, w_per_dev, step):
        block = ovvv[i : i + step].reshape(step * rows, cols)
        dressed = jnp.dot(block, dress[...], preferred_element_type=jnp.float32)
        total = ovvo[i : i + step].astype(jnp.float32) + dressed.reshape(step, rows, cols)
        formed[i : i + step] = total.astype(jnp.bfloat16)
    count = w_out.shape[0]
    chunk = count // CHUNKS
    for c in range(CHUNKS):

        def pick(i, carry):
            w_stage[i] = formed[lax.rem(w_home[w_send[0, i]], w_per_dev)]
            return carry

        lax.fori_loop(c * chunk, (c + 1) * chunk, pick, 0, unroll=8)
        part = pl.ds(c * chunk, chunk)
        copies.append(pltpu.make_async_copy(w_stage.at[part], w_out.at[part], w_sems.at[c]))
        copies[-1].start()
    for copy in copies:
        copy.wait()


def prepare(t_home, t_send, store, w_home, w_send, ovvo, ovvv, dressing):
    t_count = t_send.shape[0] * t_send.shape[1]
    w_count = w_send.shape[1]
    w_per_dev, rows, cols = ovvo.shape
    t_part = jax.ShapeDtypeStruct((t_count // SIDE, rows, cols), store.dtype)
    w_all = jax.ShapeDtypeStruct((w_count, rows, cols), jnp.bfloat16)
    return pl.pallas_call(
        prepare_kernel,
        out_shape=[t_part] * SIDE + [w_all],
        in_specs=[HBM] * 8,
        out_specs=[HBM] * (SIDE + 1),
        scratch_shapes=[
            pltpu.SMEM(t_home.shape, t_home.dtype),
            pltpu.SMEM(t_send.shape, t_send.dtype),
            pltpu.VMEM(store.shape, store.dtype),
            pltpu.SMEM(w_home.shape, w_home.dtype),
            pltpu.SMEM(w_send.shape, w_send.dtype),
            pltpu.VMEM(ovvo.shape, ovvo.dtype),
            pltpu.VMEM(ovvv.shape, ovvv.dtype),
            pltpu.VMEM(dressing.shape, dressing.dtype),
            pltpu.VMEM((SIDE,) + t_part.shape, store.dtype),
            pltpu.VMEM((w_per_dev, rows, cols), jnp.bfloat16),
            pltpu.VMEM(w_all.shape, jnp.bfloat16),
            pltpu.SemaphoreType.DMA((8,)),
            pltpu.SemaphoreType.DMA((SIDE,)),
            pltpu.SemaphoreType.DMA((CHUNKS,)),
        ],
        compiler_params=pltpu.CompilerParams(vmem_limit_bytes=62 * 1024 * 1024),
        name="prepare",
    )(t_home, t_send, store, w_home, w_send, ovvo, ovvv, dressing)


def regroup_kernel(*refs):
    ins, outs, sems = refs[:SIDE], refs[SIDE:-1], refs[-1]
    cap = ins[0].shape[0] // (2 * SIDE)
    copies = []
    for second in (2, 1, 3, 0):
        for which in (1, 0):
            for first in range(SIDE):
                src = ins[first].at[pl.ds((second * 2 + which) * cap, cap)]
                out, base = (outs[-1], (1 - which) * SIDE * cap) if second == 2 else (outs[PLACE[which, second]], 0)
                dst = out.at[pl.ds(base + first * cap, cap)]
                copies.append(pltpu.make_async_copy(src, dst, sems.at[which, second, first]))
                copies[-1].start()
    for copy in copies:
        copy.wait()


PLACE = {(0, 0): 0, (0, 1): 1, (0, 3): 2, (1, 0): 3, (1, 1): 4, (1, 3): 5}


def regroup(parts):
    count, rows, cols = parts[0].shape
    part = jax.ShapeDtypeStruct((count // 2, rows, cols), parts[0].dtype)
    return pl.pallas_call(
        regroup_kernel,
        out_shape=[part] * 6 + [jax.ShapeDtypeStruct(parts[0].shape, parts[0].dtype)],
        in_specs=[VMEM] * SIDE,
        out_specs=[HBM] * 7,
        scratch_shapes=[pltpu.SemaphoreType.DMA((2, SIDE, SIDE))],
        compiler_params=pltpu.CompilerParams(vmem_limit_bytes=VMEM_BYTES),
        cost_estimate=pl.CostEstimate(flops=10**11, bytes_accessed=4 << 20, transcendentals=0),
        name="regroup",
    )(*parts)


def shift(k, first_axis):
    pairs = []
    for y in range(SIDE):
        for x in range(SIDE):
            for core in range(2):
                ty, tx = ((y + k) % SIDE, x) if core == first_axis else (y, (x + k) % SIDE)
                pairs.append(((y * SIDE + x) * 2 + core, (ty * SIDE + tx) * 2 + core))
    return pairs


def move(part, k, first_axis):
    return lax.ppermute(part, "tasks", shift(k, first_axis))


def swap_cores(part):
    return lax.ppermute(part, "tasks", [(i, i ^ 1) for i in range(2 * SIDE * SIDE)])


def fetch_t(parts, w_fetched):
    parts = [parts[0]] + [move(parts[k], k, 0) for k in range(1, SIDE)]
    same0, same1, same3, other0, other1, other3, both2 = regroup(parts)
    other0, other1, other3 = swap_cores(other0), swap_cores(other1), swap_cores(other3)
    same1, same3, other0, other1, other3, both2 = lax.optimization_barrier(
        (same1, same3, other0, other1, other3, both2)
    )
    both2 = move(both2, 2, 1)
    same1, other1 = move(same1, 1, 1), move(other1, 1, 0)
    same3, other3 = move(same3, 3, 1), move(other3, 3, 0)
    swapped = both2[: both2.shape[0] // 2]
    w_fetched, swapped = lax.optimization_barrier((w_fetched, swapped))
    other2 = swap_cores(swapped)
    return (same0, same1, both2, same3, other0, other1, other2, other3), w_fetched


def slot_places(task_t, pos, cap):
    y, x, core = pos // (2 * SIDE), pos // 2 % SIDE, pos % 2
    owner = task_t // cap
    dy = (y - owner // (2 * SIDE)) % SIDE
    dx = (x - owner // 2 % SIDE) % SIDE
    first = jnp.where(owner % 2 == 0, dy, dx)
    second = jnp.where(owner % 2 == 0, dx, dy)
    group = jnp.where(owner % 2 == core, second, second + SIDE)
    return (group * SIDE + first) * cap + task_t % cap


def products_kernel(task_ref, w_ref, *refs):
    parts, (out_ref, t_ref, sems) = refs[: 2 * SIDE], refs[2 * SIDE :]
    copies = []
    count = parts[0].shape[0]
    for i, part in enumerate(parts):
        part = part.at[pl.ds(part.shape[0] - count, count)]
        copies.append(pltpu.make_async_copy(part, t_ref.at[pl.ds(i * count, count)], sems.at[i]))
    for copy in copies:
        copy.start()
    for copy in copies:
        copy.wait()
    slots, rows, cols = out_ref.shape
    per_slot = task_ref.shape[2]
    width, together = 4, 8

    def group(i, carry):
        for u in range(together):
            s = i * together + u
            acc = jnp.zeros((rows, cols), jnp.float32)
            for k in range(0, per_slot, width):
                left = jnp.concatenate([t_ref[task_ref[0, s, k + j]] for j in range(width)], axis=1)
                right = jnp.concatenate([w_ref[task_ref[1, s, k + j]] for j in range(width)], axis=0)
                acc = acc + jnp.dot(left, right, preferred_element_type=jnp.float32)
            out_ref[s] = acc.astype(out_ref.dtype)
        return carry

    lax.fori_loop(0, slots // together, group, 0)


def products(tasks, t_parts, w_fetched):
    count, rows, cols = t_parts[0].shape
    _, slots, per_slot = tasks.shape
    return pl.pallas_call(
        products_kernel,
        out_shape=jax.ShapeDtypeStruct((slots, rows, cols), jnp.bfloat16),
        in_specs=[SMEM, VMEM] + [HBM] * (2 * SIDE),
        out_specs=VMEM,
        scratch_shapes=[
            pltpu.VMEM((2 * SIDE * count, rows, cols), jnp.bfloat16),
            pltpu.SemaphoreType.DMA((2 * SIDE,)),
        ],
        compiler_params=pltpu.CompilerParams(vmem_limit_bytes=VMEM_BYTES),
        cost_estimate=pl.CostEstimate(flops=2 * slots * per_slot * rows * cols * cols, bytes_accessed=7 << 20, transcendentals=0),
        name="products",
    )(tasks, w_fetched, *t_parts)


def finish_kernel(slot_ref, in_ref, inverse_ref, out_hbm, out_ref, sems):
    res_dev = out_ref.shape[0]
    chunk = res_dev // CHUNKS
    copies = []
    for c in range(CHUNKS):
        for j in range(c * chunk, (c + 1) * chunk):
            total = in_ref[slot_ref[0, j]].astype(jnp.float32) + in_ref[slot_ref[1, j]].astype(jnp.float32)
            out_ref[j] = total * inverse_ref[j]
        part = pl.ds(c * chunk, chunk)
        copies.append(pltpu.make_async_copy(out_ref.at[part], out_hbm.at[part], sems.at[c]))
        copies[-1].start()
    for copy in copies:
        copy.wait()


def finish(pair_slots, incoming, inverse):
    return pl.pallas_call(
        finish_kernel,
        out_shape=jax.ShapeDtypeStruct(inverse.shape, jnp.float32),
        in_specs=[SMEM, VMEM, VMEM],
        out_specs=HBM,
        scratch_shapes=[pltpu.VMEM(inverse.shape, jnp.float32), pltpu.SemaphoreType.DMA((CHUNKS,))],
        compiler_params=pltpu.CompilerParams(vmem_limit_bytes=VMEM_BYTES),
        name="finish",
    )(pair_slots, incoming, inverse)


def per_device(
    t2_store,
    ovvo_store,
    ovvv_store,
    dressing,
    t_home,
    t_send,
    w_home,
    w_send,
    task_t,
    task_w,
    recv_rows,
    pair_orbitals,
    eps_occ,
    eps_vir,
):
    tasks_count = lax.axis_size("tasks")
    groups = lax.axis_size("grp")
    tasks_pos = lax.axis_index("tasks")
    group_pos = lax.axis_index("grp")
    tile = t2_store.shape[2]
    slots = task_t.shape[2]
    res_dev = slots // 2

    *t_out, w_out = prepare(
        t_home, t_send[0, 0].T, t2_store[0], w_home, w_send[0].T, ovvo_store, ovvv_store, dressing
    )
    w_in = lax.all_to_all(w_out, ("tasks", "grp"), split_axis=0, concat_axis=0, tiled=True)
    t_parts, w_in = fetch_t(t_out, w_in)
    tasks = jnp.stack([slot_places(task_t[0, 0], tasks_pos, t_send.shape[3]), task_w[0, 0]])
    partials = products(tasks, t_parts, w_in)
    incoming = lax.all_to_all(partials, "tasks", split_axis=0, concat_axis=0, tiled=True)

    per_pair = NV * NV
    group_pairs = tasks_count * res_dev // per_pair
    first = tasks_pos * res_dev
    pair = pair_orbitals[group_pos * group_pairs + first // per_pair]
    occ_sum = eps_occ[pair[0]] + eps_occ[pair[1]]
    vir = eps_vir.reshape(NV, tile)
    left = lax.dynamic_slice_in_dim(vir, first // NV % NV, res_dev // NV, axis=0)
    base = occ_sum - left[:, None, :, None]
    inverse = (1.0 / (base - vir[None, :, None, :])).reshape(res_dev, tile, tile)
    named = recv_rows[0, 0].T == jnp.arange(res_dev, dtype=jnp.int32)[:, None]
    slot = jnp.arange(slots, dtype=jnp.int32)[None, :]
    low = jnp.min(jnp.where(named, slot, slots - 1), axis=1)
    high = jnp.max(jnp.where(named, slot, 0), axis=1)
    return finish(jnp.stack([low, high]), incoming, inverse)[None]


def solution(mesh):
    return jax.shard_map(
        per_device,
        mesh=mesh,
        in_specs=(
            P("grp", "tasks", None, None),
            P(("tasks", "grp"), None, None),
            P(("tasks", "grp"), None, None),
            P(),
            P("grp", None),
            P("grp", "tasks", None, None),
            P(),
            P(("tasks", "grp"), None, None),
            P("grp", "tasks", None, None),
            P("grp", "tasks", None, None),
            P("grp", "tasks", None, None),
            P(),
            P(),
            P(),
        ),
        out_specs=P("grp", "tasks", None, None),
        check_vma=False,
    )
```

time: 140 us -> 120 us (0.86); the launches traced: 137 us -> 120 us
  blocking collectives: 60.3 us -> 0 us
  starting transfers between devices: 11.8 us -> 53.5 us
  Pallas kernels: 20.3 us -> 22.5 us
  local copies, waits for them, and re-layouts: 5.68 us -> 3.71 us
    all_to_all x1 -> x0, blocking collectives: 60.3 us -> none  [per_device(): lax.all_to_all(w_out, ('tasks', 'grp'), split_axis=0, concat_axis=0, tile...]
    ppermute x0 -> x12, starting transfers between devices: none -> 35.8 us  [the longest x8 19 us: move(): return lax.ppermute(part, 'tasks', shift(k, first_axis))]
    ppermute x0 -> x12, waiting for transfers between devices: none -> 24 us  [the longest x8 22.6 us: move(): return lax.ppermute(part, 'tasks', shift(k, first_axis))]
    all_to_all x1, waiting for transfers between devices: 23.2 us -> 0.01 us  [per_device(): lax.all_to_all(w_out, ('tasks', 'grp'), split_axis=0, concat_axis=0, tile...]
    all_to_all x1, starting transfers between devices: 3.86 us -> 8.26 us  [per_device(): lax.all_to_all(partials, 'tasks', split_axis=0, concat_axis=0, tiled=True)]
    unnamed x28 -> x20, local copies, waits for them, and re-layouts: 4.25 us -> 2.38 us
    pallas_call x3, Pallas kernels: 7.75 us -> 9.59 us  [the longest x1 4.96 us: prepare(): pl.pallas_call(prepare_kernel, out_shape=[t_part] * SIDE + [w_all], in_sp...]
    all_to_all x1, starting transfers between devices: 7.9 us -> 9.49 us  [per_device(): lax.all_to_all(w_out, ('tasks', 'grp'), split_axis=0, concat_axis=0, tile...]
  transfers between devices with their start and end apart: 2 -> 14, of which waited for: 2 -> 7; matrix products, arithmetic and copies ran while one was open for 1% -> 2% of each run, Pallas kernels for 2% -> 3%
where the time goes in v3:
time: 120 us
  starting transfers between devices  53.5 us (45%)
  waiting for transfers between devices  34.3 us (29%)
  Pallas kernels  22.5 us (19%)
  between operations  5.18 us (4%)
  local copies, waits for them, and re-layouts  3.71 us (3%)
    ppermute x8, waiting for transfers between devices, move(): return lax.ppermute(part, 'tasks', shift(k, first_axis))  22.6 us
    ppermute x8, starting transfers between devices, move(): return lax.ppermute(part, 'tasks', shift(k, first_axis))  19 us
    ppermute x4, starting transfers between devices, swap_cores(): lax.ppermute(part, 'tasks', [(i, i ^ 1) for i in range(2 * SIDE * SIDE)])  16.8 us
    pallas_call x1, Pallas kernels, products(): pl.pallas_call(products_kernel, out_shape=jax.ShapeDtypeStruct((slots, ro...  12.9 us
    all_to_all x1, waiting for transfers between devices, per_device(): lax.all_to_all(partials, 'tasks', split_axis=0, concat_axis=0, tiled=True)  10.3 us
    all_to_all x1, starting transfers between devices, per_device(): lax.all_to_all(w_out, ('tasks', 'grp'), split_axis=0, concat_axis=0, tile...  9.49 us
    all_to_all x1, starting transfers between devices, per_device(): lax.all_to_all(partials, 'tasks', split_axis=0, concat_axis=0, tiled=True)  8.26 us
    pallas_call x1, Pallas kernels, prepare(): pl.pallas_call(prepare_kernel, out_shape=[t_part] * SIDE + [w_all], in_sp...  4.96 us
  transfers between devices with their start and end apart: 14, of which 7 were waited for; matrix products, arithmetic and copies ran while one was open for 2% of the time, Pallas kernels for 3%

profile of v3, /device:TPU:33, one launch (start us, length us, event | category | flops | bytes accessed | tf_op | source)
XLA Modules:
  0.0 119.7 jit_solution(11412068092868594908)
XLA Ops:
  0.0 0.0 copy-start
  0.0 5.0 %prepare.1 = (bf16[16,128,128]{2,1,0:T(8,128)(2,1)}, bf16[16,128,128]{2,1,0:T(8,128)(2,1)}, bf16[16,128,128]{2,1,0:T(8,128)(2,1)}, bf16[16,128,128]{2,1,0:T(8,128)(2,1)}, bf16[128,128,128]{2,1,0:T(8,128)(2,1)}) custom-call(s32[1,2048]{1,0:T(1,128)} %t_home_hbm.1, s32[2,32]{1,0:T(2,128)} %bitcast.40, bf16[64,128,128]{2,1,0:T(8,128)(2,1)} %bitcast.36, ...), custom_call_target="tpu_custom_call" | custom-call | tf_op jit(solution)/shard_map/prepare/pallas_call | solution.py:87
  5.0 1.3 %collective-permute-start = (bf16[16,128,128]{2,1,0:T(8,128)(2,1)}, bf16[16,128,128]{2,1,0:T(8,128)(2,1)S(1)}, u32[]{:S(2)}, u32[]{:S(2)}) collective-permute-start(bf16[16,128,128]{2,1,0:T(8,128)(2,1)} %get-tuple-element.27), channel_id=1, source_target_pairs={{0,32},{4,12},{8,40},{12,20},{16,48},{20,28},{24,56},{28,4},{32,64... | collective-permute-start | bytes 1572872 | tf_op jit(solution)/shard_map/ppermute | solution.py:158
  6.3 2.4 %collective-permute-start.1 = (bf16[16,128,128]{2,1,0:T(8,128)(2,1)}, bf16[16,128,128]{2,1,0:T(8,128)(2,1)S(1)}, u32[]{:S(2)}, u32[]{:S(2)}) collective-permute-start(bf16[16,128,128]{2,1,0:T(8,128)(2,1)} %get-tuple-element.28), channel_id=1, source_target_pairs={{0,64},{4,20},{8,72},{12,28},{16,80},{20,4},{24,88},{28,12},{32,96... | collective-permute-start | bytes 1572872 | tf_op jit(solution)/shard_map/ppermute | solution.py:158
  8.7 1.2 collective-permute-start.2
  9.9 0.0 copy-start.1
  9.9 9.5 %all-to-all-start = ((bf16[128,128,128]{2,1,0:T(8,128)(2,1)}), bf16[128,128,128]{2,1,0:T(8,128)(2,1)}, u32[]{:S(2)}, u32[]{:S(2)}) async-start(bf16[128,128,128]{2,1,0:T(8,128)(2,1)} %get-tuple-element.25), calls=%async_computation | async-start | bytes 8388608 | tf_op jit(solution)/shard_map/all_to_all | solution.py:293
  19.4 0.0 collective-permute-done.refs_1_
  19.4 2.0 %collective-permute-done.1.refs_2_ = bf16[16,128,128]{2,1,0:T(8,128)(2,1)S(1)} collective-permute-done((bf16[16,128,128]{2,1,0:T(8,128)(2,1)}, bf16[16,128,128]{2,1,0:T(8,128)(2,1)S(1)}, u32[]{:S(2)}, u32[]{:S(2)}) %collective-permute-start.1) | collective-permute-done | bytes 524320 | tf_op jit(solution)/shard_map/ppermute | solution.py:158
  21.4 0.0 collective-permute-done.2.refs_3_
  21.4 0.0 copy-done.1
  21.4 0.0 copy-start.5
  21.4 0.0 copy-start.6
  21.4 3.1 %regroup.1 = (bf16[8,128,128]{2,1,0:T(8,128)(2,1)S(1)}, bf16[8,128,128]{2,1,0:T(8,128)(2,1)S(1)}, bf16[8,128,128]{2,1,0:T(8,128)(2,1)S(1)}, bf16[8,128,128]{2,1,...) custom-call(bf16[16,128,128]{2,1,0:T(8,128)(2,1)S(1)} %copy-done.1, ...), custom_call_target="tpu_custom_call" | custom-call | flops 99999997952 | bytes 4194304 | tf_op jit(solution)/shard_map/regroup/pallas_call | solution.py:135
  24.5 0.0 copy-start.2
  24.5 0.7 copy-done.2
  25.2 0.0 copy-start.3
  25.2 0.7 copy-done.3
  25.9 16.1 %collective-permute-start.3 = (bf16[8,128,128]{2,1,0:T(8,128)(2,1)S(1)}, bf16[8,128,128]{2,1,0:T(8,128)(2,1)S(1)}, u32[]{:S(2)}, u32[]{:S(2)}) collective-permute-start(bf16[8,128,128]{2,1,0:T(8,128)(2,1)S(1)} %get-tuple-element.32), channel_id=1, source_target_pairs={{0,4},{4,0},{8,12},{12,8},{16,20},{20,16},{24,28},{28,24},{32,36},... | collective-permute-start | bytes 786440 | tf_op jit(solution)/shard_map/ppermute | solution.py:162
  42.0 0.0 collective-permute-start.4
  42.0 0.5 collective-permute-start.5
  42.5 0.7 collective-permute-done.3.refs_4_
  43.1 0.4 collective-permute-done.4
  43.5 0.4 collective-permute-done.5
  43.9 0.0 collective-permute-start.6
  43.9 9.5 %collective-permute-start.7 = (bf16[8,128,128]{2,1,0:T(8,128)(2,1)}, bf16[8,128,128]{2,1,0:T(8,128)(2,1)S(1)}, u32[]{:S(2)}, u32[]{:S(2)}) collective-permute-start(bf16[8,128,128]{2,1,0:T(8,128)(2,1)} %copy-done.2), channel_id=1, source_target_pairs={{0,8},{4,36},{8,16},{12,44},{16,24},{20,52},{24,0},{28,60},{32,40}... | collective-permute-start | bytes 786440 | tf_op jit(solution)/shard_map/ppermute | solution.py:158
  53.4 0.0 collective-permute-start.8
  53.4 4.3 %collective-permute-start.9 = (bf16[8,128,128]{2,1,0:T(8,128)(2,1)S(1)}, bf16[8,128,128]{2,1,0:T(8,128)(2,1)S(1)}, u32[]{:S(2)}, u32[]{:S(2)}) collective-permute-start(bf16[8,128,128]{2,1,0:T(8,128)(2,1)S(1)} %collective-permute-done.4), channel_id=1, source_target_pairs={{0,32},{4,12},{8,40},{12,20},{16,48},{20,28},{24,56},{28,4},{32,64... | collective-permute-start | bytes 786440 | tf_op jit(solution)/shard_map/ppermute | solution.py:158
  57.7 0.3 collective-permute-start.11
  58.0 17.9 %collective-permute-done.6.refs_2_ = bf16[16,128,128]{2,1,0:T(8,128)(2,1)S(1)} collective-permute-done((bf16[16,128,128]{2,1,0:T(8,128)(2,1)S(1)}, bf16[16,128,128]{2,1,0:T(8,128)(2,1)S(1)}, u32[]{:S(2)}, u32[]{:S(2)}) %collective-permute-start.6) | collective-permute-done | bytes 524320 | tf_op jit(solution)/shard_map/ppermute | solution.py:158
  75.9 0.0 all-to-all-done.w_ref
  75.9 0.2 collective-permute-start.10
  76.1 0.0 copy-done.5
  76.1 0.1 fusion.9
  76.2 0.0 copy-done.6
  76.2 2.6 %collective-permute-done.7.refs_1_ = bf16[8,128,128]{2,1,0:T(8,128)(2,1)S(1)} collective-permute-done((bf16[8,128,128]{2,1,0:T(8,128)(2,1)}, bf16[8,128,128]{2,1,0:T(8,128)(2,1)S(1)}, u32[]{:S(2)}, u32[]{:S(2)}) %collective-permute-start.7) | collective-permute-done | bytes 262176 | tf_op jit(solution)/shard_map/ppermute | solution.py:158
  78.8 0.0 collective-permute-done.8.refs_3_
  78.8 0.0 collective-permute-done.9.refs_5_
  78.8 0.0 collective-permute-done.11.refs_7_
  78.8 0.0 collective-permute-done.10.refs_6_
  78.8 0.0 copy-start.4
  78.9 0.9 copy-done.4
  79.8 0.0 copy-start.8
  79.8 0.0 copy-start.9
  79.8 0.0 copy-start.7
  79.8 12.9 %products.1 = bf16[32,128,128]{2,1,0:T(8,128)(2,1)} custom-call(s32[2,32,32]{2,1,0:T(8,128)S(1)} %pad_add_fusion.task_ref, bf16[128,128,128]{2,1,0:T(8,128)(2,1)} %all-to-all-done.w_ref, bf16[8,128,128]{2,1,0:T(8,128)(2,1)S(1)} %copy-done.4, bf16[8,128,128]{2,1,0:T(8,128)(2,1)S(1)} %collective-permute-done.7.refs_1_, ...), custom_call_target="tpu_custom_call" | custom-call | flops 4294967296 | bytes 7340032 | tf_op jit(solution)/shard_map/products/pallas_call | solution.py:224
  92.7 8.3 %all-to-all-start.1 = ((bf16[32,128,128]{2,1,0:T(8,128)(2,1)}), bf16[32,128,128]{2,1,0:T(8,128)(2,1)S(1)}, u32[]{:S(2)}, u32[]{:S(2)}) async-start(bf16[32,128,128]{2,1,0:T(8,128)(2,1)} %products.1), calls=%async_computation.1 | async-start | bytes 2097152 | tf_op jit(solution)/shard_map/all_to_all | solution.py:297
  101.0 0.0 copy-done
  101.0 0.1 constant_dynamic-slice_fusion
  101.1 0.6 fusion.15
  105.4 0.0 copy-done.8
  105.4 0.7 fusion.14
  107.3 0.0 copy-done.9
  107.3 0.1 select_reduce_fusion.1
  107.5 0.0 copy-done.7
  107.5 0.3 subtract_divide_fusion.inverse_ref
  107.8 10.3 %all-to-all-done.1.in_ref = bf16[32,128,128]{2,1,0:T(8,128)(2,1)S(1)} async-done(((bf16[32,128,128]{2,1,0:T(8,128)(2,1)}), bf16[32,128,128]{2,1,0:T(8,128)(2,1)S(1)}, u32[]{:S(2)}, u32[]{:S(2)}) %all-to-all-start.1) | async-done | bytes 1048608 | tf_op jit(solution)/shard_map/all_to_all | solution.py:297
  118.2 1.6 %finish.1 = f32[16,128,128]{2,1,0:T(8,128)} custom-call(s32[2,16]{1,0:T(2,128)S(1)} %pad_add_fusion.1.slot_ref, bf16[32,128,128]{2,1,0:T(8,128)(2,1)S(1)} %all-to-all-done.1.in_ref, f32[16,128,128]{2,1,0:T(8,128)S(1)} %subtract_divide_fusion.inverse_ref), custom_call_target="tpu_custom_call" | custom-call | tf_op jit(solution)/shard_map/finish/pallas_call | solution.py:255
  (5 shorter events, 0.1 us)
Async XLA Ops:
  0.0 101.0 %copy-start = (s32[32,2]{0,1:T(2,128)S(1)}, s32[32,2]{0,1:T(2,128)}, u32[]{:S(2)}) copy-start(s32[32,2]{0,1:T(2,128)} %param.25) | copy-start | bytes 772
  5.0 14.4 %collective-permute-start = (bf16[16,128,128]{2,1,0:T(8,128)(2,1)}, bf16[16,128,128]{2,1,0:T(8,128)(2,1)S(1)}, u32[]{:S(2)}, u32[]{:S(2)}) collective-permute-start(bf16[16,128,128]{2,1,0:T(8,128)(2,1)} %get-tuple-element.27), channel_id=1, source_target_pairs={{0,32},{4,12},{8,40},{12,20},{16,48},{20,28},{24,56},{28,4},{32,64... | collective-permute-start | bytes 1572872 | tf_op jit(solution)/shard_map/ppermute | solution.py:158
  6.3 15.1 %collective-permute-start.1 = (bf16[16,128,128]{2,1,0:T(8,128)(2,1)}, bf16[16,128,128]{2,1,0:T(8,128)(2,1)S(1)}, u32[]{:S(2)}, u32[]{:S(2)}) collective-permute-start(bf16[16,128,128]{2,1,0:T(8,128)(2,1)} %get-tuple-element.28), channel_id=1, source_target_pairs={{0,64},{4,20},{8,72},{12,28},{16,80},{20,4},{24,88},{28,12},{32,96... | collective-permute-start | bytes 1572872 | tf_op jit(solution)/shard_map/ppermute | solution.py:158
  8.7 12.7 %collective-permute-start.2 = (bf16[16,128,128]{2,1,0:T(8,128)(2,1)}, bf16[16,128,128]{2,1,0:T(8,128)(2,1)S(1)}, u32[]{:S(2)}, u32[]{:S(2)}) collective-permute-start(bf16[16,128,128]{2,1,0:T(8,128)(2,1)} %get-tuple-element.29), channel_id=1, source_target_pairs={{0,96},{4,28},{8,104},{12,4},{16,112},{20,12},{24,120},{28,20},{32... | collective-permute-start | bytes 1572872 | tf_op jit(solution)/shard_map/ppermute | solution.py:158
  9.9 11.5 %copy-start.1 = (bf16[16,128,128]{2,1,0:T(8,128)(2,1)S(1)}, bf16[16,128,128]{2,1,0:T(8,128)(2,1)}, u32[]{:S(2)}) copy-start(bf16[16,128,128]{2,1,0:T(8,128)(2,1)} %get-tuple-element.26.refs_0_) | copy-start | bytes 1572868
  9.9 66.1 %all-to-all-start = ((bf16[128,128,128]{2,1,0:T(8,128)(2,1)}), bf16[128,128,128]{2,1,0:T(8,128)(2,1)}, u32[]{:S(2)}, u32[]{:S(2)}) async-start(bf16[128,128,128]{2,1,0:T(8,128)(2,1)} %get-tuple-element.25), calls=%async_computation | async-start | bytes 8388608 | tf_op jit(solution)/shard_map/all_to_all | solution.py:293
  21.4 54.7 %copy-start.5 = (s32[1,1,32,32]{3,2,1,0:T(8,128)S(1)}, s32[1,1,32,32]{3,2,1,0:T(8,128)}, u32[]{:S(2)}) copy-start(s32[1,1,32,32]{3,2,1,0:T(8,128)} %param.22) | copy-start | bytes 12292
  21.4 54.8 %copy-start.6 = (s32[1,1,32,32]{3,2,1,0:T(8,128)S(1)}, s32[1,1,32,32]{3,2,1,0:T(8,128)}, u32[]{:S(2)}) copy-start(s32[1,1,32,32]{3,2,1,0:T(8,128)} %param.23) | copy-start | bytes 12292
  24.5 0.7 copy-start.2
  25.2 0.7 copy-start.3
  25.9 17.3 %collective-permute-start.3 = (bf16[8,128,128]{2,1,0:T(8,128)(2,1)S(1)}, bf16[8,128,128]{2,1,0:T(8,128)(2,1)S(1)}, u32[]{:S(2)}, u32[]{:S(2)}) collective-permute-start(bf16[8,128,128]{2,1,0:T(8,128)(2,1)S(1)} %get-tuple-element.32), channel_id=1, source_target_pairs={{0,4},{4,0},{8,12},{12,8},{16,20},{20,16},{24,28},{28,24},{32,36},... | collective-permute-start | bytes 786440 | tf_op jit(solution)/shard_map/ppermute | solution.py:162
  42.0 1.5 %collective-permute-start.4 = (bf16[8,128,128]{2,1,0:T(8,128)(2,1)S(1)}, bf16[8,128,128]{2,1,0:T(8,128)(2,1)S(1)}, u32[]{:S(2)}, u32[]{:S(2)}) collective-permute-start(bf16[8,128,128]{2,1,0:T(8,128)(2,1)S(1)} %get-tuple-element.33), channel_id=1, source_target_pairs={{0,4},{4,0},{8,12},{12,8},{16,20},{20,16},{24,28},{28,24},{32,36},... | collective-permute-start | bytes 786440 | tf_op jit(solution)/shard_map/ppermute | solution.py:162
  42.0 1.9 %collective-permute-start.5 = (bf16[8,128,128]{2,1,0:T(8,128)(2,1)S(1)}, bf16[8,128,128]{2,1,0:T(8,128)(2,1)S(1)}, u32[]{:S(2)}, u32[]{:S(2)}) collective-permute-start(bf16[8,128,128]{2,1,0:T(8,128)(2,1)S(1)} %get-tuple-element.34), channel_id=1, source_target_pairs={{0,4},{4,0},{8,12},{12,8},{16,20},{20,16},{24,28},{28,24},{32,36},... | collective-permute-start | bytes 786440 | tf_op jit(solution)/shard_map/ppermute | solution.py:162
  43.9 32.0 %collective-permute-start.6 = (bf16[16,128,128]{2,1,0:T(8,128)(2,1)S(1)}, bf16[16,128,128]{2,1,0:T(8,128)(2,1)S(1)}, u32[]{:S(2)}, u32[]{:S(2)}) collective-permute-start(bf16[16,128,128]{2,1,0:T(8,128)(2,1)S(1)} %get-tuple-element.36), channel_id=1, source_target_pairs={{0,16},{4,68},{8,24},{12,76},{16,0},{20,84},{24,8},{28,92},{32,48}... | collective-permute-start | bytes 1572872 | tf_op jit(solution)/shard_map/ppermute | solution.py:158
  43.9 34.9 %collective-permute-start.7 = (bf16[8,128,128]{2,1,0:T(8,128)(2,1)}, bf16[8,128,128]{2,1,0:T(8,128)(2,1)S(1)}, u32[]{:S(2)}, u32[]{:S(2)}) collective-permute-start(bf16[8,128,128]{2,1,0:T(8,128)(2,1)} %copy-done.2), channel_id=1, source_target_pairs={{0,8},{4,36},{8,16},{12,44},{16,24},{20,52},{24,0},{28,60},{32,40}... | collective-permute-start | bytes 786440 | tf_op jit(solution)/shard_map/ppermute | solution.py:158
  53.4 25.4 %collective-permute-start.8 = (bf16[8,128,128]{2,1,0:T(8,128)(2,1)S(1)}, bf16[8,128,128]{2,1,0:T(8,128)(2,1)S(1)}, u32[]{:S(2)}, u32[]{:S(2)}) collective-permute-start(bf16[8,128,128]{2,1,0:T(8,128)(2,1)S(1)} %get-tuple-element.40), channel_id=1, source_target_pairs={{0,24},{4,100},{8,0},{12,108},{16,8},{20,116},{24,16},{28,124},{32... | collective-permute-start | bytes 786440 | tf_op jit(solution)/shard_map/ppermute | solution.py:158
  53.4 25.4 %collective-permute-start.9 = (bf16[8,128,128]{2,1,0:T(8,128)(2,1)S(1)}, bf16[8,128,128]{2,1,0:T(8,128)(2,1)S(1)}, u32[]{:S(2)}, u32[]{:S(2)}) collective-permute-start(bf16[8,128,128]{2,1,0:T(8,128)(2,1)S(1)} %collective-permute-done.4), channel_id=1, source_target_pairs={{0,32},{4,12},{8,40},{12,20},{16,48},{20,28},{24,56},{28,4},{32,64... | collective-permute-start | bytes 786440 | tf_op jit(solution)/shard_map/ppermute | solution.py:158
  57.7 21.1 %collective-permute-start.11 = (bf16[8,128,128]{2,1,0:T(8,128)(2,1)S(1)}, bf16[8,128,128]{2,1,0:T(8,128)(2,1)S(1)}, u32[]{:S(2)}, u32[]{:S(2)}) collective-permute-start(bf16[8,128,128]{2,1,0:T(8,128)(2,1)S(1)} %collective-permute-done.5), channel_id=1, source_target_pairs={{0,96},{4,28},{8,104},{12,4},{16,112},{20,12},{24,120},{28,20},{32... | collective-permute-start | bytes 786440 | tf_op jit(solution)/shard_map/ppermute | solution.py:158
  75.9 2.9 %collective-permute-start.10 = (bf16[8,128,128]{2,1,0:T(8,128)(2,1)S(1)}, bf16[8,128,128]{2,1,0:T(8,128)(2,1)S(1)}, u32[]{:S(2)}, u32[]{:S(2)}) collective-permute-start(bf16[8,128,128]{2,1,0:T(8,128)(2,1)S(1)} %slice.14), channel_id=1, source_target_pairs={{0,4},{4,0},{8,12},{12,8},{16,20},{20,16},{24,28},{28,24},{32,36},... | collective-permute-start | bytes 786440 | tf_op jit(solution)/shard_map/ppermute | solution.py:162
  78.8 1.0 copy-start.4
  79.8 25.6 %copy-start.8 = (f32[300]{0:T(512)S(1)}, f32[300]{0:T(512)}, u32[]{:S(2)}) copy-start(f32[300]{0:T(512)} %param.26) | copy-start | bytes 3604
  79.8 27.5 %copy-start.9 = (s32[1,1,32,1]{2,3,1,0:T(1,128)S(1)}, s32[1,1,32,1]{2,3,1,0:T(1,128)}, u32[]{:S(2)}) copy-start(s32[1,1,32,1]{2,3,1,0:T(1,128)} %param.24) | copy-start | bytes 388
  79.8 27.7 %copy-start.7 = (f32[1024]{0:T(1024)S(1)}, f32[1024]{0:T(1024)}, u32[]{:S(2)}) copy-start(f32[1024]{0:T(1024)} %param.27) | copy-start | bytes 12292
  92.7 25.4 %all-to-all-start.1 = ((bf16[32,128,128]{2,1,0:T(8,128)(2,1)}), bf16[32,128,128]{2,1,0:T(8,128)(2,1)S(1)}, u32[]{:S(2)}, u32[]{:S(2)}) async-start(bf16[32,128,128]{2,1,0:T(8,128)(2,1)} %products.1), calls=%async_computation.1 | async-start | bytes 2097152 | tf_op jit(solution)/shard_map/all_to_all | solution.py:297

commit v4 on v3

--- a/solution.py
+++ b/solution.py
@@ -11,6 +11,7 @@
 HBM = pl.BlockSpec(memory_space=pltpu.HBM)
 CHUNKS = 4
 SIDE = 4
+VMEM_MOST = 62 * 1024 * 1024
 VMEM_BYTES = 16 * 1024 * 1024
 
 
@@ -105,7 +106,7 @@
             pltpu.SemaphoreType.DMA((SIDE,)),
             pltpu.SemaphoreType.DMA((CHUNKS,)),
         ],
-        compiler_params=pltpu.CompilerParams(vmem_limit_bytes=62 * 1024 * 1024),
+        compiler_params=pltpu.CompilerParams(vmem_limit_bytes=VMEM_MOST),
         name="prepare",
     )(t_home, t_send, store, w_home, w_send, ovvo, ovvv, dressing)
 
@@ -138,7 +139,7 @@
         in_specs=[VMEM] * SIDE,
         out_specs=[HBM] * 7,
         scratch_shapes=[pltpu.SemaphoreType.DMA((2, SIDE, SIDE))],
-        compiler_params=pltpu.CompilerParams(vmem_limit_bytes=VMEM_BYTES),
+        compiler_params=pltpu.CompilerParams(vmem_limit_bytes=VMEM_MOST),
         cost_estimate=pl.CostEstimate(flops=10**11, bytes_accessed=4 << 20, transcendentals=0),
         name="regroup",
     )(*parts)
@@ -172,10 +173,33 @@
     both2 = move(both2, 2, 1)
     same1, other1 = move(same1, 1, 1), move(other1, 1, 0)
     same3, other3 = move(same3, 3, 1), move(other3, 3, 0)
-    swapped = both2[: both2.shape[0] // 2]
-    w_fetched, swapped = lax.optimization_barrier((w_fetched, swapped))
-    other2 = swap_cores(swapped)
+    w_fetched, both2 = lax.optimization_barrier((stage(w_fetched), both2))
+    other2 = swap_cores(both2[: both2.shape[0] // 2])
     return (same0, same1, both2, same3, other0, other1, other2, other3), w_fetched
+
+
+def stage_kernel(hbm, out_ref, sems):
+    chunk = hbm.shape[0] // CHUNKS
+    copies = []
+    for c in range(CHUNKS):
+        part = pl.ds(c * chunk, chunk)
+        copies.append(pltpu.make_async_copy(hbm.at[part], out_ref.at[part], sems.at[c]))
+        copies[-1].start()
+    for copy in copies:
+        copy.wait()
+
+
+def stage(value):
+    return pl.pallas_call(
+        stage_kernel,
+        out_shape=jax.ShapeDtypeStruct(value.shape, value.dtype),
+        in_specs=[HBM],
+        out_specs=VMEM,
+        scratch_shapes=[pltpu.SemaphoreType.DMA((CHUNKS,))],
+        compiler_params=pltpu.CompilerParams(vmem_limit_bytes=VMEM_BYTES),
+        cost_estimate=pl.CostEstimate(flops=5*10**9, bytes_accessed=8 << 20, transcendentals=0),
+        name="stage",
+    )(value)
 
 
 def slot_places(task_t, pos, cap):

time: 120 us -> 118 us (0.983)
  waiting for transfers between devices: 34.3 us -> 32.5 us
  local copies, waits for them, and re-layouts: 3.71 us -> 2.36 us
    ppermute x8, waiting for transfers between devices: 22.6 us -> 6.76 us  [move(): return lax.ppermute(part, 'tasks', shift(k, first_axis))]
    all_to_all x1, waiting for transfers between devices: 0.01 us -> 13.8 us  [per_device(): lax.all_to_all(w_out, ('tasks', 'grp'), split_axis=0, concat_axis=0, tile...]
    pallas_call x0 -> x1, Pallas kernels: none -> 2.21 us  [stage(): pl.pallas_call(stage_kernel, out_shape=jax.ShapeDtypeStruct(value.shape,...]
    unnamed x20, local copies, waits for them, and re-layouts: 2.38 us -> 1.03 us
    pallas_call x1, Pallas kernels: 12.9 us -> 11.7 us  [products(): pl.pallas_call(products_kernel, out_shape=jax.ShapeDtypeStruct((slots, ro...]
  transfers between devices with their start and end apart: 14 -> 14, of which waited for: 7 -> 8; matrix products, arithmetic and copies ran while one was open for 2% -> 2% of each run, Pallas kernels for 3% -> 5%
where the time goes in v4:
time: 118 us
  starting transfers between devices  53.4 us (45%)
  waiting for transfers between devices  32.5 us (28%)
  Pallas kernels  23.5 us (20%)
  between operations  5.2 us (4%)
  local copies, waits for them, and re-layouts  2.36 us (2%)
    ppermute x8, starting transfers between devices, move(): return lax.ppermute(part, 'tasks', shift(k, first_axis))  18.9 us
    ppermute x4, starting transfers between devices, swap_cores(): lax.ppermute(part, 'tasks', [(i, i ^ 1) for i in range(2 * SIDE * SIDE)])  16.8 us
    all_to_all x1, waiting for transfers between devices, per_device(): lax.all_to_all(w_out, ('tasks', 'grp'), split_axis=0, concat_axis=0, tile...  13.8 us
    pallas_call x1, Pallas kernels, products(): pl.pallas_call(products_kernel, out_shape=jax.ShapeDtypeStruct((slots, ro...  11.7 us
    all_to_all x1, waiting for transfers between devices, per_device(): lax.all_to_all(partials, 'tasks', split_axis=0, concat_axis=0, tiled=True)  10.3 us
    all_to_all x1, starting transfers between devices, per_device(): lax.all_to_all(w_out, ('tasks', 'grp'), split_axis=0, concat_axis=0, tile...  9.49 us
    all_to_all x1, starting transfers between devices, per_device(): lax.all_to_all(partials, 'tasks', split_axis=0, concat_axis=0, tiled=True)  8.24 us
    ppermute x8, waiting for transfers between devices, move(): return lax.ppermute(part, 'tasks', shift(k, first_axis))  6.76 us
  transfers between devices with their start and end apart: 14, of which 8 were waited for; matrix products, arithmetic and copies ran while one was open for 2% of the time, Pallas kernels for 5%

profile of v4, /device:TPU:33, one launch (start us, length us, event | category | flops | bytes accessed | tf_op | source)
XLA Modules:
  0.0 117.6 jit_solution(2362004934665512229)
XLA Ops:
  0.0 0.0 copy-start
  0.0 5.0 %prepare.1 = (bf16[16,128,128]{2,1,0:T(8,128)(2,1)}, bf16[16,128,128]{2,1,0:T(8,128)(2,1)}, bf16[16,128,128]{2,1,0:T(8,128)(2,1)}, bf16[16,128,128]{2,1,0:T(8,128)(2,1)}, bf16[128,128,128]{2,1,0:T(8,128)(2,1)}) custom-call(s32[1,2048]{1,0:T(1,128)} %t_home_hbm.1, s32[2,32]{1,0:T(2,128)} %bitcast.40, bf16[64,128,128]{2,1,0:T(8,128)(2,1)} %bitcast.36, ...), custom_call_target="tpu_custom_call" | custom-call | tf_op jit(solution)/shard_map/prepare/pallas_call | solution.py:88
  5.0 1.3 %collective-permute-start = (bf16[16,128,128]{2,1,0:T(8,128)(2,1)}, bf16[16,128,128]{2,1,0:T(8,128)(2,1)S(1)}, u32[]{:S(2)}, u32[]{:S(2)}) collective-permute-start(bf16[16,128,128]{2,1,0:T(8,128)(2,1)} %get-tuple-element.27), channel_id=1, source_target_pairs={{0,32},{4,12},{8,40},{12,20},{16,48},{20,28},{24,56},{28,4},{32,64... | collective-permute-start | bytes 1572872 | tf_op jit(solution)/shard_map/ppermute | solution.py:159
  6.3 2.4 %collective-permute-start.1 = (bf16[16,128,128]{2,1,0:T(8,128)(2,1)}, bf16[16,128,128]{2,1,0:T(8,128)(2,1)S(1)}, u32[]{:S(2)}, u32[]{:S(2)}) collective-permute-start(bf16[16,128,128]{2,1,0:T(8,128)(2,1)} %get-tuple-element.28), channel_id=1, source_target_pairs={{0,64},{4,20},{8,72},{12,28},{16,80},{20,4},{24,88},{28,12},{32,96... | collective-permute-start | bytes 1572872 | tf_op jit(solution)/shard_map/ppermute | solution.py:159
  8.7 1.2 collective-permute-start.2
  9.9 9.5 %all-to-all-start = ((bf16[128,128,128]{2,1,0:T(8,128)(2,1)}), bf16[128,128,128]{2,1,0:T(8,128)(2,1)}, u32[]{:S(2)}, u32[]{:S(2)}) async-start(bf16[128,128,128]{2,1,0:T(8,128)(2,1)} %get-tuple-element.25), calls=%async_computation | async-start | bytes 8388608 | tf_op jit(solution)/shard_map/all_to_all | solution.py:317
  19.4 0.0 collective-permute-done.refs_1_
  19.4 0.0 copy-start.6
  19.4 2.0 %collective-permute-done.1.refs_2_ = bf16[16,128,128]{2,1,0:T(8,128)(2,1)S(1)} collective-permute-done((bf16[16,128,128]{2,1,0:T(8,128)(2,1)}, bf16[16,128,128]{2,1,0:T(8,128)(2,1)S(1)}, u32[]{:S(2)}, u32[]{:S(2)}) %collective-permute-start.1) | collective-permute-done | bytes 524320 | tf_op jit(solution)/shard_map/ppermute | solution.py:159
  21.4 0.0 copy-start.7
  21.4 0.0 collective-permute-done.2.refs_3_
  21.4 0.0 copy-start.8
  21.4 0.0 copy-done.6
  21.4 0.8 copy-done.7
  22.2 0.2 copy-done.8
  22.4 3.1 %regroup.1 = (bf16[8,128,128]{2,1,0:T(8,128)(2,1)}, bf16[8,128,128]{2,1,0:T(8,128)(2,1)}, bf16[8,128,128]{2,1,0:T(8,128)(2,1)}, bf16[8,128,128]{2,1,0:T(8,128)(2...) custom-call(bf16[16,128,128]{2,1,0:T(8,128)(2,1)} %get-tuple-element.26.refs_0_, ...), custom_call_target="tpu_custom_call" | custom-call | flops 99999997952 | bytes 4194304 | tf_op jit(solution)/shard_map/regroup/pallas_call | solution.py:136
  25.5 16.1 %collective-permute-start.3 = (bf16[8,128,128]{2,1,0:T(8,128)(2,1)}, bf16[8,128,128]{2,1,0:T(8,128)(2,1)S(1)}, u32[]{:S(2)}, u32[]{:S(2)}) collective-permute-start(bf16[8,128,128]{2,1,0:T(8,128)(2,1)} %get-tuple-element.32), channel_id=1, source_target_pairs={{0,4},{4,0},{8,12},{12,8},{16,20},{20,16},{24,28},{28,24},{32,36},... | collective-permute-start | bytes 786440 | tf_op jit(solution)/shard_map/ppermute | solution.py:163
  41.6 0.1 collective-permute-start.4
  41.6 0.4 collective-permute-start.5
  42.1 0.9 collective-permute-done.3.refs_4_
  42.9 0.4 collective-permute-done.4
  43.3 0.4 collective-permute-done.5
  43.7 0.0 collective-permute-start.6
  43.7 0.0 copy-start.2
  43.7 0.0 copy-start.3
  43.7 0.0 copy-start.1
  43.7 9.5 %collective-permute-start.7 = (bf16[8,128,128]{2,1,0:T(8,128)(2,1)}, bf16[8,128,128]{2,1,0:T(8,128)(2,1)S(1)}, u32[]{:S(2)}, u32[]{:S(2)}) collective-permute-start(bf16[8,128,128]{2,1,0:T(8,128)(2,1)} %get-tuple-element.39), channel_id=1, source_target_pairs={{0,8},{4,36},{8,16},{12,44},{16,24},{20,52},{24,0},{28,60},{32,40}... | collective-permute-start | bytes 786440 | tf_op jit(solution)/shard_map/ppermute | solution.py:159
  53.2 0.0 collective-permute-start.8
  53.2 4.2 %collective-permute-start.9 = (bf16[8,128,128]{2,1,0:T(8,128)(2,1)S(1)}, bf16[8,128,128]{2,1,0:T(8,128)(2,1)S(1)}, u32[]{:S(2)}, u32[]{:S(2)}) collective-permute-start(bf16[8,128,128]{2,1,0:T(8,128)(2,1)S(1)} %collective-permute-done.4), channel_id=1, source_target_pairs={{0,32},{4,12},{8,40},{12,20},{16,48},{20,28},{24,56},{28,4},{32,64... | collective-permute-start | bytes 786440 | tf_op jit(solution)/shard_map/ppermute | solution.py:159
  57.4 0.3 collective-permute-start.11
  57.7 13.8 %all-to-all-done.hbm = bf16[128,128,128]{2,1,0:T(8,128)(2,1)} async-done(((bf16[128,128,128]{2,1,0:T(8,128)(2,1)}), bf16[128,128,128]{2,1,0:T(8,128)(2,1)}, u32[]{:S(2)}, u32[]{:S(2)}) %all-to-all-start) | async-done | bytes 4194336 | tf_op jit(solution)/shard_map/all_to_all | solution.py:317
  71.6 2.2 %stage.1.w_ref = bf16[128,128,128]{2,1,0:T(8,128)(2,1)S(1)} custom-call(bf16[128,128,128]{2,1,0:T(8,128)(2,1)} %all-to-all-done.hbm), custom_call_target="tpu_custom_call" | custom-call | flops 5000000000 | bytes 8388608 | tf_op jit(solution)/shard_map/stage/pallas_call | solution.py:193
  73.8 2.1 %collective-permute-done.6.refs_2_ = bf16[16,128,128]{2,1,0:T(8,128)(2,1)S(1)} collective-permute-done((bf16[16,128,128]{2,1,0:T(8,128)(2,1)}, bf16[16,128,128]{2,1,0:T(8,128)(2,1)S(1)}, u32[]{:S(2)}, u32[]{:S(2)}) %collective-permute-start.6) | collective-permute-done | bytes 524320 | tf_op jit(solution)/shard_map/ppermute | solution.py:159
  75.9 0.2 collective-permute-start.10
  76.1 0.0 copy-done.2
  76.1 0.1 fusion.9
  76.2 0.0 copy-done.3
  76.2 2.6 %collective-permute-done.7.refs_1_ = bf16[8,128,128]{2,1,0:T(8,128)(2,1)S(1)} collective-permute-done((bf16[8,128,128]{2,1,0:T(8,128)(2,1)}, bf16[8,128,128]{2,1,0:T(8,128)(2,1)S(1)}, u32[]{:S(2)}, u32[]{:S(2)}) %collective-permute-start.7) | collective-permute-done | bytes 262176 | tf_op jit(solution)/shard_map/ppermute | solution.py:159
  78.8 0.0 collective-permute-done.8.refs_3_
  78.8 0.0 collective-permute-done.9.refs_5_
  78.8 0.0 collective-permute-done.11.refs_7_
  78.8 0.0 collective-permute-done.10.refs_6_
  78.9 0.0 copy-done.1
  78.9 0.0 copy-start.5
  78.9 0.0 copy-start.9
  78.9 0.0 copy-start.4
  78.9 11.7 %products.1 = bf16[32,128,128]{2,1,0:T(8,128)(2,1)} custom-call(s32[2,32,32]{2,1,0:T(8,128)S(1)} %pad_add_fusion.task_ref, bf16[128,128,128]{2,1,0:T(8,128)(2,1)S(1)} %stage.1.w_ref, bf16[8,128,128]{2,1,0:T(8,128)(2,1)S(1)} %copy-done.1, bf16[8,128,128]{2,1,0:T(8,128)(2,1)S(1)} %collective-permute-done.7.refs_1_, ...), custom_call_target="tpu_custom_call" | custom-call | flops 4294967296 | bytes 7340032 | tf_op jit(solution)/shard_map/products/pallas_call | solution.py:248
  90.6 8.2 %all-to-all-start.1 = ((bf16[32,128,128]{2,1,0:T(8,128)(2,1)}), bf16[32,128,128]{2,1,0:T(8,128)(2,1)S(1)}, u32[]{:S(2)}, u32[]{:S(2)}) async-start(bf16[32,128,128]{2,1,0:T(8,128)(2,1)} %products.1), calls=%async_computation.1 | async-start | bytes 2097152 | tf_op jit(solution)/shard_map/all_to_all | solution.py:321
  98.8 0.0 copy-done
  98.8 0.1 constant_dynamic-slice_fusion
  98.9 0.6 fusion.15
  103.2 0.0 copy-done.5
  103.2 0.7 fusion.14
  105.1 0.0 copy-done.9
  105.1 0.1 select_reduce_fusion.1
  105.3 0.0 copy-done.4
  105.3 0.3 subtract_divide_fusion.inverse_ref
  105.7 10.3 %all-to-all-done.1.in_ref = bf16[32,128,128]{2,1,0:T(8,128)(2,1)S(1)} async-done(((bf16[32,128,128]{2,1,0:T(8,128)(2,1)}), bf16[32,128,128]{2,1,0:T(8,128)(2,1)S(1)}, u32[]{:S(2)}, u32[]{:S(2)}) %all-to-all-start.1) | async-done | bytes 1048608 | tf_op jit(solution)/shard_map/all_to_all | solution.py:321
  116.0 1.6 %finish.1 = f32[16,128,128]{2,1,0:T(8,128)} custom-call(s32[2,16]{1,0:T(2,128)S(1)} %pad_add_fusion.1.slot_ref, bf16[32,128,128]{2,1,0:T(8,128)(2,1)S(1)} %all-to-all-done.1.in_ref, f32[16,128,128]{2,1,0:T(8,128)S(1)} %subtract_divide_fusion.inverse_ref), custom_call_target="tpu_custom_call" | custom-call | tf_op jit(solution)/shard_map/finish/pallas_call | solution.py:279
  (5 shorter events, 0.1 us)
Async XLA Ops:
  0.0 98.8 %copy-start = (s32[32,2]{0,1:T(2,128)S(1)}, s32[32,2]{0,1:T(2,128)}, u32[]{:S(2)}) copy-start(s32[32,2]{0,1:T(2,128)} %param.25) | copy-start | bytes 772
  5.0 14.4 %collective-permute-start = (bf16[16,128,128]{2,1,0:T(8,128)(2,1)}, bf16[16,128,128]{2,1,0:T(8,128)(2,1)S(1)}, u32[]{:S(2)}, u32[]{:S(2)}) collective-permute-start(bf16[16,128,128]{2,1,0:T(8,128)(2,1)} %get-tuple-element.27), channel_id=1, source_target_pairs={{0,32},{4,12},{8,40},{12,20},{16,48},{20,28},{24,56},{28,4},{32,64... | collective-permute-start | bytes 1572872 | tf_op jit(solution)/shard_map/ppermute | solution.py:159
  6.3 15.1 %collective-permute-start.1 = (bf16[16,128,128]{2,1,0:T(8,128)(2,1)}, bf16[16,128,128]{2,1,0:T(8,128)(2,1)S(1)}, u32[]{:S(2)}, u32[]{:S(2)}) collective-permute-start(bf16[16,128,128]{2,1,0:T(8,128)(2,1)} %get-tuple-element.28), channel_id=1, source_target_pairs={{0,64},{4,20},{8,72},{12,28},{16,80},{20,4},{24,88},{28,12},{32,96... | collective-permute-start | bytes 1572872 | tf_op jit(solution)/shard_map/ppermute | solution.py:159
  8.7 12.7 %collective-permute-start.2 = (bf16[16,128,128]{2,1,0:T(8,128)(2,1)}, bf16[16,128,128]{2,1,0:T(8,128)(2,1)S(1)}, u32[]{:S(2)}, u32[]{:S(2)}) collective-permute-start(bf16[16,128,128]{2,1,0:T(8,128)(2,1)} %get-tuple-element.29), channel_id=1, source_target_pairs={{0,96},{4,28},{8,104},{12,4},{16,112},{20,12},{24,120},{28,20},{32... | collective-permute-start | bytes 1572872 | tf_op jit(solution)/shard_map/ppermute | solution.py:159
  9.9 61.7 %all-to-all-start = ((bf16[128,128,128]{2,1,0:T(8,128)(2,1)}), bf16[128,128,128]{2,1,0:T(8,128)(2,1)}, u32[]{:S(2)}, u32[]{:S(2)}) async-start(bf16[128,128,128]{2,1,0:T(8,128)(2,1)} %get-tuple-element.25), calls=%async_computation | async-start | bytes 8388608 | tf_op jit(solution)/shard_map/all_to_all | solution.py:317
  19.4 2.0 %copy-start.6 = (bf16[16,128,128]{2,1,0:T(8,128)(2,1)}, bf16[16,128,128]{2,1,0:T(8,128)(2,1)S(1)}, u32[]{:S(2)}) copy-start(bf16[16,128,128]{2,1,0:T(8,128)(2,1)S(1)} %collective-permute-done.refs_1_) | copy-start | bytes 1572868
  21.4 0.8 copy-start.7
  21.4 1.0 copy-start.8
  25.5 17.4 %collective-permute-start.3 = (bf16[8,128,128]{2,1,0:T(8,128)(2,1)}, bf16[8,128,128]{2,1,0:T(8,128)(2,1)S(1)}, u32[]{:S(2)}, u32[]{:S(2)}) collective-permute-start(bf16[8,128,128]{2,1,0:T(8,128)(2,1)} %get-tuple-element.32), channel_id=1, source_target_pairs={{0,4},{4,0},{8,12},{12,8},{16,20},{20,16},{24,28},{28,24},{32,36},... | collective-permute-start | bytes 786440 | tf_op jit(solution)/shard_map/ppermute | solution.py:163
  41.6 1.7 %collective-permute-start.4 = (bf16[8,128,128]{2,1,0:T(8,128)(2,1)}, bf16[8,128,128]{2,1,0:T(8,128)(2,1)S(1)}, u32[]{:S(2)}, u32[]{:S(2)}) collective-permute-start(bf16[8,128,128]{2,1,0:T(8,128)(2,1)} %get-tuple-element.33), channel_id=1, source_target_pairs={{0,4},{4,0},{8,12},{12,8},{16,20},{20,16},{24,28},{28,24},{32,36},... | collective-permute-start | bytes 786440 | tf_op jit(solution)/shard_map/ppermute | solution.py:163
  41.6 2.0 %collective-permute-start.5 = (bf16[8,128,128]{2,1,0:T(8,128)(2,1)}, bf16[8,128,128]{2,1,0:T(8,128)(2,1)S(1)}, u32[]{:S(2)}, u32[]{:S(2)}) collective-permute-start(bf16[8,128,128]{2,1,0:T(8,128)(2,1)} %get-tuple-element.34), channel_id=1, source_target_pairs={{0,4},{4,0},{8,12},{12,8},{16,20},{20,16},{24,28},{28,24},{32,36},... | collective-permute-start | bytes 786440 | tf_op jit(solution)/shard_map/ppermute | solution.py:163
  43.7 32.2 %collective-permute-start.6 = (bf16[16,128,128]{2,1,0:T(8,128)(2,1)}, bf16[16,128,128]{2,1,0:T(8,128)(2,1)S(1)}, u32[]{:S(2)}, u32[]{:S(2)}) collective-permute-start(bf16[16,128,128]{2,1,0:T(8,128)(2,1)} %get-tuple-element.36), channel_id=1, source_target_pairs={{0,16},{4,68},{8,24},{12,76},{16,0},{20,84},{24,8},{28,92},{32,48}... | collective-permute-start | bytes 1572872 | tf_op jit(solution)/shard_map/ppermute | solution.py:159
  43.7 32.4 %copy-start.2 = (s32[1,1,32,32]{3,2,1,0:T(8,128)S(1)}, s32[1,1,32,32]{3,2,1,0:T(8,128)}, u32[]{:S(2)}) copy-start(s32[1,1,32,32]{3,2,1,0:T(8,128)} %param.22) | copy-start | bytes 12292
  43.7 32.5 %copy-start.3 = (s32[1,1,32,32]{3,2,1,0:T(8,128)S(1)}, s32[1,1,32,32]{3,2,1,0:T(8,128)}, u32[]{:S(2)}) copy-start(s32[1,1,32,32]{3,2,1,0:T(8,128)} %param.23) | copy-start | bytes 12292
  43.7 35.2 %copy-start.1 = (bf16[8,128,128]{2,1,0:T(8,128)(2,1)S(1)}, bf16[8,128,128]{2,1,0:T(8,128)(2,1)}, u32[]{:S(2)}) copy-start(bf16[8,128,128]{2,1,0:T(8,128)(2,1)} %get-tuple-element.38.refs_0_) | copy-start | bytes 786436
  43.7 35.1 %collective-permute-start.7 = (bf16[8,128,128]{2,1,0:T(8,128)(2,1)}, bf16[8,128,128]{2,1,0:T(8,128)(2,1)S(1)}, u32[]{:S(2)}, u32[]{:S(2)}) collective-permute-start(bf16[8,128,128]{2,1,0:T(8,128)(2,1)} %get-tuple-element.39), channel_id=1, source_target_pairs={{0,8},{4,36},{8,16},{12,44},{16,24},{20,52},{24,0},{28,60},{32,40}... | collective-permute-start | bytes 786440 | tf_op jit(solution)/shard_map/ppermute | solution.py:159
  53.2 25.6 %collective-permute-start.8 = (bf16[8,128,128]{2,1,0:T(8,128)(2,1)}, bf16[8,128,128]{2,1,0:T(8,128)(2,1)S(1)}, u32[]{:S(2)}, u32[]{:S(2)}) collective-permute-start(bf16[8,128,128]{2,1,0:T(8,128)(2,1)} %get-tuple-element.41), channel_id=1, source_target_pairs={{0,24},{4,100},{8,0},{12,108},{16,8},{20,116},{24,16},{28,124},{32... | collective-permute-start | bytes 786440 | tf_op jit(solution)/shard_map/ppermute | solution.py:159
  53.2 25.6 %collective-permute-start.9 = (bf16[8,128,128]{2,1,0:T(8,128)(2,1)S(1)}, bf16[8,128,128]{2,1,0:T(8,128)(2,1)S(1)}, u32[]{:S(2)}, u32[]{:S(2)}) collective-permute-start(bf16[8,128,128]{2,1,0:T(8,128)(2,1)S(1)} %collective-permute-done.4), channel_id=1, source_target_pairs={{0,32},{4,12},{8,40},{12,20},{16,48},{20,28},{24,56},{28,4},{32,64... | collective-permute-start | bytes 786440 | tf_op jit(solution)/shard_map/ppermute | solution.py:159
  57.4 21.4 %collective-permute-start.11 = (bf16[8,128,128]{2,1,0:T(8,128)(2,1)S(1)}, bf16[8,128,128]{2,1,0:T(8,128)(2,1)S(1)}, u32[]{:S(2)}, u32[]{:S(2)}) collective-permute-start(bf16[8,128,128]{2,1,0:T(8,128)(2,1)S(1)} %collective-permute-done.5), channel_id=1, source_target_pairs={{0,96},{4,28},{8,104},{12,4},{16,112},{20,12},{24,120},{28,20},{32... | collective-permute-start | bytes 786440 | tf_op jit(solution)/shard_map/ppermute | solution.py:159
  75.9 2.9 %collective-permute-start.10 = (bf16[8,128,128]{2,1,0:T(8,128)(2,1)S(1)}, bf16[8,128,128]{2,1,0:T(8,128)(2,1)S(1)}, u32[]{:S(2)}, u32[]{:S(2)}) collective-permute-start(bf16[8,128,128]{2,1,0:T(8,128)(2,1)S(1)} %slice.11), channel_id=1, source_target_pairs={{0,4},{4,0},{8,12},{12,8},{16,20},{20,16},{24,28},{28,24},{32,36},... | collective-permute-start | bytes 786440 | tf_op jit(solution)/shard_map/ppermute | solution.py:163
  78.9 24.4 %copy-start.5 = (f32[300]{0:T(512)S(1)}, f32[300]{0:T(512)}, u32[]{:S(2)}) copy-start(f32[300]{0:T(512)} %param.26) | copy-start | bytes 3604
  78.9 26.3 %copy-start.9 = (s32[1,1,32,1]{2,3,1,0:T(1,128)S(1)}, s32[1,1,32,1]{2,3,1,0:T(1,128)}, u32[]{:S(2)}) copy-start(s32[1,1,32,1]{2,3,1,0:T(1,128)} %param.24) | copy-start | bytes 388
  78.9 26.4 %copy-start.4 = (f32[1024]{0:T(1024)S(1)}, f32[1024]{0:T(1024)}, u32[]{:S(2)}) copy-start(f32[1024]{0:T(1024)} %param.27) | copy-start | bytes 12292
  90.6 25.4 %all-to-all-start.1 = ((bf16[32,128,128]{2,1,0:T(8,128)(2,1)}), bf16[32,128,128]{2,1,0:T(8,128)(2,1)S(1)}, u32[]{:S(2)}, u32[]{:S(2)}) async-start(bf16[32,128,128]{2,1,0:T(8,128)(2,1)} %products.1), calls=%async_computation.1 | async-start | bytes 2097152 | tf_op jit(solution)/shard_map/all_to_all | solution.py:321

commit v5 on v4

--- a/solution.py
+++ b/solution.py
@@ -18,29 +18,51 @@
 def prepare_kernel(t_home_hbm, t_send_hbm, store_hbm, w_home_hbm, w_send_hbm, ovvo_hbm, ovvv_hbm, dress_hbm, *refs):
     t_outs, w_out, scratch = refs[:SIDE], refs[SIDE], refs[SIDE + 1 :]
     t_home, t_send, store, w_home, w_send, ovvo, ovvv, dress, t_stage, formed, w_stage, in_sems, t_sems, w_sems = scratch
+    w_per_dev, rows, cols = formed.shape
+    half = w_per_dev // 2
+    pairs = [(dress_hbm, dress)]
+    for c in range(2):
+        part = pl.ds(c * half, half)
+        pairs += [(ovvv_hbm.at[part], ovvv.at[part]), (ovvo_hbm.at[part], ovvo.at[part])]
+    pairs += [(w_home_hbm, w_home), (w_send_hbm, w_send), (t_home_hbm, t_home), (t_send_hbm, t_send)]
+    pairs += [(store_hbm, store)]
     loads = []
-    for i, (src, dst) in enumerate(
-        (
-            (t_home_hbm, t_home),
-            (t_send_hbm, t_send),
-            (store_hbm, store),
-            (ovvv_hbm, ovvv),
-            (ovvo_hbm, ovvo),
-            (dress_hbm, dress),
-            (w_home_hbm, w_home),
-            (w_send_hbm, w_send),
-        )
-    ):
+    for i, (src, dst) in enumerate(pairs):
         loads.append(pltpu.make_async_copy(src, dst, in_sems.at[i]))
         loads[-1].start()
 
-    for load in loads[:3]:
+    step = 4
+    loads[0].wait()
+    for c in range(2):
+        loads[1 + 2 * c].wait()
+        loads[2 + 2 * c].wait()
+        for i in range(c * half, (c + 1) * half, step):
+            block = ovvv[i : i + step].reshape(step * rows, cols)
+            dressed = jnp.dot(block, dress[...], preferred_element_type=jnp.float32)
+            total = ovvo[i : i + step].astype(jnp.float32) + dressed.reshape(step, rows, cols)
+            formed[i : i + step] = total.astype(jnp.bfloat16)
+    for load in loads[5:7]:
+        load.wait()
+    copies = []
+    count = w_out.shape[0]
+    chunk = count // CHUNKS
+    for c in range(CHUNKS):
+
+        def pick(i, carry):
+            w_stage[i] = formed[lax.rem(w_home[w_send[0, i]], w_per_dev)]
+            return carry
+
+        lax.fori_loop(c * chunk, (c + 1) * chunk, pick, 0, unroll=8)
+        part = pl.ds(c * chunk, chunk)
+        copies.append(pltpu.make_async_copy(w_stage.at[part], w_out.at[part], w_sems.at[c]))
+        copies[-1].start()
+
+    for load in loads[7:]:
         load.wait()
     t_per_dev = store.shape[0]
     cap = t_send.shape[0]
     pos = lax.axis_index("tasks")
     y, x, core = pos // (2 * SIDE), lax.rem(pos // 2, SIDE), lax.rem(pos, 2)
-    copies = []
     for first in (1, 2, 3, 0):
         for second in range(SIDE):
             dy = jnp.where(core == 0, first, second)
@@ -52,28 +74,6 @@
                     row = lax.rem(t_home[0, t_send[c, there]], t_per_dev)
                     t_stage[first, (second * 2 + other) * cap + c] = store[row]
         copies.append(pltpu.make_async_copy(t_stage.at[first], t_outs[first], t_sems.at[first]))
-        copies[-1].start()
-
-    for load in loads[3:]:
-        load.wait()
-    w_per_dev, rows, cols = formed.shape
-    step = 4
-    for i in range(0, w_per_dev, step):
-        block = ovvv[i : i + step].reshape(step * rows, cols)
-        dressed = jnp.dot(block, dress[...], preferred_element_type=jnp.float32)
-        total = ovvo[i : i + step].astype(jnp.float32) + dressed.reshape(step, rows, cols)
-        formed[i : i + step] = total.astype(jnp.bfloat16)
-    count = w_out.shape[0]
-    chunk = count // CHUNKS
-    for c in range(CHUNKS):
-
-        def pick(i, carry):
-            w_stage[i] = formed[lax.rem(w_home[w_send[0, i]], w_per_dev)]
-            return carry
-
-        lax.fori_loop(c * chunk, (c + 1) * chunk, pick, 0, unroll=8)
-        part = pl.ds(c * chunk, chunk)
-        copies.append(pltpu.make_async_copy(w_stage.at[part], w_out.at[part], w_sems.at[c]))
         copies[-1].start()
     for copy in copies:
         copy.wait()
@@ -102,7 +102,7 @@
             pltpu.VMEM((SIDE,) + t_part.shape, store.dtype),
             pltpu.VMEM((w_per_dev, rows, cols), jnp.bfloat16),
             pltpu.VMEM(w_all.shape, jnp.bfloat16),
-            pltpu.SemaphoreType.DMA((8,)),
+            pltpu.SemaphoreType.DMA((10,)),
             pltpu.SemaphoreType.DMA((SIDE,)),
             pltpu.SemaphoreType.DMA((CHUNKS,)),
         ],
@@ -213,9 +213,9 @@
     return (group * SIDE + first) * cap + task_t % cap
 
 
-def products_kernel(task_ref, w_ref, *refs):
-    parts, (out_ref, t_ref, sems) = refs[: 2 * SIDE], refs[2 * SIDE :]
-    copies = []
+def products_kernel(task_hbm, w_ref, *refs):
+    parts, (out_hbm, out_ref, task_ref, t_ref, sems, out_sems) = refs[: 2 * SIDE], refs[2 * SIDE :]
+    copies = [pltpu.make_async_copy(task_hbm, task_ref, sems.at[2 * SIDE])]
     count = parts[0].shape[0]
     for i, part in enumerate(parts):
         part = part.at[pl.ds(part.shape[0] - count, count)]
@@ -226,7 +226,12 @@
         copy.wait()
     slots, rows, cols = out_ref.shape
     per_slot = task_ref.shape[2]
-    width, together = 4, 8
+    width, pieces = 4, out_sems.shape[0]
+    together = slots // pieces
+
+    def out(i):
+        part = pl.ds(i * together, together)
+        return pltpu.make_async_copy(out_ref.at[part], out_hbm.at[part], out_sems.at[i])
 
     def group(i, carry):
         for u in range(together):
@@ -237,9 +242,12 @@
                 right = jnp.concatenate([w_ref[task_ref[1, s, k + j]] for j in range(width)], axis=0)
                 acc = acc + jnp.dot(left, right, preferred_element_type=jnp.float32)
             out_ref[s] = acc.astype(out_ref.dtype)
+        out(i).start()
         return carry
 
-    lax.fori_loop(0, slots // together, group, 0)
+    lax.fori_loop(0, pieces, group, 0)
+    for i in range(pieces):
+        out(i).wait()
 
 
 def products(tasks, t_parts, w_fetched):
@@ -248,11 +256,14 @@
     return pl.pallas_call(
         products_kernel,
         out_shape=jax.ShapeDtypeStruct((slots, rows, cols), jnp.bfloat16),
-        in_specs=[SMEM, VMEM] + [HBM] * (2 * SIDE),
-        out_specs=VMEM,
+        in_specs=[HBM, VMEM] + [HBM] * (2 * SIDE),
+        out_specs=HBM,
         scratch_shapes=[
+            pltpu.VMEM((slots, rows, cols), jnp.bfloat16),
+            pltpu.SMEM(tasks.shape, tasks.dtype),
             pltpu.VMEM((2 * SIDE * count, rows, cols), jnp.bfloat16),
-            pltpu.SemaphoreType.DMA((2 * SIDE,)),
+            pltpu.SemaphoreType.DMA((2 * SIDE + 1,)),
+            pltpu.SemaphoreType.DMA((2,)),
         ],
         compiler_params=pltpu.CompilerParams(vmem_limit_bytes=VMEM_BYTES),
         cost_estimate=pl.CostEstimate(flops=2 * slots * per_slot * rows * cols * cols, bytes_accessed=7 << 20, transcendentals=0),

time: 118 us -> 117 us (level)
  no operation moved by 1% of the time
where the time goes in v5:
time: 117 us
  starting transfers between devices  53.4 us (46%)
  waiting for transfers between devices  32.5 us (28%)
  Pallas kernels  22.8 us (19%)
  between operations  5.2 us (4%)
  local copies, waits for them, and re-layouts  2.36 us (2%)
    ppermute x8, starting transfers between devices, move(): return lax.ppermute(part, 'tasks', shift(k, first_axis))  18.9 us
    ppermute x4, starting transfers between devices, swap_cores(): lax.ppermute(part, 'tasks', [(i, i ^ 1) for i in range(2 * SIDE * SIDE)])  16.8 us
    all_to_all x1, waiting for transfers between devices, per_device(): lax.all_to_all(w_out, ('tasks', 'grp'), split_axis=0, concat_axis=0, tile...  13.8 us
    pallas_call x1, Pallas kernels, products(): pl.pallas_call(products_kernel, out_shape=jax.ShapeDtypeStruct((slots, ro...  11.1 us
    all_to_all x1, waiting for transfers between devices, per_device(): lax.all_to_all(partials, 'tasks', split_axis=0, concat_axis=0, tiled=True)  10.3 us
    all_to_all x1, starting transfers between devices, per_device(): lax.all_to_all(w_out, ('tasks', 'grp'), split_axis=0, concat_axis=0, tile...  9.49 us
    all_to_all x1, starting transfers between devices, per_device(): lax.all_to_all(partials, 'tasks', split_axis=0, concat_axis=0, tiled=True)  8.24 us
    ppermute x8, waiting for transfers between devices, move(): return lax.ppermute(part, 'tasks', shift(k, first_axis))  6.76 us
  transfers between devices with their start and end apart: 14, of which 8 were waited for; matrix products, arithmetic and copies ran while one was open for 2% of the time, Pallas kernels for 5%

profile of v5, /device:TPU:33, one launch (start us, length us, event | category | flops | bytes accessed | tf_op | source)
XLA Modules:
  0.0 116.8 jit_solution(5988939018686093467)
XLA Ops:
  0.0 0.0 copy-start
  0.0 4.8 %prepare.1 = (bf16[16,128,128]{2,1,0:T(8,128)(2,1)}, bf16[16,128,128]{2,1,0:T(8,128)(2,1)}, bf16[16,128,128]{2,1,0:T(8,128)(2,1)}, bf16[16,128,128]{2,1,0:T(8,128)(2,1)}, bf16[128,128,128]{2,1,0:T(8,128)(2,1)}) custom-call(s32[1,2048]{1,0:T(1,128)} %t_home_hbm.1, s32[2,32]{1,0:T(2,128)} %bitcast.40, bf16[64,128,128]{2,1,0:T(8,128)(2,1)} %bitcast.36, ...), custom_call_target="tpu_custom_call" | custom-call | tf_op jit(solution)/shard_map/prepare/pallas_call | solution.py:88
  4.8 1.3 %collective-permute-start = (bf16[16,128,128]{2,1,0:T(8,128)(2,1)}, bf16[16,128,128]{2,1,0:T(8,128)(2,1)S(1)}, u32[]{:S(2)}, u32[]{:S(2)}) collective-permute-start(bf16[16,128,128]{2,1,0:T(8,128)(2,1)} %get-tuple-element.27), channel_id=1, source_target_pairs={{0,32},{4,12},{8,40},{12,20},{16,48},{20,28},{24,56},{28,4},{32,64... | collective-permute-start | bytes 1572872 | tf_op jit(solution)/shard_map/ppermute | solution.py:159
  6.1 2.4 %collective-permute-start.1 = (bf16[16,128,128]{2,1,0:T(8,128)(2,1)}, bf16[16,128,128]{2,1,0:T(8,128)(2,1)S(1)}, u32[]{:S(2)}, u32[]{:S(2)}) collective-permute-start(bf16[16,128,128]{2,1,0:T(8,128)(2,1)} %get-tuple-element.28), channel_id=1, source_target_pairs={{0,64},{4,20},{8,72},{12,28},{16,80},{20,4},{24,88},{28,12},{32,96... | collective-permute-start | bytes 1572872 | tf_op jit(solution)/shard_map/ppermute | solution.py:159
  8.5 1.2 collective-permute-start.2
  9.7 9.5 %all-to-all-start = ((bf16[128,128,128]{2,1,0:T(8,128)(2,1)}), bf16[128,128,128]{2,1,0:T(8,128)(2,1)}, u32[]{:S(2)}, u32[]{:S(2)}) async-start(bf16[128,128,128]{2,1,0:T(8,128)(2,1)} %get-tuple-element.25), calls=%async_computation | async-start | bytes 8388608 | tf_op jit(solution)/shard_map/all_to_all | solution.py:328
  19.2 0.0 collective-permute-done.refs_1_
  19.2 0.0 copy-start.6
  19.2 2.0 %collective-permute-done.1.refs_2_ = bf16[16,128,128]{2,1,0:T(8,128)(2,1)S(1)} collective-permute-done((bf16[16,128,128]{2,1,0:T(8,128)(2,1)}, bf16[16,128,128]{2,1,0:T(8,128)(2,1)S(1)}, u32[]{:S(2)}, u32[]{:S(2)}) %collective-permute-start.1) | collective-permute-done | bytes 524320 | tf_op jit(solution)/shard_map/ppermute | solution.py:159
  21.2 0.0 copy-start.7
  21.2 0.0 collective-permute-done.2.refs_3_
  21.2 0.0 copy-start.8
  21.2 0.0 copy-done.6
  21.2 0.8 copy-done.7
  22.0 0.2 copy-done.8
  22.2 3.1 %regroup.1 = (bf16[8,128,128]{2,1,0:T(8,128)(2,1)}, bf16[8,128,128]{2,1,0:T(8,128)(2,1)}, bf16[8,128,128]{2,1,0:T(8,128)(2,1)}, bf16[8,128,128]{2,1,0:T(8,128)(2...) custom-call(bf16[16,128,128]{2,1,0:T(8,128)(2,1)} %get-tuple-element.26.refs_0_, ...), custom_call_target="tpu_custom_call" | custom-call | flops 99999997952 | bytes 4194304 | tf_op jit(solution)/shard_map/regroup/pallas_call | solution.py:136
  25.3 16.1 %collective-permute-start.3 = (bf16[8,128,128]{2,1,0:T(8,128)(2,1)}, bf16[8,128,128]{2,1,0:T(8,128)(2,1)S(1)}, u32[]{:S(2)}, u32[]{:S(2)}) collective-permute-start(bf16[8,128,128]{2,1,0:T(8,128)(2,1)} %get-tuple-element.32), channel_id=1, source_target_pairs={{0,4},{4,0},{8,12},{12,8},{16,20},{20,16},{24,28},{28,24},{32,36},... | collective-permute-start | bytes 786440 | tf_op jit(solution)/shard_map/ppermute | solution.py:163
  41.4 0.1 collective-permute-start.4
  41.5 0.4 collective-permute-start.5
  41.9 0.9 collective-permute-done.3.refs_4_
  42.7 0.4 collective-permute-done.4
  43.1 0.4 collective-permute-done.5
  43.5 0.0 collective-permute-start.6
  43.5 0.0 copy-start.2
  43.5 0.0 copy-start.3
  43.5 0.0 copy-start.1
  43.5 9.5 %collective-permute-start.7 = (bf16[8,128,128]{2,1,0:T(8,128)(2,1)}, bf16[8,128,128]{2,1,0:T(8,128)(2,1)S(1)}, u32[]{:S(2)}, u32[]{:S(2)}) collective-permute-start(bf16[8,128,128]{2,1,0:T(8,128)(2,1)} %get-tuple-element.39), channel_id=1, source_target_pairs={{0,8},{4,36},{8,16},{12,44},{16,24},{20,52},{24,0},{28,60},{32,40}... | collective-permute-start | bytes 786440 | tf_op jit(solution)/shard_map/ppermute | solution.py:159
  53.0 0.0 collective-permute-start.8
  53.0 4.2 %collective-permute-start.9 = (bf16[8,128,128]{2,1,0:T(8,128)(2,1)S(1)}, bf16[8,128,128]{2,1,0:T(8,128)(2,1)S(1)}, u32[]{:S(2)}, u32[]{:S(2)}) collective-permute-start(bf16[8,128,128]{2,1,0:T(8,128)(2,1)S(1)} %collective-permute-done.4), channel_id=1, source_target_pairs={{0,32},{4,12},{8,40},{12,20},{16,48},{20,28},{24,56},{28,4},{32,64... | collective-permute-start | bytes 786440 | tf_op jit(solution)/shard_map/ppermute | solution.py:159
  57.3 0.3 collective-permute-start.11
  57.6 13.8 %all-to-all-done.hbm = bf16[128,128,128]{2,1,0:T(8,128)(2,1)} async-done(((bf16[128,128,128]{2,1,0:T(8,128)(2,1)}), bf16[128,128,128]{2,1,0:T(8,128)(2,1)}, u32[]{:S(2)}, u32[]{:S(2)}) %all-to-all-start) | async-done | bytes 4194336 | tf_op jit(solution)/shard_map/all_to_all | solution.py:328
  71.4 2.2 %stage.1.w_ref = bf16[128,128,128]{2,1,0:T(8,128)(2,1)S(1)} custom-call(bf16[128,128,128]{2,1,0:T(8,128)(2,1)} %all-to-all-done.hbm), custom_call_target="tpu_custom_call" | custom-call | flops 5000000000 | bytes 8388608 | tf_op jit(solution)/shard_map/stage/pallas_call | solution.py:193
  73.6 2.1 %collective-permute-done.6.refs_2_ = bf16[16,128,128]{2,1,0:T(8,128)(2,1)S(1)} collective-permute-done((bf16[16,128,128]{2,1,0:T(8,128)(2,1)}, bf16[16,128,128]{2,1,0:T(8,128)(2,1)S(1)}, u32[]{:S(2)}, u32[]{:S(2)}) %collective-permute-start.6) | collective-permute-done | bytes 524320 | tf_op jit(solution)/shard_map/ppermute | solution.py:159
  75.7 0.2 collective-permute-start.10
  75.9 0.0 copy-done.2
  75.9 0.1 fusion.9
  76.0 0.0 copy-done.3
  76.0 2.6 %collective-permute-done.7.refs_1_ = bf16[8,128,128]{2,1,0:T(8,128)(2,1)S(1)} collective-permute-done((bf16[8,128,128]{2,1,0:T(8,128)(2,1)}, bf16[8,128,128]{2,1,0:T(8,128)(2,1)S(1)}, u32[]{:S(2)}, u32[]{:S(2)}) %collective-permute-start.7) | collective-permute-done | bytes 262176 | tf_op jit(solution)/shard_map/ppermute | solution.py:159
  78.6 0.0 collective-permute-done.8.refs_3_
  78.6 0.0 collective-permute-done.9.refs_5_
  78.6 0.0 collective-permute-done.11.refs_7_
  78.6 0.0 collective-permute-done.10.refs_6_
  78.7 0.0 copy-done.1
  78.7 0.0 copy-start.5
  78.7 0.0 copy-start.9
  78.7 0.0 copy-start.4
  78.7 11.1 %products.1 = bf16[32,128,128]{2,1,0:T(8,128)(2,1)} custom-call(s32[2,32,32]{2,1,0:T(8,128)S(1)} %pad_add_fusion.task_hbm, bf16[128,128,128]{2,1,0:T(8,128)(2,1)S(1)} %stage.1.w_ref, bf16[8,128,128]{2,1,0:T(8,128)(2,1)S(1)} %copy-done.1, bf16[8,128,128]{2,1,0:T(8,128)(2,1)S(1)} %collective-permute-done.7.refs_1_, ...), custom_call_target="tpu_custom_call" | custom-call | flops 4294967296 | bytes 7340032 | tf_op jit(solution)/shard_map/products/pallas_call | solution.py:256
  89.8 8.2 %all-to-all-start.1 = ((bf16[32,128,128]{2,1,0:T(8,128)(2,1)}), bf16[32,128,128]{2,1,0:T(8,128)(2,1)S(1)}, u32[]{:S(2)}, u32[]{:S(2)}) async-start(bf16[32,128,128]{2,1,0:T(8,128)(2,1)} %products.1), calls=%async_computation.1 | async-start | bytes 2097152 | tf_op jit(solution)/shard_map/all_to_all | solution.py:332
  98.1 0.0 copy-done
  98.1 0.1 constant_dynamic-slice_fusion
  98.2 0.6 fusion.15
  102.5 0.0 copy-done.5
  102.5 0.7 fusion.14
  104.4 0.0 copy-done.9
  104.4 0.1 select_reduce_fusion.1
  104.5 0.0 copy-done.4
  104.6 0.3 subtract_divide_fusion.inverse_ref
  104.9 10.3 %all-to-all-done.1.in_ref = bf16[32,128,128]{2,1,0:T(8,128)(2,1)S(1)} async-done(((bf16[32,128,128]{2,1,0:T(8,128)(2,1)}), bf16[32,128,128]{2,1,0:T(8,128)(2,1)S(1)}, u32[]{:S(2)}, u32[]{:S(2)}) %all-to-all-start.1) | async-done | bytes 1048608 | tf_op jit(solution)/shard_map/all_to_all | solution.py:332
  115.2 1.6 %finish.1 = f32[16,128,128]{2,1,0:T(8,128)} custom-call(s32[2,16]{1,0:T(2,128)S(1)} %pad_add_fusion.1.slot_ref, bf16[32,128,128]{2,1,0:T(8,128)(2,1)S(1)} %all-to-all-done.1.in_ref, f32[16,128,128]{2,1,0:T(8,128)S(1)} %subtract_divide_fusion.inverse_ref), custom_call_target="tpu_custom_call" | custom-call | tf_op jit(solution)/shard_map/finish/pallas_call | solution.py:290
  (5 shorter events, 0.1 us)
Async XLA Ops:
  0.0 98.1 %copy-start = (s32[32,2]{0,1:T(2,128)S(1)}, s32[32,2]{0,1:T(2,128)}, u32[]{:S(2)}) copy-start(s32[32,2]{0,1:T(2,128)} %param.25) | copy-start | bytes 772
  4.8 14.4 %collective-permute-start = (bf16[16,128,128]{2,1,0:T(8,128)(2,1)}, bf16[16,128,128]{2,1,0:T(8,128)(2,1)S(1)}, u32[]{:S(2)}, u32[]{:S(2)}) collective-permute-start(bf16[16,128,128]{2,1,0:T(8,128)(2,1)} %get-tuple-element.27), channel_id=1, source_target_pairs={{0,32},{4,12},{8,40},{12,20},{16,48},{20,28},{24,56},{28,4},{32,64... | collective-permute-start | bytes 1572872 | tf_op jit(solution)/shard_map/ppermute | solution.py:159
  6.1 15.1 %collective-permute-start.1 = (bf16[16,128,128]{2,1,0:T(8,128)(2,1)}, bf16[16,128,128]{2,1,0:T(8,128)(2,1)S(1)}, u32[]{:S(2)}, u32[]{:S(2)}) collective-permute-start(bf16[16,128,128]{2,1,0:T(8,128)(2,1)} %get-tuple-element.28), channel_id=1, source_target_pairs={{0,64},{4,20},{8,72},{12,28},{16,80},{20,4},{24,88},{28,12},{32,96... | collective-permute-start | bytes 1572872 | tf_op jit(solution)/shard_map/ppermute | solution.py:159
  8.5 12.7 %collective-permute-start.2 = (bf16[16,128,128]{2,1,0:T(8,128)(2,1)}, bf16[16,128,128]{2,1,0:T(8,128)(2,1)S(1)}, u32[]{:S(2)}, u32[]{:S(2)}) collective-permute-start(bf16[16,128,128]{2,1,0:T(8,128)(2,1)} %get-tuple-element.29), channel_id=1, source_target_pairs={{0,96},{4,28},{8,104},{12,4},{16,112},{20,12},{24,120},{28,20},{32... | collective-permute-start | bytes 1572872 | tf_op jit(solution)/shard_map/ppermute | solution.py:159
  9.7 61.7 %all-to-all-start = ((bf16[128,128,128]{2,1,0:T(8,128)(2,1)}), bf16[128,128,128]{2,1,0:T(8,128)(2,1)}, u32[]{:S(2)}, u32[]{:S(2)}) async-start(bf16[128,128,128]{2,1,0:T(8,128)(2,1)} %get-tuple-element.25), calls=%async_computation | async-start | bytes 8388608 | tf_op jit(solution)/shard_map/all_to_all | solution.py:328
  19.2 2.0 %copy-start.6 = (bf16[16,128,128]{2,1,0:T(8,128)(2,1)}, bf16[16,128,128]{2,1,0:T(8,128)(2,1)S(1)}, u32[]{:S(2)}) copy-start(bf16[16,128,128]{2,1,0:T(8,128)(2,1)S(1)} %collective-permute-done.refs_1_) | copy-start | bytes 1572868
  21.2 0.8 copy-start.7
  21.2 1.0 copy-start.8
  25.3 17.4 %collective-permute-start.3 = (bf16[8,128,128]{2,1,0:T(8,128)(2,1)}, bf16[8,128,128]{2,1,0:T(8,128)(2,1)S(1)}, u32[]{:S(2)}, u32[]{:S(2)}) collective-permute-start(bf16[8,128,128]{2,1,0:T(8,128)(2,1)} %get-tuple-element.32), channel_id=1, source_target_pairs={{0,4},{4,0},{8,12},{12,8},{16,20},{20,16},{24,28},{28,24},{32,36},... | collective-permute-start | bytes 786440 | tf_op jit(solution)/shard_map/ppermute | solution.py:163
  41.4 1.7 %collective-permute-start.4 = (bf16[8,128,128]{2,1,0:T(8,128)(2,1)}, bf16[8,128,128]{2,1,0:T(8,128)(2,1)S(1)}, u32[]{:S(2)}, u32[]{:S(2)}) collective-permute-start(bf16[8,128,128]{2,1,0:T(8,128)(2,1)} %get-tuple-element.33), channel_id=1, source_target_pairs={{0,4},{4,0},{8,12},{12,8},{16,20},{20,16},{24,28},{28,24},{32,36},... | collective-permute-start | bytes 786440 | tf_op jit(solution)/shard_map/ppermute | solution.py:163
  41.5 2.0 %collective-permute-start.5 = (bf16[8,128,128]{2,1,0:T(8,128)(2,1)}, bf16[8,128,128]{2,1,0:T(8,128)(2,1)S(1)}, u32[]{:S(2)}, u32[]{:S(2)}) collective-permute-start(bf16[8,128,128]{2,1,0:T(8,128)(2,1)} %get-tuple-element.34), channel_id=1, source_target_pairs={{0,4},{4,0},{8,12},{12,8},{16,20},{20,16},{24,28},{28,24},{32,36},... | collective-permute-start | bytes 786440 | tf_op jit(solution)/shard_map/ppermute | solution.py:163
  43.5 32.2 %collective-permute-start.6 = (bf16[16,128,128]{2,1,0:T(8,128)(2,1)}, bf16[16,128,128]{2,1,0:T(8,128)(2,1)S(1)}, u32[]{:S(2)}, u32[]{:S(2)}) collective-permute-start(bf16[16,128,128]{2,1,0:T(8,128)(2,1)} %get-tuple-element.36), channel_id=1, source_target_pairs={{0,16},{4,68},{8,24},{12,76},{16,0},{20,84},{24,8},{28,92},{32,48}... | collective-permute-start | bytes 1572872 | tf_op jit(solution)/shard_map/ppermute | solution.py:159
  43.5 32.4 %copy-start.2 = (s32[1,1,32,32]{3,2,1,0:T(8,128)S(1)}, s32[1,1,32,32]{3,2,1,0:T(8,128)}, u32[]{:S(2)}) copy-start(s32[1,1,32,32]{3,2,1,0:T(8,128)} %param.22) | copy-start | bytes 12292
  43.5 32.5 %copy-start.3 = (s32[1,1,32,32]{3,2,1,0:T(8,128)S(1)}, s32[1,1,32,32]{3,2,1,0:T(8,128)}, u32[]{:S(2)}) copy-start(s32[1,1,32,32]{3,2,1,0:T(8,128)} %param.23) | copy-start | bytes 12292
  43.5 35.2 %copy-start.1 = (bf16[8,128,128]{2,1,0:T(8,128)(2,1)S(1)}, bf16[8,128,128]{2,1,0:T(8,128)(2,1)}, u32[]{:S(2)}) copy-start(bf16[8,128,128]{2,1,0:T(8,128)(2,1)} %get-tuple-element.38.refs_0_) | copy-start | bytes 786436
  43.5 35.1 %collective-permute-start.7 = (bf16[8,128,128]{2,1,0:T(8,128)(2,1)}, bf16[8,128,128]{2,1,0:T(8,128)(2,1)S(1)}, u32[]{:S(2)}, u32[]{:S(2)}) collective-permute-start(bf16[8,128,128]{2,1,0:T(8,128)(2,1)} %get-tuple-element.39), channel_id=1, source_target_pairs={{0,8},{4,36},{8,16},{12,44},{16,24},{20,52},{24,0},{28,60},{32,40}... | collective-permute-start | bytes 786440 | tf_op jit(solution)/shard_map/ppermute | solution.py:159
  53.0 25.6 %collective-permute-start.8 = (bf16[8,128,128]{2,1,0:T(8,128)(2,1)}, bf16[8,128,128]{2,1,0:T(8,128)(2,1)S(1)}, u32[]{:S(2)}, u32[]{:S(2)}) collective-permute-start(bf16[8,128,128]{2,1,0:T(8,128)(2,1)} %get-tuple-element.41), channel_id=1, source_target_pairs={{0,24},{4,100},{8,0},{12,108},{16,8},{20,116},{24,16},{28,124},{32... | collective-permute-start | bytes 786440 | tf_op jit(solution)/shard_map/ppermute | solution.py:159
  53.0 25.6 %collective-permute-start.9 = (bf16[8,128,128]{2,1,0:T(8,128)(2,1)S(1)}, bf16[8,128,128]{2,1,0:T(8,128)(2,1)S(1)}, u32[]{:S(2)}, u32[]{:S(2)}) collective-permute-start(bf16[8,128,128]{2,1,0:T(8,128)(2,1)S(1)} %collective-permute-done.4), channel_id=1, source_target_pairs={{0,32},{4,12},{8,40},{12,20},{16,48},{20,28},{24,56},{28,4},{32,64... | collective-permute-start | bytes 786440 | tf_op jit(solution)/shard_map/ppermute | solution.py:159
  57.3 21.4 %collective-permute-start.11 = (bf16[8,128,128]{2,1,0:T(8,128)(2,1)S(1)}, bf16[8,128,128]{2,1,0:T(8,128)(2,1)S(1)}, u32[]{:S(2)}, u32[]{:S(2)}) collective-permute-start(bf16[8,128,128]{2,1,0:T(8,128)(2,1)S(1)} %collective-permute-done.5), channel_id=1, source_target_pairs={{0,96},{4,28},{8,104},{12,4},{16,112},{20,12},{24,120},{28,20},{32... | collective-permute-start | bytes 786440 | tf_op jit(solution)/shard_map/ppermute | solution.py:159
  75.7 2.9 %collective-permute-start.10 = (bf16[8,128,128]{2,1,0:T(8,128)(2,1)S(1)}, bf16[8,128,128]{2,1,0:T(8,128)(2,1)S(1)}, u32[]{:S(2)}, u32[]{:S(2)}) collective-permute-start(bf16[8,128,128]{2,1,0:T(8,128)(2,1)S(1)} %slice.11), channel_id=1, source_target_pairs={{0,4},{4,0},{8,12},{12,8},{16,20},{20,16},{24,28},{28,24},{32,36},... | collective-permute-start | bytes 786440 | tf_op jit(solution)/shard_map/ppermute | solution.py:163
  78.7 23.8 %copy-start.5 = (f32[300]{0:T(512)S(1)}, f32[300]{0:T(512)}, u32[]{:S(2)}) copy-start(f32[300]{0:T(512)} %param.26) | copy-start | bytes 3604
  78.7 25.7 %copy-start.9 = (s32[1,1,32,1]{2,3,1,0:T(1,128)S(1)}, s32[1,1,32,1]{2,3,1,0:T(1,128)}, u32[]{:S(2)}) copy-start(s32[1,1,32,1]{2,3,1,0:T(1,128)} %param.24) | copy-start | bytes 388
  78.7 25.8 %copy-start.4 = (f32[1024]{0:T(1024)S(1)}, f32[1024]{0:T(1024)}, u32[]{:S(2)}) copy-start(f32[1024]{0:T(1024)} %param.27) | copy-start | bytes 12292
  89.8 25.4 %all-to-all-start.1 = ((bf16[32,128,128]{2,1,0:T(8,128)(2,1)}), bf16[32,128,128]{2,1,0:T(8,128)(2,1)S(1)}, u32[]{:S(2)}, u32[]{:S(2)}) async-start(bf16[32,128,128]{2,1,0:T(8,128)(2,1)} %products.1), calls=%async_computation.1 | async-start | bytes 2097152 | tf_op jit(solution)/shard_map/all_to_all | solution.py:332

commit v6 on v5

--- a/solution.py
+++ b/solution.py
@@ -164,7 +164,8 @@
 
 
 def fetch_t(parts, w_fetched):
-    parts = [parts[0]] + [move(parts[k], k, 0) for k in range(1, SIDE)]
+    moved = {k: move(parts[k], k, 0) for k in (2, 1, 3)}
+    parts = [parts[0]] + [moved[k] for k in range(1, SIDE)]
     same0, same1, same3, other0, other1, other3, both2 = regroup(parts)
     other0, other1, other3 = swap_cores(other0), swap_cores(other1), swap_cores(other3)
     same1, same3, other0, other1, other3, both2 = lax.optimization_barrier(

time: 117 us -> 117 us (level)
  no operation moved by 1% of the time
where the time goes in v6:
time: 117 us
  starting transfers between devices  53.4 us (46%)
  waiting for transfers between devices  32.5 us (28%)
  Pallas kernels  22.8 us (19%)
  between operations  5.2 us (4%)
  local copies, waits for them, and re-layouts  2.36 us (2%)
    ppermute x8, starting transfers between devices, move(): return lax.ppermute(part, 'tasks', shift(k, first_axis))  18.9 us
    ppermute x4, starting transfers between devices, swap_cores(): lax.ppermute(part, 'tasks', [(i, i ^ 1) for i in range(2 * SIDE * SIDE)])  16.8 us
    all_to_all x1, waiting for transfers between devices, per_device(): lax.all_to_all(w_out, ('tasks', 'grp'), split_axis=0, concat_axis=0, tile...  13.8 us
    pallas_call x1, Pallas kernels, products(): pl.pallas_call(products_kernel, out_shape=jax.ShapeDtypeStruct((slots, ro...  11.1 us
    all_to_all x1, waiting for transfers between devices, per_device(): lax.all_to_all(partials, 'tasks', split_axis=0, concat_axis=0, tiled=True)  10.3 us
    all_to_all x1, starting transfers between devices, per_device(): lax.all_to_all(w_out, ('tasks', 'grp'), split_axis=0, concat_axis=0, tile...  9.49 us
    all_to_all x1, starting transfers between devices, per_device(): lax.all_to_all(partials, 'tasks', split_axis=0, concat_axis=0, tiled=True)  8.24 us
    ppermute x8, waiting for transfers between devices, move(): return lax.ppermute(part, 'tasks', shift(k, first_axis))  6.76 us
  transfers between devices with their start and end apart: 14, of which 8 were waited for; matrix products, arithmetic and copies ran while one was open for 2% of the time, Pallas kernels for 5%

profile of v6, /device:TPU:33, one launch (start us, length us, event | category | flops | bytes accessed | tf_op | source)
XLA Modules:
  0.0 116.8 jit_solution(5988939018686093467)
XLA Ops:
  0.0 0.0 copy-start
  0.0 4.8 %prepare.1 = (bf16[16,128,128]{2,1,0:T(8,128)(2,1)}, bf16[16,128,128]{2,1,0:T(8,128)(2,1)}, bf16[16,128,128]{2,1,0:T(8,128)(2,1)}, bf16[16,128,128]{2,1,0:T(8,128)(2,1)}, bf16[128,128,128]{2,1,0:T(8,128)(2,1)}) custom-call(s32[1,2048]{1,0:T(1,128)} %t_home_hbm.1, s32[2,32]{1,0:T(2,128)} %bitcast.40, bf16[64,128,128]{2,1,0:T(8,128)(2,1)} %bitcast.36, ...), custom_call_target="tpu_custom_call" | custom-call | tf_op jit(solution)/shard_map/prepare/pallas_call | solution.py:88
  4.8 1.3 %collective-permute-start = (bf16[16,128,128]{2,1,0:T(8,128)(2,1)}, bf16[16,128,128]{2,1,0:T(8,128)(2,1)S(1)}, u32[]{:S(2)}, u32[]{:S(2)}) collective-permute-start(bf16[16,128,128]{2,1,0:T(8,128)(2,1)} %get-tuple-element.27), channel_id=1, source_target_pairs={{0,32},{4,12},{8,40},{12,20},{16,48},{20,28},{24,56},{28,4},{32,64... | collective-permute-start | bytes 1572872 | tf_op jit(solution)/shard_map/ppermute | solution.py:159
  6.1 2.4 %collective-permute-start.1 = (bf16[16,128,128]{2,1,0:T(8,128)(2,1)}, bf16[16,128,128]{2,1,0:T(8,128)(2,1)S(1)}, u32[]{:S(2)}, u32[]{:S(2)}) collective-permute-start(bf16[16,128,128]{2,1,0:T(8,128)(2,1)} %get-tuple-element.28), channel_id=1, source_target_pairs={{0,64},{4,20},{8,72},{12,28},{16,80},{20,4},{24,88},{28,12},{32,96... | collective-permute-start | bytes 1572872 | tf_op jit(solution)/shard_map/ppermute | solution.py:159
  8.5 1.2 collective-permute-start.2
  9.7 9.5 %all-to-all-start = ((bf16[128,128,128]{2,1,0:T(8,128)(2,1)}), bf16[128,128,128]{2,1,0:T(8,128)(2,1)}, u32[]{:S(2)}, u32[]{:S(2)}) async-start(bf16[128,128,128]{2,1,0:T(8,128)(2,1)} %get-tuple-element.25), calls=%async_computation | async-start | bytes 8388608 | tf_op jit(solution)/shard_map/all_to_all | solution.py:329
  19.2 0.0 collective-permute-done.refs_1_
  19.2 0.0 copy-start.6
  19.2 2.0 %collective-permute-done.1.refs_2_ = bf16[16,128,128]{2,1,0:T(8,128)(2,1)S(1)} collective-permute-done((bf16[16,128,128]{2,1,0:T(8,128)(2,1)}, bf16[16,128,128]{2,1,0:T(8,128)(2,1)S(1)}, u32[]{:S(2)}, u32[]{:S(2)}) %collective-permute-start.1) | collective-permute-done | bytes 524320 | tf_op jit(solution)/shard_map/ppermute | solution.py:159
  21.2 0.0 copy-start.7
  21.2 0.0 collective-permute-done.2.refs_3_
  21.2 0.0 copy-start.8
  21.2 0.0 copy-done.6
  21.2 0.8 copy-done.7
  22.0 0.2 copy-done.8
  22.2 3.1 %regroup.1 = (bf16[8,128,128]{2,1,0:T(8,128)(2,1)}, bf16[8,128,128]{2,1,0:T(8,128)(2,1)}, bf16[8,128,128]{2,1,0:T(8,128)(2,1)}, bf16[8,128,128]{2,1,0:T(8,128)(2...) custom-call(bf16[16,128,128]{2,1,0:T(8,128)(2,1)} %get-tuple-element.26.refs_0_, ...), custom_call_target="tpu_custom_call" | custom-call | flops 99999997952 | bytes 4194304 | tf_op jit(solution)/shard_map/regroup/pallas_call | solution.py:136
  25.3 16.1 %collective-permute-start.3 = (bf16[8,128,128]{2,1,0:T(8,128)(2,1)}, bf16[8,128,128]{2,1,0:T(8,128)(2,1)S(1)}, u32[]{:S(2)}, u32[]{:S(2)}) collective-permute-start(bf16[8,128,128]{2,1,0:T(8,128)(2,1)} %get-tuple-element.32), channel_id=1, source_target_pairs={{0,4},{4,0},{8,12},{12,8},{16,20},{20,16},{24,28},{28,24},{32,36},... | collective-permute-start | bytes 786440 | tf_op jit(solution)/shard_map/ppermute | solution.py:163
  41.4 0.1 collective-permute-start.4
  41.5 0.4 collective-permute-start.5
  41.9 0.9 collective-permute-done.3.refs_4_
  42.7 0.4 collective-permute-done.4
  43.1 0.4 collective-permute-done.5
  43.5 0.0 collective-permute-start.6
  43.5 0.0 copy-start.2
  43.5 0.0 copy-start.3
  43.5 0.0 copy-start.1
  43.5 9.5 %collective-permute-start.7 = (bf16[8,128,128]{2,1,0:T(8,128)(2,1)}, bf16[8,128,128]{2,1,0:T(8,128)(2,1)S(1)}, u32[]{:S(2)}, u32[]{:S(2)}) collective-permute-start(bf16[8,128,128]{2,1,0:T(8,128)(2,1)} %get-tuple-element.39), channel_id=1, source_target_pairs={{0,8},{4,36},{8,16},{12,44},{16,24},{20,52},{24,0},{28,60},{32,40}... | collective-permute-start | bytes 786440 | tf_op jit(solution)/shard_map/ppermute | solution.py:159
  53.0 0.0 collective-permute-start.8
  53.0 4.2 %collective-permute-start.9 = (bf16[8,128,128]{2,1,0:T(8,128)(2,1)S(1)}, bf16[8,128,128]{2,1,0:T(8,128)(2,1)S(1)}, u32[]{:S(2)}, u32[]{:S(2)}) collective-permute-start(bf16[8,128,128]{2,1,0:T(8,128)(2,1)S(1)} %collective-permute-done.4), channel_id=1, source_target_pairs={{0,32},{4,12},{8,40},{12,20},{16,48},{20,28},{24,56},{28,4},{32,64... | collective-permute-start | bytes 786440 | tf_op jit(solution)/shard_map/ppermute | solution.py:159
  57.3 0.3 collective-permute-start.11
  57.6 13.8 %all-to-all-done.hbm = bf16[128,128,128]{2,1,0:T(8,128)(2,1)} async-done(((bf16[128,128,128]{2,1,0:T(8,128)(2,1)}), bf16[128,128,128]{2,1,0:T(8,128)(2,1)}, u32[]{:S(2)}, u32[]{:S(2)}) %all-to-all-start) | async-done | bytes 4194336 | tf_op jit(solution)/shard_map/all_to_all | solution.py:329
  71.4 2.2 %stage.1.w_ref = bf16[128,128,128]{2,1,0:T(8,128)(2,1)S(1)} custom-call(bf16[128,128,128]{2,1,0:T(8,128)(2,1)} %all-to-all-done.hbm), custom_call_target="tpu_custom_call" | custom-call | flops 5000000000 | bytes 8388608 | tf_op jit(solution)/shard_map/stage/pallas_call | solution.py:194
  73.6 2.1 %collective-permute-done.6.refs_2_ = bf16[16,128,128]{2,1,0:T(8,128)(2,1)S(1)} collective-permute-done((bf16[16,128,128]{2,1,0:T(8,128)(2,1)}, bf16[16,128,128]{2,1,0:T(8,128)(2,1)S(1)}, u32[]{:S(2)}, u32[]{:S(2)}) %collective-permute-start.6) | collective-permute-done | bytes 524320 | tf_op jit(solution)/shard_map/ppermute | solution.py:159
  75.7 0.2 collective-permute-start.10
  75.9 0.0 copy-done.2
  75.9 0.1 fusion.9
  76.0 0.0 copy-done.3
  76.0 2.6 %collective-permute-done.7.refs_1_ = bf16[8,128,128]{2,1,0:T(8,128)(2,1)S(1)} collective-permute-done((bf16[8,128,128]{2,1,0:T(8,128)(2,1)}, bf16[8,128,128]{2,1,0:T(8,128)(2,1)S(1)}, u32[]{:S(2)}, u32[]{:S(2)}) %collective-permute-start.7) | collective-permute-done | bytes 262176 | tf_op jit(solution)/shard_map/ppermute | solution.py:159
  78.6 0.0 collective-permute-done.8.refs_3_
  78.6 0.0 collective-permute-done.9.refs_5_
  78.6 0.0 collective-permute-done.11.refs_7_
  78.6 0.0 collective-permute-done.10.refs_6_
  78.7 0.0 copy-done.1
  78.7 0.0 copy-start.5
  78.7 0.0 copy-start.9
  78.7 0.0 copy-start.4
  78.7 11.1 %products.1 = bf16[32,128,128]{2,1,0:T(8,128)(2,1)} custom-call(s32[2,32,32]{2,1,0:T(8,128)S(1)} %pad_add_fusion.task_hbm, bf16[128,128,128]{2,1,0:T(8,128)(2,1)S(1)} %stage.1.w_ref, bf16[8,128,128]{2,1,0:T(8,128)(2,1)S(1)} %copy-done.1, bf16[8,128,128]{2,1,0:T(8,128)(2,1)S(1)} %collective-permute-done.7.refs_1_, ...), custom_call_target="tpu_custom_call" | custom-call | flops 4294967296 | bytes 7340032 | tf_op jit(solution)/shard_map/products/pallas_call | solution.py:257
  89.8 8.2 %all-to-all-start.1 = ((bf16[32,128,128]{2,1,0:T(8,128)(2,1)}), bf16[32,128,128]{2,1,0:T(8,128)(2,1)S(1)}, u32[]{:S(2)}, u32[]{:S(2)}) async-start(bf16[32,128,128]{2,1,0:T(8,128)(2,1)} %products.1), calls=%async_computation.1 | async-start | bytes 2097152 | tf_op jit(solution)/shard_map/all_to_all | solution.py:333
  98.1 0.0 copy-done
  98.1 0.1 constant_dynamic-slice_fusion
  98.2 0.6 fusion.15
  102.5 0.0 copy-done.5
  102.5 0.7 fusion.14
  104.4 0.0 copy-done.9
  104.4 0.1 select_reduce_fusion.1
  104.5 0.0 copy-done.4
  104.6 0.3 subtract_divide_fusion.inverse_ref
  104.9 10.3 %all-to-all-done.1.in_ref = bf16[32,128,128]{2,1,0:T(8,128)(2,1)S(1)} async-done(((bf16[32,128,128]{2,1,0:T(8,128)(2,1)}), bf16[32,128,128]{2,1,0:T(8,128)(2,1)S(1)}, u32[]{:S(2)}, u32[]{:S(2)}) %all-to-all-start.1) | async-done | bytes 1048608 | tf_op jit(solution)/shard_map/all_to_all | solution.py:333
  115.2 1.6 %finish.1 = f32[16,128,128]{2,1,0:T(8,128)} custom-call(s32[2,16]{1,0:T(2,128)S(1)} %pad_add_fusion.1.slot_ref, bf16[32,128,128]{2,1,0:T(8,128)(2,1)S(1)} %all-to-all-done.1.in_ref, f32[16,128,128]{2,1,0:T(8,128)S(1)} %subtract_divide_fusion.inverse_ref), custom_call_target="tpu_custom_call" | custom-call | tf_op jit(solution)/shard_map/finish/pallas_call | solution.py:291
  (5 shorter events, 0.1 us)
Async XLA Ops:
  0.0 98.1 %copy-start = (s32[32,2]{0,1:T(2,128)S(1)}, s32[32,2]{0,1:T(2,128)}, u32[]{:S(2)}) copy-start(s32[32,2]{0,1:T(2,128)} %param.25) | copy-start | bytes 772
  4.8 14.4 %collective-permute-start = (bf16[16,128,128]{2,1,0:T(8,128)(2,1)}, bf16[16,128,128]{2,1,0:T(8,128)(2,1)S(1)}, u32[]{:S(2)}, u32[]{:S(2)}) collective-permute-start(bf16[16,128,128]{2,1,0:T(8,128)(2,1)} %get-tuple-element.27), channel_id=1, source_target_pairs={{0,32},{4,12},{8,40},{12,20},{16,48},{20,28},{24,56},{28,4},{32,64... | collective-permute-start | bytes 1572872 | tf_op jit(solution)/shard_map/ppermute | solution.py:159
  6.1 15.1 %collective-permute-start.1 = (bf16[16,128,128]{2,1,0:T(8,128)(2,1)}, bf16[16,128,128]{2,1,0:T(8,128)(2,1)S(1)}, u32[]{:S(2)}, u32[]{:S(2)}) collective-permute-start(bf16[16,128,128]{2,1,0:T(8,128)(2,1)} %get-tuple-element.28), channel_id=1, source_target_pairs={{0,64},{4,20},{8,72},{12,28},{16,80},{20,4},{24,88},{28,12},{32,96... | collective-permute-start | bytes 1572872 | tf_op jit(solution)/shard_map/ppermute | solution.py:159
  8.5 12.7 %collective-permute-start.2 = (bf16[16,128,128]{2,1,0:T(8,128)(2,1)}, bf16[16,128,128]{2,1,0:T(8,128)(2,1)S(1)}, u32[]{:S(2)}, u32[]{:S(2)}) collective-permute-start(bf16[16,128,128]{2,1,0:T(8,128)(2,1)} %get-tuple-element.29), channel_id=1, source_target_pairs={{0,96},{4,28},{8,104},{12,4},{16,112},{20,12},{24,120},{28,20},{32... | collective-permute-start | bytes 1572872 | tf_op jit(solution)/shard_map/ppermute | solution.py:159
  9.7 61.7 %all-to-all-start = ((bf16[128,128,128]{2,1,0:T(8,128)(2,1)}), bf16[128,128,128]{2,1,0:T(8,128)(2,1)}, u32[]{:S(2)}, u32[]{:S(2)}) async-start(bf16[128,128,128]{2,1,0:T(8,128)(2,1)} %get-tuple-element.25), calls=%async_computation | async-start | bytes 8388608 | tf_op jit(solution)/shard_map/all_to_all | solution.py:329
  19.2 2.0 %copy-start.6 = (bf16[16,128,128]{2,1,0:T(8,128)(2,1)}, bf16[16,128,128]{2,1,0:T(8,128)(2,1)S(1)}, u32[]{:S(2)}) copy-start(bf16[16,128,128]{2,1,0:T(8,128)(2,1)S(1)} %collective-permute-done.refs_1_) | copy-start | bytes 1572868
  21.2 0.8 copy-start.7
  21.2 1.0 copy-start.8
  25.3 17.4 %collective-permute-start.3 = (bf16[8,128,128]{2,1,0:T(8,128)(2,1)}, bf16[8,128,128]{2,1,0:T(8,128)(2,1)S(1)}, u32[]{:S(2)}, u32[]{:S(2)}) collective-permute-start(bf16[8,128,128]{2,1,0:T(8,128)(2,1)} %get-tuple-element.32), channel_id=1, source_target_pairs={{0,4},{4,0},{8,12},{12,8},{16,20},{20,16},{24,28},{28,24},{32,36},... | collective-permute-start | bytes 786440 | tf_op jit(solution)/shard_map/ppermute | solution.py:163
  41.4 1.7 %collective-permute-start.4 = (bf16[8,128,128]{2,1,0:T(8,128)(2,1)}, bf16[8,128,128]{2,1,0:T(8,128)(2,1)S(1)}, u32[]{:S(2)}, u32[]{:S(2)}) collective-permute-start(bf16[8,128,128]{2,1,0:T(8,128)(2,1)} %get-tuple-element.33), channel_id=1, source_target_pairs={{0,4},{4,0},{8,12},{12,8},{16,20},{20,16},{24,28},{28,24},{32,36},... | collective-permute-start | bytes 786440 | tf_op jit(solution)/shard_map/ppermute | solution.py:163
  41.5 2.0 %collective-permute-start.5 = (bf16[8,128,128]{2,1,0:T(8,128)(2,1)}, bf16[8,128,128]{2,1,0:T(8,128)(2,1)S(1)}, u32[]{:S(2)}, u32[]{:S(2)}) collective-permute-start(bf16[8,128,128]{2,1,0:T(8,128)(2,1)} %get-tuple-element.34), channel_id=1, source_target_pairs={{0,4},{4,0},{8,12},{12,8},{16,20},{20,16},{24,28},{28,24},{32,36},... | collective-permute-start | bytes 786440 | tf_op jit(solution)/shard_map/ppermute | solution.py:163
  43.5 32.2 %collective-permute-start.6 = (bf16[16,128,128]{2,1,0:T(8,128)(2,1)}, bf16[16,128,128]{2,1,0:T(8,128)(2,1)S(1)}, u32[]{:S(2)}, u32[]{:S(2)}) collective-permute-start(bf16[16,128,128]{2,1,0:T(8,128)(2,1)} %get-tuple-element.36), channel_id=1, source_target_pairs={{0,16},{4,68},{8,24},{12,76},{16,0},{20,84},{24,8},{28,92},{32,48}... | collective-permute-start | bytes 1572872 | tf_op jit(solution)/shard_map/ppermute | solution.py:159
  43.5 32.4 %copy-start.2 = (s32[1,1,32,32]{3,2,1,0:T(8,128)S(1)}, s32[1,1,32,32]{3,2,1,0:T(8,128)}, u32[]{:S(2)}) copy-start(s32[1,1,32,32]{3,2,1,0:T(8,128)} %param.22) | copy-start | bytes 12292
  43.5 32.5 %copy-start.3 = (s32[1,1,32,32]{3,2,1,0:T(8,128)S(1)}, s32[1,1,32,32]{3,2,1,0:T(8,128)}, u32[]{:S(2)}) copy-start(s32[1,1,32,32]{3,2,1,0:T(8,128)} %param.23) | copy-start | bytes 12292
  43.5 35.2 %copy-start.1 = (bf16[8,128,128]{2,1,0:T(8,128)(2,1)S(1)}, bf16[8,128,128]{2,1,0:T(8,128)(2,1)}, u32[]{:S(2)}) copy-start(bf16[8,128,128]{2,1,0:T(8,128)(2,1)} %get-tuple-element.38.refs_0_) | copy-start | bytes 786436
  43.5 35.1 %collective-permute-start.7 = (bf16[8,128,128]{2,1,0:T(8,128)(2,1)}, bf16[8,128,128]{2,1,0:T(8,128)(2,1)S(1)}, u32[]{:S(2)}, u32[]{:S(2)}) collective-permute-start(bf16[8,128,128]{2,1,0:T(8,128)(2,1)} %get-tuple-element.39), channel_id=1, source_target_pairs={{0,8},{4,36},{8,16},{12,44},{16,24},{20,52},{24,0},{28,60},{32,40}... | collective-permute-start | bytes 786440 | tf_op jit(solution)/shard_map/ppermute | solution.py:159
  53.0 25.6 %collective-permute-start.8 = (bf16[8,128,128]{2,1,0:T(8,128)(2,1)}, bf16[8,128,128]{2,1,0:T(8,128)(2,1)S(1)}, u32[]{:S(2)}, u32[]{:S(2)}) collective-permute-start(bf16[8,128,128]{2,1,0:T(8,128)(2,1)} %get-tuple-element.41), channel_id=1, source_target_pairs={{0,24},{4,100},{8,0},{12,108},{16,8},{20,116},{24,16},{28,124},{32... | collective-permute-start | bytes 786440 | tf_op jit(solution)/shard_map/ppermute | solution.py:159
  53.0 25.6 %collective-permute-start.9 = (bf16[8,128,128]{2,1,0:T(8,128)(2,1)S(1)}, bf16[8,128,128]{2,1,0:T(8,128)(2,1)S(1)}, u32[]{:S(2)}, u32[]{:S(2)}) collective-permute-start(bf16[8,128,128]{2,1,0:T(8,128)(2,1)S(1)} %collective-permute-done.4), channel_id=1, source_target_pairs={{0,32},{4,12},{8,40},{12,20},{16,48},{20,28},{24,56},{28,4},{32,64... | collective-permute-start | bytes 786440 | tf_op jit(solution)/shard_map/ppermute | solution.py:159
  57.3 21.4 %collective-permute-start.11 = (bf16[8,128,128]{2,1,0:T(8,128)(2,1)S(1)}, bf16[8,128,128]{2,1,0:T(8,128)(2,1)S(1)}, u32[]{:S(2)}, u32[]{:S(2)}) collective-permute-start(bf16[8,128,128]{2,1,0:T(8,128)(2,1)S(1)} %collective-permute-done.5), channel_id=1, source_target_pairs={{0,96},{4,28},{8,104},{12,4},{16,112},{20,12},{24,120},{28,20},{32... | collective-permute-start | bytes 786440 | tf_op jit(solution)/shard_map/ppermute | solution.py:159
  75.7 2.9 %collective-permute-start.10 = (bf16[8,128,128]{2,1,0:T(8,128)(2,1)S(1)}, bf16[8,128,128]{2,1,0:T(8,128)(2,1)S(1)}, u32[]{:S(2)}, u32[]{:S(2)}) collective-permute-start(bf16[8,128,128]{2,1,0:T(8,128)(2,1)S(1)} %slice.11), channel_id=1, source_target_pairs={{0,4},{4,0},{8,12},{12,8},{16,20},{20,16},{24,28},{28,24},{32,36},... | collective-permute-start | bytes 786440 | tf_op jit(solution)/shard_map/ppermute | solution.py:163
  78.7 23.8 %copy-start.5 = (f32[300]{0:T(512)S(1)}, f32[300]{0:T(512)}, u32[]{:S(2)}) copy-start(f32[300]{0:T(512)} %param.26) | copy-start | bytes 3604
  78.7 25.7 %copy-start.9 = (s32[1,1,32,1]{2,3,1,0:T(1,128)S(1)}, s32[1,1,32,1]{2,3,1,0:T(1,128)}, u32[]{:S(2)}) copy-start(s32[1,1,32,1]{2,3,1,0:T(1,128)} %param.24) | copy-start | bytes 388
  78.7 25.8 %copy-start.4 = (f32[1024]{0:T(1024)S(1)}, f32[1024]{0:T(1024)}, u32[]{:S(2)}) copy-start(f32[1024]{0:T(1024)} %param.27) | copy-start | bytes 12292
  89.8 25.4 %all-to-all-start.1 = ((bf16[32,128,128]{2,1,0:T(8,128)(2,1)}), bf16[32,128,128]{2,1,0:T(8,128)(2,1)S(1)}, u32[]{:S(2)}, u32[]{:S(2)}) async-start(bf16[32,128,128]{2,1,0:T(8,128)(2,1)} %products.1), calls=%async_computation.1 | async-start | bytes 2097152 | tf_op jit(solution)/shard_map/all_to_all | solution.py:333
